TPU v7x, 128 devices: a whole 4x4x4 slice. The times are simulated.
128 devices in a mesh: ctx: 16 (over y, z_lo, core), tp: 8 (over x, z_hi).
Axes of the slice: x: 4, y: 4, z: 4 (z_hi: 2, z_lo: 2; z = z_hi * 2 + z_lo), core: 2. Of those that a mesh axis runs over, the one named last changes fastest.
Arguments:
- tokens: bfloat16 [2048, 16384], P('ctx', 'tp'), may hold values from -6 to 6
- kv_weight: bfloat16 [16384, 2048], P('tp'), may hold values from -0.0625 to 0.0625
- queries: bfloat16 [2048, 8192], P('ctx', 'tp'), may hold values from -8 to 8
- cache_keys: bfloat16 [32768, 1024], P('ctx', 'tp'), may hold values from -8 to 8
- cache_values: bfloat16 [32768, 1024], P('ctx', 'tp'), may hold values from -6 to 6
- cache_lengths: int32 [16], replicated, may hold values from 512 to 2048, as said below
- page_owner: int32 [64], replicated, may hold values from 0 to 15, as said below
- page_slot: int32 [64], replicated, may hold values from 0 to 7, as said below
Outputs:
- attended: bfloat16 [2048, 8192], P('ctx', 'tp')
- kv_pages: bfloat16 [4096, 2048], P('ctx', 'tp')
Inputs may be any that keep to these rules, and one draw needn't show every extreme that they name: `page_owner`: each owner receives at most 8 pages, in distinct slots; some owner receives exactly 8 in every draw. `page_slot`: slots of pages with the same owner are distinct. `cache_lengths`: some owner is full in every draw.
All inputs are finite; a program needn't handle non-finite values.
Results may differ from a plain program's by a relative error of at most 0.035.
Values may be sent and summed in bfloat16 or wider, within the bound.
No kernel may reach another device: no remote copies, remote signals or barrier semaphores. Data moves between devices by JAX's collectives and lax.ppermute only.
A program may use at most 192 MiB of HBM per device.

v0:
```python
import math

import jax
import jax.numpy as jnp
from jax import lax
from jax.sharding import PartitionSpec as P

PAGE = 32


def block_update(run_state, query_rows, query_pos, key_block, key_codes):
    run_max, run_sum, run_out = run_state
    head_dim = key_block.shape[1] // 2
    scores = jnp.einsum(
        "rgd,kd->rgk", query_rows, key_block[:, :head_dim], preferred_element_type=jnp.float32
    ) * head_dim ** (-0.5)
    visible = (key_codes[None, :] == -1) | (key_codes[None, :] >= 0) & (
        key_codes[None, :] <= query_pos[:, None]
    )
    scores = jnp.where(visible[:, None, :], scores, -1e30)
    new_max = jnp.maximum(run_max, jnp.max(scores, axis=-1))
    weights = jnp.where(visible[:, None, :], jnp.exp(scores - new_max[..., None]), 0.0)
    rescale = jnp.exp(run_max - new_max)
    run_sum = run_sum * rescale + jnp.sum(weights, axis=-1)
    mixed = jnp.einsum(
        "rgk,kd->rgd",
        weights.astype(jnp.bfloat16),
        key_block[:, head_dim:],
        preferred_element_type=jnp.float32,
    )
    run_out = run_out * rescale[..., None] + mixed
    return (new_max, run_sum, run_out)


def attend_keys(run_state, query_rows, query_pos, key_vals, key_codes):
    total_keys = key_vals.shape[0]
    block_size = math.gcd(total_keys, 4608)
    blocks = total_keys // block_size

    def advance(current, inputs):
        return (block_update(current, query_rows, query_pos, inputs[0], inputs[1]), None)

    run_state, _ = lax.scan(
        advance,
        run_state,
        (
            key_vals.reshape(blocks, block_size, key_vals.shape[1]),
            key_codes.reshape(blocks, block_size),
        ),
    )
    return run_state


def empty_state(row_count, groups, head_dim):
    return (
        jnp.full((row_count, groups), -1e30, jnp.float32),
        jnp.zeros((row_count, groups), jnp.float32),
        jnp.zeros((row_count, groups, head_dim), jnp.float32),
    )


def body(
    tokens, kv_weight, queries, cache_keys, cache_values, cache_lengths, page_owner, page_slot
):
    cycle_size = lax.axis_size("ctx")
    my_index = lax.axis_index("ctx")
    tok_rows = tokens.shape[0]
    head_dim = cache_keys.shape[1]
    pair_width = 2 * head_dim
    groups = queries.shape[1] // head_dim
    cache_rows = cache_keys.shape[0]
    fresh_t = lax.psum_scatter(
        lax.dot_general(
            kv_weight, tokens, (((0,), (1,)), ((), ())), preferred_element_type=jnp.float32
        ).astype(jnp.bfloat16),
        "tp",
        scatter_dimension=0,
        tiled=True,
    ).astype(jnp.float32)
    fresh = fresh_t.T.astype(jnp.bfloat16)
    page_count = tok_rows // PAGE
    total_pages = page_count * cycle_size
    capacity = 2 * page_count
    local_pages = fresh.reshape(page_count, PAGE, pair_width)
    my_owners = lax.dynamic_slice_in_dim(page_owner, my_index * page_count, page_count)
    cycle_ids = jnp.arange(cycle_size, dtype=jnp.int32)
    onehot = (my_owners[None, :] == cycle_ids[:, None]).astype(jnp.bfloat16)
    outgoing = onehot[:, :, None, None] * local_pages[None]
    incoming = lax.all_to_all(outgoing, "ctx", split_axis=0, concat_axis=0, tiled=True)
    slot_ids = jnp.arange(capacity, dtype=jnp.int32)
    matches = (page_owner[None, None, :] == cycle_ids[:, None, None]) & (
        page_slot[None, None, :] == slot_ids[None, :, None]
    )
    my_matches = lax.dynamic_index_in_dim(matches, my_index, 0, keepdims=False)
    placed = jnp.dot(
        my_matches.astype(jnp.bfloat16),
        incoming.reshape(total_pages, PAGE * pair_width),
        preferred_element_type=jnp.float32,
    )
    kv_pages = placed.astype(jnp.bfloat16).reshape(capacity * PAGE, pair_width)
    page_ids = jnp.arange(total_pages, dtype=jnp.int32)
    occupied = jnp.any(matches, axis=-1)
    page_here = jnp.sum(jnp.where(matches, page_ids[None, None, :], 0), axis=-1)
    offsets = jnp.arange(PAGE, dtype=jnp.int32)
    new_codes = jnp.where(
        occupied[:, :, None], page_here[:, :, None] * PAGE + offsets[None, None, :], -2
    )
    cache_pos = jnp.arange(cache_rows, dtype=jnp.int32)
    old_codes = jnp.where(cache_pos[None, :] < cache_lengths[:, None], -1, -2)
    all_codes = jnp.concatenate([old_codes, new_codes.reshape(cycle_size, capacity * PAGE)], 1)
    keys_dev = all_codes.shape[1]
    all_codes = all_codes.reshape(cycle_size * keys_dev)
    key_vals = jnp.concatenate([jnp.concatenate([cache_keys, cache_values], 1), kv_pages], 0)
    query_rows = queries.reshape(tok_rows, groups, head_dim)
    own_pos = my_index * tok_rows + jnp.arange(tok_rows, dtype=jnp.int32)
    run_max, run_sum, run_out = attend_keys(
        empty_state(tok_rows, groups, head_dim),
        query_rows,
        own_pos,
        lax.all_gather(key_vals, "ctx", axis=0, tiled=True),
        all_codes,
    )
    result = run_out / run_sum[..., None]
    attended = result.reshape(tok_rows, groups * head_dim).astype(jnp.bfloat16)
    return (attended, kv_pages)


def solution(mesh):
    placed = (
        P("ctx", "tp"),
        P("tp", None),
        P("ctx", "tp"),
        P("ctx", "tp"),
        P("ctx", "tp"),
        P(),
        P(),
        P(),
    )
    return jax.shard_map(
        body,
        mesh=mesh,
        in_specs=placed,
        out_specs=(P("ctx", "tp"), P("ctx", "tp")),
        check_vma=False,
    )
```

profile of v0, /device:TPU:1, one launch (start us, length us, event | category | flops | bytes accessed | tf_op | source)
XLA Modules:
  0.0 524.3 jit_solution(3630794506368259424)
XLA Ops:
  8.2 6.6 %convolution_convert_fusion.1 = bf16[2048,128]{1,0:T(8,128)(2,1)} fusion(bf16[2048,2048]{1,0:T(8,128)(2,1)} %param.11, bf16[128,2048]{1,0:T(8,128)(2,1)S(1)} %copy-done), kind=kOutput, calls=%fused_computation.28 | convolution fusion | flops 1074003968 | bytes 9437184 | tf_op jit(solution)/shard_map/dot_general | solution.py:73
  14.9 72.1 %reduce-scatter.2.cloned.1.call-done = bf16[256,128]{1,0:T(8,128)(2,1)} async-done(((bf16[2048,128]{1,0:T(8,128)(2,1)}), bf16[256,128]{1,0:T(8,128)(2,1)}) %reduce-scatter.2.cloned.1.call-update) | async-done | bytes 65552 | tf_op jit(solution)/shard_map/reduce_scatter | solution.py:72
  87.9 1.1 broadcast_multiply_fusion
  89.0 7.1 %all-to-all-start = ((bf16[16,4,32,256]{3,2,1,0:T(8,128)(2,1)}), bf16[16,4,32,256]{3,2,1,0:T(8,128)(2,1)S(1)}, u32[]{:S(2)}, u32[]{:S(2)}) async-start(bf16[16,4,32,256]{3,2,1,0:T(8,128)(2,1)} %broadcast_multiply_fusion), calls=%async_computation.1 | async-start | bytes 2097152 | tf_op jit(solution)/shard_map/all_to_all | solution.py:89
  96.6 15.3 %all-to-all-done = bf16[16,4,32,256]{3,2,1,0:T(8,128)(2,1)S(1)} async-done(((bf16[16,4,32,256]{3,2,1,0:T(8,128)(2,1)}), bf16[16,4,32,256]{3,2,1,0:T(8,128)(2,1)S(1)}, u32[]{:S(2)}, u32[]{:S(2)}) %all-to-all-start) | async-done | bytes 1048608 | tf_op jit(solution)/shard_map/all_to_all | solution.py:89
  112.8 1.2 pad_maximum_fusion
  116.7 97.3 %all-gather.2.cloned.1.call-done = bf16[36864,256]{1,0:T(8,128)(2,1)} async-done(((bf16[2304,256]{1,0:T(8,128)(2,1)}), bf16[36864,256]{1,0:T(8,128)(2,1)}) %all-gather.2.cloned.1.call-update) | async-done | bytes 18874384 | tf_op jit(solution)/shard_map/all_gather | solution.py:120
  214.0 301.4 %while.15 = (s32[]{:T(128)}, f32[128,8]{0,1:T(8,128)S(1)}, f32[128,8]{0,1:T(8,128)S(1)}, f32[128,8,128]{2,0,1:T(8,128)}, s32[8,4608]{1,0:T(8,128)}, /*index=5*/b...) while((s32[]{:T(128)}, f32[128,8]{0,1:T(8,128)S(1)}, ...), condition=%wide.region_6.7_spmd.clone, body=%wide.region_3.6_spmd.clone.sunk | while | flops 2479437824 | bytes 67529864 | solution.py:43
  214.0 1.0 compare_reduce_fusion.3
  215.1 1.0 fusion.37
  216.0 3.9 and_or_fusion.2
  219.9 1.8 dynamic-slice_bitcast_fusion.2
  221.8 8.9 %fusion.38 = (f32[128,8]{0,1:T(8,128)S(1)}, f32[4608,128,8]{1,0,2:T(8,128)}) fusion(pred[128,4608]{0,1:T(8,128)(4,1)S(1)} %and_or_fusion.2, bf16[128,8,128]{2,0,1:T(8,128)(2,1)} %get-tuple-element.204, bf16[4608,256]{1,0:T(8,128)(2,1)S(1)} %dynamic-slice_bitcast_fusion.2), kind=kOutput, calls=%fused_computation.3.clone.1 | convolution fusion | flops 1222114304 | bytes 20910080 | tf_op jit(solution)/shard_map/while/body/eval_jaxpr/rgd,kd->rgk/dot_general | solution.py:14
  230.7 10.8 %fusion.39 = f32[128,8]{0,1:T(8,128)S(1)} fusion(f32[4608,128,8]{1,0,2:T(8,128)} %get-tuple-element.175, f32[128,8]{0,1:T(8,128)S(1)} %select_maximum_fusion.2, pred[128,4608]{0,1:T(8,128)(4,1)S(1)} %and_or_fusion.2), kind=kLoop, calls=%fused_computation.5.clone.1 | loop fusion | flops 23591936 | bytes 19472384 | tf_op jit(solution)/shard_map/while/body/eval_jaxpr/reduce_sum | solution.py:24
  241.5 10.1 %fusion.41 = f32[128,8,128]{2,0,1:T(8,128)} fusion(f32[4608,128,8]{1,0,2:T(8,128)} %get-tuple-element.175, f32[128,8]{0,1:T(8,128)S(1)} %select_maximum_fusion.2, pred[128,4608]{0,1:T(8,128)(4,1)S(1)} %and_or_fusion.2, bf16[4608,256]{1,0:T(8,128)(2,1)S(1)} %dynamic-slice_bitcast_fusion.2, f32[128,8,128]{2,0,1:T(8,128)} %get-tuple-element.191, ...), kind=kOutput, calls=%fused_computation.10.clone.1 | convolution fusion | flops 1231945728 | bytes 21700608 | tf_op jit(solution)/shard_map/while/body/eval_jaxpr/rgk,kd->rgd/dot_general | solution.py:25
  251.6 1.0 compare_reduce_fusion.3
  252.7 1.0 fusion.37
  253.6 3.9 and_or_fusion.2
  257.5 1.8 dynamic-slice_bitcast_fusion.2
  259.3 8.9 %fusion.38 = (f32[128,8]{0,1:T(8,128)S(1)}, f32[4608,128,8]{1,0,2:T(8,128)}) fusion(pred[128,4608]{0,1:T(8,128)(4,1)S(1)} %and_or_fusion.2, bf16[128,8,128]{2,0,1:T(8,128)(2,1)} %get-tuple-element.204, bf16[4608,256]{1,0:T(8,128)(2,1)S(1)} %dynamic-slice_bitcast_fusion.2), kind=kOutput, calls=%fused_computation.3.clone.1 | convolution fusion | flops 1222114304 | bytes 20910080 | tf_op jit(solution)/shard_map/while/body/eval_jaxpr/rgd,kd->rgk/dot_general | solution.py:14
  268.3 10.8 %fusion.39 = f32[128,8]{0,1:T(8,128)S(1)} fusion(f32[4608,128,8]{1,0,2:T(8,128)} %get-tuple-element.175, f32[128,8]{0,1:T(8,128)S(1)} %select_maximum_fusion.2, pred[128,4608]{0,1:T(8,128)(4,1)S(1)} %and_or_fusion.2), kind=kLoop, calls=%fused_computation.5.clone.1 | loop fusion | flops 23591936 | bytes 19472384 | tf_op jit(solution)/shard_map/while/body/eval_jaxpr/reduce_sum | solution.py:24
  279.1 10.2 %fusion.41 = f32[128,8,128]{2,0,1:T(8,128)} fusion(f32[4608,128,8]{1,0,2:T(8,128)} %get-tuple-element.175, f32[128,8]{0,1:T(8,128)S(1)} %select_maximum_fusion.2, pred[128,4608]{0,1:T(8,128)(4,1)S(1)} %and_or_fusion.2, bf16[4608,256]{1,0:T(8,128)(2,1)S(1)} %dynamic-slice_bitcast_fusion.2, f32[128,8,128]{2,0,1:T(8,128)} %get-tuple-element.191, ...), kind=kOutput, calls=%fused_computation.10.clone.1 | convolution fusion | flops 1231945728 | bytes 21700608 | tf_op jit(solution)/shard_map/while/body/eval_jaxpr/rgk,kd->rgd/dot_general | solution.py:25
  289.3 1.0 compare_reduce_fusion.3
  290.4 1.0 fusion.37
  291.3 3.9 and_or_fusion.2
  295.2 1.8 dynamic-slice_bitcast_fusion.2
  297.0 8.9 %fusion.38 = (f32[128,8]{0,1:T(8,128)S(1)}, f32[4608,128,8]{1,0,2:T(8,128)}) fusion(pred[128,4608]{0,1:T(8,128)(4,1)S(1)} %and_or_fusion.2, bf16[128,8,128]{2,0,1:T(8,128)(2,1)} %get-tuple-element.204, bf16[4608,256]{1,0:T(8,128)(2,1)S(1)} %dynamic-slice_bitcast_fusion.2), kind=kOutput, calls=%fused_computation.3.clone.1 | convolution fusion | flops 1222114304 | bytes 20910080 | tf_op jit(solution)/shard_map/while/body/eval_jaxpr/rgd,kd->rgk/dot_general | solution.py:14
  306.0 10.8 %fusion.39 = f32[128,8]{0,1:T(8,128)S(1)} fusion(f32[4608,128,8]{1,0,2:T(8,128)} %get-tuple-element.175, f32[128,8]{0,1:T(8,128)S(1)} %select_maximum_fusion.2, pred[128,4608]{0,1:T(8,128)(4,1)S(1)} %and_or_fusion.2), kind=kLoop, calls=%fused_computation.5.clone.1 | loop fusion | flops 23591936 | bytes 19472384 | tf_op jit(solution)/shard_map/while/body/eval_jaxpr/reduce_sum | solution.py:24
  316.8 10.2 %fusion.41 = f32[128,8,128]{2,0,1:T(8,128)} fusion(f32[4608,128,8]{1,0,2:T(8,128)} %get-tuple-element.175, f32[128,8]{0,1:T(8,128)S(1)} %select_maximum_fusion.2, pred[128,4608]{0,1:T(8,128)(4,1)S(1)} %and_or_fusion.2, bf16[4608,256]{1,0:T(8,128)(2,1)S(1)} %dynamic-slice_bitcast_fusion.2, f32[128,8,128]{2,0,1:T(8,128)} %get-tuple-element.191, ...), kind=kOutput, calls=%fused_computation.10.clone.1 | convolution fusion | flops 1231945728 | bytes 21700608 | tf_op jit(solution)/shard_map/while/body/eval_jaxpr/rgk,kd->rgd/dot_general | solution.py:25
  327.0 1.0 compare_reduce_fusion.3
  328.0 1.0 fusion.37
  329.0 3.9 and_or_fusion.2
  332.9 1.8 dynamic-slice_bitcast_fusion.2
  334.7 8.9 %fusion.38 = (f32[128,8]{0,1:T(8,128)S(1)}, f32[4608,128,8]{1,0,2:T(8,128)}) fusion(pred[128,4608]{0,1:T(8,128)(4,1)S(1)} %and_or_fusion.2, bf16[128,8,128]{2,0,1:T(8,128)(2,1)} %get-tuple-element.204, bf16[4608,256]{1,0:T(8,128)(2,1)S(1)} %dynamic-slice_bitcast_fusion.2), kind=kOutput, calls=%fused_computation.3.clone.1 | convolution fusion | flops 1222114304 | bytes 20910080 | tf_op jit(solution)/shard_map/while/body/eval_jaxpr/rgd,kd->rgk/dot_general | solution.py:14
  343.7 10.8 %fusion.39 = f32[128,8]{0,1:T(8,128)S(1)} fusion(f32[4608,128,8]{1,0,2:T(8,128)} %get-tuple-element.175, f32[128,8]{0,1:T(8,128)S(1)} %select_maximum_fusion.2, pred[128,4608]{0,1:T(8,128)(4,1)S(1)} %and_or_fusion.2), kind=kLoop, calls=%fused_computation.5.clone.1 | loop fusion | flops 23591936 | bytes 19472384 | tf_op jit(solution)/shard_map/while/body/eval_jaxpr/reduce_sum | solution.py:24
  354.5 10.2 %fusion.41 = f32[128,8,128]{2,0,1:T(8,128)} fusion(f32[4608,128,8]{1,0,2:T(8,128)} %get-tuple-element.175, f32[128,8]{0,1:T(8,128)S(1)} %select_maximum_fusion.2, pred[128,4608]{0,1:T(8,128)(4,1)S(1)} %and_or_fusion.2, bf16[4608,256]{1,0:T(8,128)(2,1)S(1)} %dynamic-slice_bitcast_fusion.2, f32[128,8,128]{2,0,1:T(8,128)} %get-tuple-element.191, ...), kind=kOutput, calls=%fused_computation.10.clone.1 | convolution fusion | flops 1231945728 | bytes 21700608 | tf_op jit(solution)/shard_map/while/body/eval_jaxpr/rgk,kd->rgd/dot_general | solution.py:25
  364.7 1.0 compare_reduce_fusion.3
  366.7 3.9 and_or_fusion.2
  370.6 1.8 dynamic-slice_bitcast_fusion.2
  372.4 8.9 %fusion.38 = (f32[128,8]{0,1:T(8,128)S(1)}, f32[4608,128,8]{1,0,2:T(8,128)}) fusion(pred[128,4608]{0,1:T(8,128)(4,1)S(1)} %and_or_fusion.2, bf16[128,8,128]{2,0,1:T(8,128)(2,1)} %get-tuple-element.204, bf16[4608,256]{1,0:T(8,128)(2,1)S(1)} %dynamic-slice_bitcast_fusion.2), kind=kOutput, calls=%fused_computation.3.clone.1 | convolution fusion | flops 1222114304 | bytes 20910080 | tf_op jit(solution)/shard_map/while/body/eval_jaxpr/rgd,kd->rgk/dot_general | solution.py:14
  381.3 10.8 %fusion.39 = f32[128,8]{0,1:T(8,128)S(1)} fusion(f32[4608,128,8]{1,0,2:T(8,128)} %get-tuple-element.175, f32[128,8]{0,1:T(8,128)S(1)} %select_maximum_fusion.2, pred[128,4608]{0,1:T(8,128)(4,1)S(1)} %and_or_fusion.2), kind=kLoop, calls=%fused_computation.5.clone.1 | loop fusion | flops 23591936 | bytes 19472384 | tf_op jit(solution)/shard_map/while/body/eval_jaxpr/reduce_sum | solution.py:24
  392.1 10.2 %fusion.41 = f32[128,8,128]{2,0,1:T(8,128)} fusion(f32[4608,128,8]{1,0,2:T(8,128)} %get-tuple-element.175, f32[128,8]{0,1:T(8,128)S(1)} %select_maximum_fusion.2, pred[128,4608]{0,1:T(8,128)(4,1)S(1)} %and_or_fusion.2, bf16[4608,256]{1,0:T(8,128)(2,1)S(1)} %dynamic-slice_bitcast_fusion.2, f32[128,8,128]{2,0,1:T(8,128)} %get-tuple-element.191, ...), kind=kOutput, calls=%fused_computation.10.clone.1 | convolution fusion | flops 1231945728 | bytes 21700608 | tf_op jit(solution)/shard_map/while/body/eval_jaxpr/rgk,kd->rgd/dot_general | solution.py:25
  402.4 1.0 compare_reduce_fusion.3
  403.4 1.0 fusion.37
  404.4 3.9 and_or_fusion.2
  408.3 1.8 dynamic-slice_bitcast_fusion.2
  410.1 8.9 %fusion.38 = (f32[128,8]{0,1:T(8,128)S(1)}, f32[4608,128,8]{1,0,2:T(8,128)}) fusion(pred[128,4608]{0,1:T(8,128)(4,1)S(1)} %and_or_fusion.2, bf16[128,8,128]{2,0,1:T(8,128)(2,1)} %get-tuple-element.204, bf16[4608,256]{1,0:T(8,128)(2,1)S(1)} %dynamic-slice_bitcast_fusion.2), kind=kOutput, calls=%fused_computation.3.clone.1 | convolution fusion | flops 1222114304 | bytes 20910080 | tf_op jit(solution)/shard_map/while/body/eval_jaxpr/rgd,kd->rgk/dot_general | solution.py:14
  419.0 10.8 %fusion.39 = f32[128,8]{0,1:T(8,128)S(1)} fusion(f32[4608,128,8]{1,0,2:T(8,128)} %get-tuple-element.175, f32[128,8]{0,1:T(8,128)S(1)} %select_maximum_fusion.2, pred[128,4608]{0,1:T(8,128)(4,1)S(1)} %and_or_fusion.2), kind=kLoop, calls=%fused_computation.5.clone.1 | loop fusion | flops 23591936 | bytes 19472384 | tf_op jit(solution)/shard_map/while/body/eval_jaxpr/reduce_sum | solution.py:24
  429.8 10.2 %fusion.41 = f32[128,8,128]{2,0,1:T(8,128)} fusion(f32[4608,128,8]{1,0,2:T(8,128)} %get-tuple-element.175, f32[128,8]{0,1:T(8,128)S(1)} %select_maximum_fusion.2, pred[128,4608]{0,1:T(8,128)(4,1)S(1)} %and_or_fusion.2, bf16[4608,256]{1,0:T(8,128)(2,1)S(1)} %dynamic-slice_bitcast_fusion.2, f32[128,8,128]{2,0,1:T(8,128)} %get-tuple-element.191, ...), kind=kOutput, calls=%fused_computation.10.clone.1 | convolution fusion | flops 1231945728 | bytes 21700608 | tf_op jit(solution)/shard_map/while/body/eval_jaxpr/rgk,kd->rgd/dot_general | solution.py:25
  440.1 1.0 compare_reduce_fusion.3
  441.1 1.0 fusion.37
  442.1 3.9 and_or_fusion.2
  446.0 1.8 dynamic-slice_bitcast_fusion.2
  447.8 8.9 %fusion.38 = (f32[128,8]{0,1:T(8,128)S(1)}, f32[4608,128,8]{1,0,2:T(8,128)}) fusion(pred[128,4608]{0,1:T(8,128)(4,1)S(1)} %and_or_fusion.2, bf16[128,8,128]{2,0,1:T(8,128)(2,1)} %get-tuple-element.204, bf16[4608,256]{1,0:T(8,128)(2,1)S(1)} %dynamic-slice_bitcast_fusion.2), kind=kOutput, calls=%fused_computation.3.clone.1 | convolution fusion | flops 1222114304 | bytes 20910080 | tf_op jit(solution)/shard_map/while/body/eval_jaxpr/rgd,kd->rgk/dot_general | solution.py:14
  456.7 10.8 %fusion.39 = f32[128,8]{0,1:T(8,128)S(1)} fusion(f32[4608,128,8]{1,0,2:T(8,128)} %get-tuple-element.175, f32[128,8]{0,1:T(8,128)S(1)} %select_maximum_fusion.2, pred[128,4608]{0,1:T(8,128)(4,1)S(1)} %and_or_fusion.2), kind=kLoop, calls=%fused_computation.5.clone.1 | loop fusion | flops 23591936 | bytes 19472384 | tf_op jit(solution)/shard_map/while/body/eval_jaxpr/reduce_sum | solution.py:24
  467.5 10.2 %fusion.41 = f32[128,8,128]{2,0,1:T(8,128)} fusion(f32[4608,128,8]{1,0,2:T(8,128)} %get-tuple-element.175, f32[128,8]{0,1:T(8,128)S(1)} %select_maximum_fusion.2, pred[128,4608]{0,1:T(8,128)(4,1)S(1)} %and_or_fusion.2, bf16[4608,256]{1,0:T(8,128)(2,1)S(1)} %dynamic-slice_bitcast_fusion.2, f32[128,8,128]{2,0,1:T(8,128)} %get-tuple-element.191, ...), kind=kOutput, calls=%fused_computation.10.clone.1 | convolution fusion | flops 1231945728 | bytes 21700608 | tf_op jit(solution)/shard_map/while/body/eval_jaxpr/rgk,kd->rgd/dot_general | solution.py:25
  477.8 1.0 compare_reduce_fusion.3
  478.8 1.0 fusion.37
  479.8 3.9 and_or_fusion.2
  483.7 1.8 dynamic-slice_bitcast_fusion.2
  485.5 8.9 %fusion.38 = (f32[128,8]{0,1:T(8,128)S(1)}, f32[4608,128,8]{1,0,2:T(8,128)}) fusion(pred[128,4608]{0,1:T(8,128)(4,1)S(1)} %and_or_fusion.2, bf16[128,8,128]{2,0,1:T(8,128)(2,1)} %get-tuple-element.204, bf16[4608,256]{1,0:T(8,128)(2,1)S(1)} %dynamic-slice_bitcast_fusion.2), kind=kOutput, calls=%fused_computation.3.clone.1 | convolution fusion | flops 1222114304 | bytes 20910080 | tf_op jit(solution)/shard_map/while/body/eval_jaxpr/rgd,kd->rgk/dot_general | solution.py:14
  494.4 10.8 %fusion.39 = f32[128,8]{0,1:T(8,128)S(1)} fusion(f32[4608,128,8]{1,0,2:T(8,128)} %get-tuple-element.175, f32[128,8]{0,1:T(8,128)S(1)} %select_maximum_fusion.2, pred[128,4608]{0,1:T(8,128)(4,1)S(1)} %and_or_fusion.2), kind=kLoop, calls=%fused_computation.5.clone.1 | loop fusion | flops 23591936 | bytes 19472384 | tf_op jit(solution)/shard_map/while/body/eval_jaxpr/reduce_sum | solution.py:24
  505.2 10.2 %fusion.41 = f32[128,8,128]{2,0,1:T(8,128)} fusion(f32[4608,128,8]{1,0,2:T(8,128)} %get-tuple-element.175, f32[128,8]{0,1:T(8,128)S(1)} %select_maximum_fusion.2, pred[128,4608]{0,1:T(8,128)(4,1)S(1)} %and_or_fusion.2, bf16[4608,256]{1,0:T(8,128)(2,1)S(1)} %dynamic-slice_bitcast_fusion.2, f32[128,8,128]{2,0,1:T(8,128)} %get-tuple-element.191, ...), kind=kOutput, calls=%fused_computation.10.clone.1 | convolution fusion | flops 1231945728 | bytes 21700608 | tf_op jit(solution)/shard_map/while/body/eval_jaxpr/rgk,kd->rgd/dot_general | solution.py:25
  515.5 2.0 copy_bitcast_fusion
  (79 shorter events, 7.2 us)
Async XLA Ops:
  7.2 1.0 copy-start
  7.2 7.6 %copy-start.6 = (s32[64]{0:T(128)S(1)}, s32[64]{0:T(128)}, u32[]{:S(2)}) copy-start(s32[64]{0:T(128)} %param.16) | copy-start | bytes 772
  7.2 89.0 %copy-start.7 = (s32[64]{0:T(128)S(1)}, s32[64]{0:T(128)}, u32[]{:S(2)}) copy-start(s32[64]{0:T(128)} %param.17) | copy-start | bytes 772
  7.2 105.6 %copy-start.2 = (bf16[2048,128]{1,0:T(8,128)(2,1)S(1)}, bf16[2048,128]{1,0:T(8,128)(2,1)}, u32[]{:S(2)}) copy-start(bf16[2048,128]{1,0:T(8,128)(2,1)} %param.14) | copy-start | bytes 1572868
  7.2 105.6 %copy-start.3 = (bf16[2048,128]{1,0:T(8,128)(2,1)S(1)}, bf16[2048,128]{1,0:T(8,128)(2,1)}, u32[]{:S(2)}) copy-start(bf16[2048,128]{1,0:T(8,128)(2,1)} %param.13) | copy-start | bytes 1572868
  7.2 107.7 %copy-start.5 = (s32[16]{0:T(128)S(1)}, s32[16]{0:T(128)}, u32[]{:S(2)}) copy-start(s32[16]{0:T(128)} %param.15) | copy-start | bytes 196
  7.2 108.5 %copy-start.4 = (bf16[128,1024]{1,0:T(8,128)(2,1)S(1)}, bf16[128,1024]{1,0:T(8,128)(2,1)}, u32[]{:S(2)}) copy-start(bf16[128,1024]{1,0:T(8,128)(2,1)} %param.12) | copy-start | bytes 786436
  7.2 79.7 %reduce-scatter.2.cloned.1.call-start = ((), (), s32[]{:S(2)}) async-start(), calls=%async_computation.2 | async-start | bytes 589824 | tf_op jit(solution)/shard_map/reduce_scatter | solution.py:72
  89.0 22.8 %all-to-all-start = ((bf16[16,4,32,256]{3,2,1,0:T(8,128)(2,1)}), bf16[16,4,32,256]{3,2,1,0:T(8,128)(2,1)S(1)}, u32[]{:S(2)}, u32[]{:S(2)}) async-start(bf16[16,4,32,256]{3,2,1,0:T(8,128)(2,1)} %broadcast_multiply_fusion), calls=%async_computation.1 | async-start | bytes 2097152 | tf_op jit(solution)/shard_map/all_to_all | solution.py:89
  96.1 117.9 %all-gather.2.cloned.1.call-start = ((), (), s32[]{:S(2)}) async-start(), calls=%async_computation.3 | async-start | bytes 20054016 | tf_op jit(solution)/shard_map/all_gather | solution.py:120
  112.8 2.1 copy-start.1
Sparse Core Ops, SparseCore 0:
  14.9 72.0 reduce-scatter.1
  114.1 99.8 all-gather.1
where the time goes:
time: 526 us; the launch traced here: 524 us
  waiting for transfers between devices  185 us (35%)
  matrix products  160 us (30%)
  other arithmetic  131 us (25%)
  local copies, waits for them, and re-layouts  27.2 us (5%)
  between operations  14.3 us (3%)
  starting transfers between devices  7.16 us (1%)
    all_gather x1, waiting for transfers between devices, body(): lax.all_gather(key_vals, 'ctx', axis=0, tiled=True)  97.3 us
    reduce_sum x8, other arithmetic, block_update(): run_sum = run_sum * rescale + jnp.sum(weights, axis=-1)  86.2 us
    dot_general x8, matrix products, block_update(): jnp.einsum('rgk,kd->rgd', weights.astype(jnp.bfloat16), key_block[:, head...  81.9 us
    reduce_scatter x1, waiting for transfers between devices, body(): lax.psum_scatter(lax.dot_general(kv_weight, tokens, (((0,), (1,)), ((), (...  72.1 us
    dot_general x8, matrix products, block_update(): jnp.einsum('rgd,kd->rgk', query_rows, key_block[:, :head_dim], preferred_...  71.3 us
    or x8, other arithmetic, block_update(): (key_codes[None, :] == -1) | (key_codes[None, :] >= 0) & (key_codes[None,...  31 us
    all_to_all x1, waiting for transfers between devices, body(): lax.all_to_all(outgoing, 'ctx', split_axis=0, concat_axis=0, tiled=True)  15.3 us
    squeeze x8, local copies, waits for them, and re-layouts, attend_keys(): lax.scan(advance, run_state, (key_vals.reshape(blocks, block_size, key_va...  14.6 us
  transfers between devices with their start and end apart: 3, of which 3 were waited for; matrix products, arithmetic and copies ran while one was open for 1% of the time, Pallas kernels for 0%

commit v1 on v0

v1 whole, which is shorter than its diff:
```python
import functools

import jax
import jax.numpy as jnp
from jax import lax
from jax.experimental import pallas as pl
from jax.experimental.pallas import tpu as pltpu
from jax.sharding import PartitionSpec as P

PAGE = 32
HD = 128
LOG2E = 1.4426950408889634
SCALE = LOG2E / HD**0.5
BIG = 2.0**100
F32 = jnp.float32
BF16 = jnp.bfloat16
VMEM_LIMIT = 56 * 2**20


def nt_dot(a, b):
    return lax.dot_general(a, b, (((1,), (1,)), ((), ())), preferred_element_type=F32)


def nn_dot(a, b):
    return lax.dot_general(a, b, (((1,), (0,)), ((), ())), preferred_element_type=F32)


def vmem_spec():
    return pl.BlockSpec(memory_space=pltpu.VMEM)


def smem_spec():
    return pl.BlockSpec(memory_space=pltpu.SMEM)


def project_kernel(tok_ref, w_ref, out_ref):
    out_ref[0] = nn_dot(tok_ref[...], w_ref[...]).astype(BF16)


def project(tokens, kv_weight):
    rows, depth = tokens.shape
    heads = kv_weight.shape[1] // (2 * HD)
    return pl.pallas_call(
        project_kernel,
        grid=(heads,),
        in_specs=[
            pl.BlockSpec((rows, depth), lambda h: (0, 0)),
            pl.BlockSpec((depth, 2 * HD), lambda h: (0, h)),
        ],
        out_specs=pl.BlockSpec((1, rows, 2 * HD), lambda h: (h, 0, 0)),
        out_shape=jax.ShapeDtypeStruct((heads, rows, 2 * HD), BF16),
        compiler_params=pltpu.CompilerParams(vmem_limit_bytes=VMEM_LIMIT),
        cost_estimate=pl.CostEstimate(
            flops=2 * rows * depth * heads * 2 * HD,
            bytes_accessed=2 * depth * heads * 2 * HD,
            transcendentals=0,
        ),
        name="project",
    )(tokens, kv_weight)


def attend_kernel(cfg, *refs):
    nq, nseg, seg, owner_xor, base, shifts, state_in, fresh, final = cfg
    refs = list(refs)
    take = lambda n: [refs.pop(0) for _ in range(n)]
    (len_ref,) = take(1)
    q_refs = take(nq)
    k_refs = take(nseg)
    v_refs = take(nseg)
    f_refs = take(4) if fresh else []
    st_in = take(3) if state_in else []
    outs = take(1) if final else take(3)
    qb, kb, vb, acc, ll, mm, sems = refs
    me = lax.axis_index("ctx")
    my_y = me // 4
    my_q = me % 4
    step = pl.program_id(0)
    rows = qb.shape[0]
    groups = rows // 128

    copies = []
    for s in range(nseg):
        copies.append(
            pltpu.make_async_copy(k_refs[s], kb.at[pl.ds(s * seg, seg)], sems.at[2 * s])
        )
        copies.append(
            pltpu.make_async_copy(v_refs[s], vb.at[pl.ds(s * seg, seg)], sems.at[2 * s + 1])
        )

    @pl.when(step == 0)
    def _():
        for c in copies:
            c.start()
        if fresh:
            for d in range(4):
                at = pl.ds(pl.multiple_of(nseg * seg + (my_q ^ d) * 128, 128), 128)
                kb[at, :] = f_refs[d][:, :HD]
                vb[at, :] = f_refs[d][:, HD:]

    for i in range(nq):

        @pl.when(step == i)
        def _():
            for g in range(groups):
                qb[g * 128 : (g + 1) * 128, :] = q_refs[i][:, g * 128 : (g + 1) * 128]

    @pl.when(step == 0)
    def _():
        for c in copies:
            c.wait()

    if state_in:
        mm[...] = st_in[2][0]
    else:
        top = jnp.max(nt_dot(qb[...], kb[:256, :]), axis=-1, keepdims=True) * SCALE
        mm[...] = jnp.broadcast_to(top.astype(BF16).astype(F32), mm.shape)

    query_y = shifts[0]
    for i in range(1, nq):
        query_y = jnp.where(step == i, shifts[i], query_y)
    query_y = lax.rem(my_y + 4 - query_y, 4)

    def masked(vals, size, limit, slope, fill):
        col = lax.broadcasted_iota(jnp.int32, (rows, size), 1)
        row = lax.rem(lax.broadcasted_iota(jnp.int32, (rows, size), 0), 128)
        return jnp.where(col <= limit + row * slope, vals, fill)

    def accumulate(at, size, limit=None, slope=None):
        at = pl.ds(pl.multiple_of(at, 128), size)
        s = nt_dot(qb[...], kb[at, :])
        tops = jnp.concatenate([mm[...]] * (size // 128), axis=1)
        p = jnp.exp2(s * SCALE - tops)
        if limit is not None:
            p = masked(p, size, limit, slope, 0.0)
        acc[...] += nn_dot(p.astype(BF16), vb[at, :])
        total = ll[...]
        for g in range(size // 128):
            total = total + p[:, g * 128 : (g + 1) * 128]
        ll[...] = total

    def segment(s):
        owner = me ^ owner_xor[0]
        for i in range(1, nseg):
            owner = jnp.where(s == i, me ^ owner_xor[i], owner)
        if fresh:
            owner = jnp.minimum(owner, 15)
        length = jnp.clip(len_ref[owner] - base, 0, seg)
        whole = length // 512 * 512
        rest = length - whole
        limit = rest - 1
        slope = 0
        if fresh:
            is_fresh = s == nseg
            diagonal = query_y == my_y
            whole = jnp.where(is_fresh, jnp.where(query_y > my_y, 512, 0), whole)
            rest = jnp.where(is_fresh, jnp.where(diagonal, 512, 0), rest)
            limit = jnp.where(is_fresh, my_q * 128, limit)
            slope = jnp.where(is_fresh, 1, 0)
        return s * seg, whole, rest, limit, slope

    nsegs = nseg + (1 if fresh else 0)

    def sweep():
        acc[...] = jnp.zeros_like(acc)
        ll[...] = jnp.zeros_like(ll)

        def one(s, carry):
            start, whole, rest, limit, slope = segment(s)
            wide = whole // 1024

            def wide_step(j, c):
                accumulate(start + j * 1024, 1024)
                return c

            lax.fori_loop(0, wide, wide_step, 0)

            @pl.when(whole > wide * 1024)
            def _():
                accumulate(start + wide * 1024, 512)

            @pl.when(rest > 256)
            def _():
                accumulate(start + whole, 512, limit, slope)

            @pl.when((rest > 0) & (rest <= 256))
            def _():
                accumulate(start + whole, 256, limit, slope)

            return carry

        lax.fori_loop(0, nsegs, one, 0)

    def raise_tops():
        def one(s, carry):
            start, whole, rest, limit, slope = segment(s)

            def part(j, c):
                at = pl.ds(pl.multiple_of(start + j * 128, 128), 128)
                s_now = nt_dot(qb[...], kb[at, :]) * SCALE
                edge = jnp.where(
                    j * 128 < whole, 128, limit - (j * 128 - whole)
                )
                tilt = jnp.where(j * 128 < whole, 0, slope)
                s_now = masked(s_now, 128, edge, tilt, -3.0e38)
                top = jnp.max(s_now, axis=-1, keepdims=True)
                mm[...] = jnp.maximum(mm[...], top.astype(BF16).astype(F32))
                return c

            return lax.fori_loop(0, (whole + rest + 127) // 128, part, carry)

        lax.fori_loop(0, nsegs, one, 0)

    def attempt(turn):
        @pl.when(turn == 1)
        def _():
            raise_tops()

        sweep()
        fits = jnp.max(ll[...]) < BIG
        return jnp.where((turn == 0) & jnp.logical_not(fits), 1, 2)

    lax.while_loop(lambda turn: turn < 2, attempt, 0)

    if state_in:
        decay = jnp.exp2(st_in[2][0] - mm[...])
        acc[...] += st_in[0][0] * decay
        ll[...] += st_in[1][0] * decay
    if not final:
        outs[0][0] = acc[...]
        outs[1][0] = ll[...]
        outs[2][0] = mm[...]
        return
    out = outs[0]
    lane = lax.broadcasted_iota(jnp.int32, (128, 128), 1)
    side = jnp.zeros((128, 128), F32)
    for g in range(groups):
        part = slice(g * 128, (g + 1) * 128)
        out[0, :, part] = acc[part, :].astype(BF16)
        total = jnp.sum(ll[part, :], axis=-1, keepdims=True)
        high = total.astype(BF16).astype(F32)
        side = jnp.where(lane == g, mm[part, :], side)
        side = jnp.where(lane == 8 + g, high, side)
        side = jnp.where(lane == 16 + g, total - high, side)
    out[0, :, groups * 128 :] = side.astype(BF16)


def attend(lengths, qs, ks, vs, owner_xor, base, shifts, state=None, fresh=None, final=False, share=0.7):
    nq, nseg, seg = len(qs), len(ks), ks[0].shape[0]
    width = qs[0].shape[1]
    rows = width
    cfg = (nq, nseg, seg, owner_xor, base, shifts, state is not None, fresh is not None, final)
    state_spec = pl.BlockSpec((1, rows, HD), lambda i: (i, 0, 0))
    any_spec = pl.BlockSpec(memory_space=pl.ANY)
    args = [lengths, *qs, *ks, *vs]
    in_specs = [smem_spec()] + [vmem_spec()] * nq + [any_spec] * (2 * nseg)
    if fresh is not None:
        args += list(fresh)
        in_specs += [vmem_spec()] * 4
    if state is not None:
        args += list(state)
        in_specs += [state_spec] * 3
    if final:
        out_specs = [pl.BlockSpec((1, 128, width + 128), lambda i: (i, 0, 0))]
        out_shape = [jax.ShapeDtypeStruct((nq, 128, width + 128), BF16)]
    else:
        out_specs = [state_spec] * 3
        out_shape = [jax.ShapeDtypeStruct((nq, rows, HD), F32)] * 3
    keys = nseg * seg + (512 if fresh is not None else 0)
    return pl.pallas_call(
        functools.partial(attend_kernel, cfg),
        grid=(nq,),
        in_specs=in_specs,
        out_specs=out_specs,
        out_shape=out_shape,
        scratch_shapes=[
            pltpu.VMEM((rows, HD), BF16),
            pltpu.VMEM((keys, HD), BF16),
            pltpu.VMEM((keys, HD), BF16),
            pltpu.VMEM((rows, HD), F32),
            pltpu.VMEM((rows, HD), F32),
            pltpu.VMEM((rows, HD), F32),
            pltpu.SemaphoreType.DMA((2 * nseg,)),
        ],
        compiler_params=pltpu.CompilerParams(vmem_limit_bytes=VMEM_LIMIT),
        cost_estimate=pl.CostEstimate(
            flops=int(share * 8 * nq * rows * keys * HD),
            bytes_accessed=4 * keys * HD,
            transcendentals=0,
        ),
        name="attend",
    )(*args)


def merge_kernel(*refs):
    parts, out = refs[:-1], refs[-1]
    groups = out.shape[1] // 128
    sides = [r[0, :, groups * 128 :].astype(F32) for r in parts]
    for g in range(groups):
        tops = [s[:, g : g + 1] for s in sides]
        sums = [s[:, 8 + g : 9 + g] + s[:, 16 + g : 17 + g] for s in sides]
        top = functools.reduce(jnp.maximum, tops)
        scales = [jnp.exp2(t - top) for t in tops]
        total = sum(a * b for a, b in zip(scales, sums))
        part = slice(g * 128, (g + 1) * 128)
        mixed = sum(a * r[0, :, part].astype(F32) for a, r in zip(scales, parts))
        out[:, part] = (mixed / total).astype(BF16)


def merge(parts):
    rows, width = parts[0].shape[1:]
    return pl.pallas_call(
        merge_kernel,
        in_specs=[vmem_spec()] * len(parts),
        out_specs=vmem_spec(),
        out_shape=jax.ShapeDtypeStruct((rows, width - 128), BF16),
        compiler_params=pltpu.CompilerParams(vmem_limit_bytes=VMEM_LIMIT),
        name="merge",
    )(*parts)


def pages_kernel(owner_ref, slot_ref, *refs):
    quads, out = refs[:-1], refs[-1]
    me = lax.axis_index("ctx")
    my_y = me // 4
    my_q = me % 4
    out[...] = jnp.zeros_like(out)
    for k in range(4):
        block_y = lax.rem(my_y + 4 - k, 4)

        def one(i, carry):
            page = block_y * 16 + i

            @pl.when(owner_ref[page] == me)
            def _():
                src = (my_q ^ (i // 4)) * 128 + (i % 4) * PAGE
                dst = slot_ref[page] * PAGE
                out[pl.ds(pl.multiple_of(dst, PAGE), PAGE), :] = quads[k][
                    pl.ds(pl.multiple_of(src, PAGE), PAGE), :
                ]

            return carry

        lax.fori_loop(0, 16, one, 0)


def pick_pages(page_owner, page_slot, quads):
    return pl.pallas_call(
        pages_kernel,
        in_specs=[smem_spec()] * 2 + [vmem_spec()] * len(quads),
        out_specs=vmem_spec(),
        out_shape=jax.ShapeDtypeStruct((8 * PAGE, 2 * HD), BF16),
        compiler_params=pltpu.CompilerParams(vmem_limit_bytes=VMEM_LIMIT),
        name="pages",
    )(page_owner, page_slot, *quads)


def flip(x, bits):
    return lax.ppermute(x, "ctx", [(i, i ^ bits) for i in range(16)])


def turn(x, k):
    return lax.ppermute(x, "ctx", [(i, (i + 4 * k) % 16) for i in range(16)])


def body(
    tokens, kv_weight, queries, cache_keys, cache_values, cache_lengths, page_owner, page_slot
):
    half = cache_keys.shape[0] // 2
    others = {k: turn(queries, k) for k in (1, 3, 2)}
    k_core, v_core = flip(cache_keys, 1), flip(cache_values, 1)
    far = []
    for c in range(2):
        part = slice(c * half, (c + 1) * half)
        kz, vz = flip(cache_keys[part], 2), flip(cache_values[part], 2)
        far.append(((kz, flip(kz, 1)), (vz, flip(vz, 1))))

    partial = project(tokens, kv_weight)
    gathered = lax.all_to_all(partial, "tp", 0, 0, tiled=True)
    fresh0 = jnp.sum(gathered.astype(F32), axis=0).astype(BF16)
    fresh = [fresh0] + [flip(fresh0, d) for d in (1, 2, 3)]
    quad = jnp.concatenate(fresh, axis=0)
    quads = [quad] + [turn(quad, k) for k in (1, 2, 3)]
    kv_pages = pick_pages(page_owner, page_slot, quads)

    near_k, near_v = (cache_keys, k_core), (cache_values, v_core)
    own = attend(cache_lengths, [queries], near_k, near_v, (0, 1), 0, (0,))
    order = (1, 3, 2)
    rest = attend(
        cache_lengths, [others[k] for k in order], near_k, near_v, (0, 1), 0, order
    )
    rest = attend(
        cache_lengths, [others[k] for k in order], far[0][0], far[0][1], (2, 3), 0, order,
        state=rest,
    )
    (sent,) = attend(
        cache_lengths, [others[k] for k in order], far[1][0], far[1][1], (2, 3), half, order,
        state=rest, fresh=fresh, final=True,
    )
    back = [turn(sent[i : i + 1], 4 - k) for i, k in enumerate(order)]
    own = attend(
        cache_lengths, [queries], far[0][0], far[0][1], (2, 3), 0, (0,), state=own
    )
    (mine,) = attend(
        cache_lengths, [queries], far[1][0], far[1][1], (2, 3), half, (0,),
        state=own, fresh=fresh, final=True,
    )
    attended = merge([mine, *back])
    return (attended, kv_pages)


def solution(mesh):
    placed = (
        P("ctx", "tp"),
        P("tp", None),
        P("ctx", "tp"),
        P("ctx", "tp"),
        P("ctx", "tp"),
        P(),
        P(),
        P(),
    )
    return jax.shard_map(
        body,
        mesh=mesh,
        in_specs=placed,
        out_specs=(P("ctx", "tp"), P("ctx", "tp")),
        check_vma=False,
    )
```

time: 526 us -> 150 us (0.29)
  waiting for transfers between devices: 185 us -> 20.8 us
  matrix products: 160 us -> 0 us
  other arithmetic: 131 us -> 0.09 us
  Pallas kernels: 0 us -> 89.6 us
  starting transfers between devices: 7.16 us -> 31.2 us
  local copies, waits for them, and re-layouts: 27.2 us -> 5.48 us
  between operations: 14.3 us -> 1 us
    dot_general x18 -> x0, matrix products: 160 us -> none  [the longest x8 81.9 us: block_update(): jnp.einsum('rgk,kd->rgd', weights.astype(jnp.bfloat16), key_block[:, head...]
    all_gather x1 -> x0, waiting for transfers between devices: 97.3 us -> none  [body(): lax.all_gather(key_vals, 'ctx', axis=0, tiled=True)]
    pallas_call x0 -> x9, Pallas kernels: none -> 89.6 us  [the longest x6 76.1 us: attend(): pl.pallas_call(functools.partial(attend_kernel, cfg), grid=(nq,), in_spec...]
    reduce_sum x9 -> x1, other arithmetic: 86.6 us -> 0.07 us  [body(): fresh0 = jnp.sum(gathered.astype(F32), axis=0).astype(BF16)]
    reduce_scatter x1 -> x0, waiting for transfers between devices: 72.1 us -> none  [body(): lax.psum_scatter(lax.dot_general(kv_weight, tokens, (((0,), (1,)), ((), (...]
    or x8 -> x0, other arithmetic: 31 us -> none  [block_update(): (key_codes[None, :] == -1) | (key_codes[None, :] >= 0) & (key_codes[None,...]
    ppermute x0 -> x22, starting transfers between devices: none -> 23.7 us  [the longest x13 14.7 us: flip(): return lax.ppermute(x, 'ctx', [(i, i ^ bits) for i in range(16)])]
    ppermute x0 -> x22, waiting for transfers between devices: none -> 15.2 us  [the longest x13 15.1 us: flip(): return lax.ppermute(x, 'ctx', [(i, i ^ bits) for i in range(16)])]
  transfers between devices with their start and end apart: 3 -> 23, of which waited for: 3 -> 6; matrix products, arithmetic and copies ran while one was open for 1% -> 1% of each run, Pallas kernels for 0% -> 59%
where the time goes in v1:
time: 150 us; the launch traced here: 148 us
  Pallas kernels  89.6 us (60%)
  starting transfers between devices  31.2 us (21%)
  waiting for transfers between devices  20.8 us (14%)
  local copies, waits for them, and re-layouts  5.48 us (4%)
    pallas_call x6, Pallas kernels, attend(): pl.pallas_call(functools.partial(attend_kernel, cfg), grid=(nq,), in_spec...  76.1 us
    ppermute x13, waiting for transfers between devices, flip(): return lax.ppermute(x, 'ctx', [(i, i ^ bits) for i in range(16)])  15.1 us
    ppermute x13, starting transfers between devices, flip(): return lax.ppermute(x, 'ctx', [(i, i ^ bits) for i in range(16)])  14.7 us
    ppermute x9, starting transfers between devices, turn(): return lax.ppermute(x, 'ctx', [(i, (i + 4 * k) % 16) for i in range(16)])  9.01 us
    pallas_call x1, Pallas kernels, project(): pl.pallas_call(project_kernel, grid=(heads,), in_specs=[pl.BlockSpec((row...  7.82 us
    all_to_all x1, starting transfers between devices, body(): gathered = lax.all_to_all(partial, 'tp', 0, 0, tiled=True)  7.47 us
    all_to_all x1, waiting for transfers between devices, body(): gathered = lax.all_to_all(partial, 'tp', 0, 0, tiled=True)  5.6 us
    unnamed x46, local copies, waits for them, and re-layouts  4.2 us
  transfers between devices with their start and end apart: 23, of which 6 were waited for; matrix products, arithmetic and copies ran while one was open for 1% of the time, Pallas kernels for 59%

profile of v1, /device:TPU:1, one launch (start us, length us, event | category | flops | bytes accessed | tf_op | source)
XLA Modules:
  0.0 148.1 jit_solution(11936781417472467895)
XLA Ops:
  0.6 0.0 copy-start.2
  0.6 2.2 %collective-permute-start.13 = (bf16[128,1024]{1,0:T(8,128)(2,1)}, bf16[128,1024]{1,0:T(8,128)(2,1)}, u32[]{:S(2)}, u32[]{:S(2)}) collective-permute-start(bf16[128,1024]{1,0:T(8,128)(2,1)} %refs_1_.5), channel_id=1, source_target_pairs={{0,32},{8,40},{16,48},{24,56},{32,64},{40,72},{48,80},{56,88},{64,... | collective-permute-start | bytes 786440 | tf_op jit(solution)/shard_map/ppermute | solution.py:362
  2.8 1.5 %collective-permute-start.14 = (bf16[128,1024]{1,0:T(8,128)(2,1)}, bf16[128,1024]{1,0:T(8,128)(2,1)}, u32[]{:S(2)}, u32[]{:S(2)}) collective-permute-start(bf16[128,1024]{1,0:T(8,128)(2,1)} %refs_1_.5), channel_id=1, source_target_pairs={{0,96},{8,104},{16,112},{24,120},{32,0},{40,8},{48,16},{56,24},{64... | collective-permute-start | bytes 786440 | tf_op jit(solution)/shard_map/ppermute | solution.py:362
  4.4 1.6 %collective-permute-start.15 = (bf16[128,1024]{1,0:T(8,128)(2,1)}, bf16[128,1024]{1,0:T(8,128)(2,1)}, u32[]{:S(2)}, u32[]{:S(2)}) collective-permute-start(bf16[128,1024]{1,0:T(8,128)(2,1)} %refs_1_.5), channel_id=1, source_target_pairs={{0,64},{8,72},{16,80},{24,88},{32,96},{40,104},{48,112},{56,120},{... | collective-permute-start | bytes 786440 | tf_op jit(solution)/shard_map/ppermute | solution.py:362
  5.9 7.8 %project.1 = bf16[8,128,256]{2,1,0:T(8,128)(2,1)} custom-call(bf16[128,2048]{1,0:T(8,128)(2,1)} %tok_ref.1, bf16[2048,2048]{1,0:T(8,128)(2,1)} %w_ref.1), custom_call_target="tpu_custom_call" | custom-call | flops 1073741824 | bytes 8388608 | tf_op jit(solution)/shard_map/project/pallas_call | solution.py:43
  13.7 7.5 %all-to-all-start = ((bf16[8,128,256]{2,1,0:T(8,128)(2,1)}), bf16[8,128,256]{2,1,0:T(8,128)(2,1)S(1)}, u32[]{:S(2)}, u32[]{:S(2)}) async-start(bf16[8,128,256]{2,1,0:T(8,128)(2,1)} %project.1), calls=%async_computation | async-start | bytes 1048576 | tf_op jit(solution)/shard_map/all_to_all | solution.py:378
  21.3 0.8 collective-permute-start.9
  22.1 2.1 %collective-permute-start.11 = (bf16[2048,128]{1,0:T(8,128)(2,1)S(1)}, bf16[2048,128]{1,0:T(8,128)(2,1)S(1)}, u32[]{:S(2)}, u32[]{:S(2)}) collective-permute-start(bf16[2048,128]{1,0:T(8,128)(2,1)S(1)} %copy-done.1), channel_id=1, source_target_pairs={{0,8},{8,0},{16,24},{24,16},{32,40},{40,32},{48,56},{56,48},{64,72... | collective-permute-start | bytes 1572872 | tf_op jit(solution)/shard_map/ppermute | solution.py:358
  24.2 0.0 collective-permute-done.13.refs_1_
  24.2 0.1 collective-permute-start.12
  24.2 5.6 %all-to-all-done = bf16[8,128,256]{2,1,0:T(8,128)(2,1)S(1)} async-done(((bf16[8,128,256]{2,1,0:T(8,128)(2,1)}), bf16[8,128,256]{2,1,0:T(8,128)(2,1)S(1)}, u32[]{:S(2)}, u32[]{:S(2)}) %all-to-all-start) | async-done | bytes 524320 | tf_op jit(solution)/shard_map/all_to_all | solution.py:378
  29.8 0.1 reduce_sum.12.refs_6_.refs_8_
  29.9 0.0 copy-start.9
  29.9 0.0 collective-permute-done.14.refs_2_
  29.9 4.1 %collective-permute-start.4 = (bf16[128,256]{1,0:T(8,128)(2,1)S(1)}, bf16[128,256]{1,0:T(8,128)(2,1)S(1)}, u32[]{:S(2)}, u32[]{:S(2)}) collective-permute-start(bf16[128,256]{1,0:T(8,128)(2,1)S(1)} %reduce_sum.12.refs_6_.refs_8_), channel_id=1, source_target_pairs={{0,8},{8,0},{16,24},{24,16},{32,40},{40,32},{48,56},{56,48},{64,72... | collective-permute-start | bytes 196616 | tf_op jit(solution)/shard_map/ppermute | solution.py:358
  34.1 0.0 collective-permute-done.15.refs_3_
  34.1 0.8 collective-permute-start.5
  34.9 0.0 collective-permute-done.9.refs_4_.refs_6_
  34.9 0.9 collective-permute-start.6
  35.8 0.0 collective-permute-done.4.refs_7_.refs_9_
  35.9 0.9 collective-permute-start.7
  36.8 1.0 collective-permute-done.5.refs_8_.refs_10_
  37.7 0.8 collective-permute-start
  38.5 1.2 collective-permute-done.6.refs_9_.refs_11_
  39.7 0.9 collective-permute-start.2
  40.6 4.2 %collective-permute-done.7.refs_2_.refs_4_ = bf16[1024,128]{1,0:T(8,128)(2,1)S(1)} collective-permute-done((bf16[1024,128]{1,0:T(8,128)(2,1)S(1)}, bf16[1024,128]{1,0:T(8,128)(2,1)S(1)}, u32[]{:S(2)}, u32[]{:S(2)}) %collective-permute-start.7) | collective-permute-done | bytes 262176 | tf_op jit(solution)/shard_map/ppermute | solution.py:358
  44.8 1.2 collective-permute-start.10
  46.0 4.4 %collective-permute-done.refs_2_.refs_4_ = bf16[1024,128]{1,0:T(8,128)(2,1)S(1)} collective-permute-done((bf16[1024,128]{1,0:T(8,128)(2,1)S(1)}, bf16[1024,128]{1,0:T(8,128)(2,1)S(1)}, u32[]{:S(2)}, u32[]{:S(2)}) %collective-permute-start) | collective-permute-done | bytes 262176 | tf_op jit(solution)/shard_map/ppermute | solution.py:358
  50.4 1.2 collective-permute-start.8
  51.6 4.4 %collective-permute-done.2.refs_4_.refs_6_ = bf16[1024,128]{1,0:T(8,128)(2,1)S(1)} collective-permute-done((bf16[1024,128]{1,0:T(8,128)(2,1)S(1)}, bf16[1024,128]{1,0:T(8,128)(2,1)S(1)}, u32[]{:S(2)}, u32[]{:S(2)}) %collective-permute-start.2) | collective-permute-done | bytes 262176 | tf_op jit(solution)/shard_map/ppermute | solution.py:358
  56.0 0.8 collective-permute-start.1
  56.9 0.0 collective-permute-done.11.refs_3_.refs_5_
  56.9 0.1 collective-permute-start.3
  57.0 0.0 collective-permute-done.12.refs_5_.refs_7_
  57.0 0.4 collective-permute-start.19
  57.4 0.3 copy-done.13
  57.7 0.2 copy-done.14
  57.8 22.3 %attend.9 = (f32[3,1024,128]{2,1,0:T(8,128)}, f32[3,1024,128]{2,1,0:T(8,128)}, f32[3,1024,128]{2,1,0:T(8,128)}) custom-call(s32[16]{0:T(128)} %refs_0_.11, bf16[128,1024]{1,0:T(8,128)(2,1)} %collective-permute-done.13.refs_1_, bf16[128,1024]{1,0:T(8,128)(2,1)} %collective-permute-done.14.refs_2_, bf16[128,1024]{1,0:T(8,128)(2,1)} %collective-permute-done.15.refs_3_, ...), custom_call_target="tpu_custom_call" | custom-call | flops 9019430912 | bytes 2097152 | tf_op jit(solution)/shard_map/attend/pallas_call | solution.py:269
  80.2 0.0 collective-permute-done.10.refs_5_.refs_7_
  80.2 0.1 collective-permute-start.20
  80.3 1.6 %collective-permute-start.21 = (bf16[512,256]{1,0:T(8,128)(2,1)S(1)}, bf16[512,256]{1,0:T(8,128)(2,1)S(1)}, u32[]{:S(2)}, u32[]{:S(2)}) collective-permute-start(bf16[512,256]{1,0:T(8,128)(2,1)S(1)} %pad_maximum_fusion.refs_0_), channel_id=1, source_target_pairs={{0,96},{8,104},{16,112},{24,120},{32,0},{40,8},{48,16},{56,24},{64... | collective-permute-start | bytes 786440 | tf_op jit(solution)/shard_map/ppermute | solution.py:362
  82.0 14.6 %attend.10 = (f32[3,1024,128]{2,1,0:T(8,128)}, f32[3,1024,128]{2,1,0:T(8,128)}, f32[3,1024,128]{2,1,0:T(8,128)}) custom-call(s32[16]{0:T(128)} %refs_0_.11, bf16[128,1024]{1,0:T(8,128)(2,1)} %collective-permute-done.13.refs_1_, bf16[128,1024]{1,0:T(8,128)(2,1)} %collective-permute-done.14.refs_2_, bf16[128,1024]{1,0:T(8,128)(2,1)} %collective-permute-done.15.refs_3_, ...), custom_call_target="tpu_custom_call" | custom-call | flops 4509715456 | bytes 1048576 | tf_op jit(solution)/shard_map/attend/pallas_call | solution.py:269
  96.6 0.0 collective-permute-done.3.refs_5_.refs_7_
  96.6 0.7 copy-done.20
  97.3 0.1 copy-done.22
  97.4 15.1 %attend.11 = bf16[3,128,1152]{2,1,0:T(8,128)(2,1)} custom-call(s32[16]{0:T(128)} %refs_0_.11, bf16[128,1024]{1,0:T(8,128)(2,1)} %collective-permute-done.13.refs_1_, bf16[128,1024]{1,0:T(8,128)(2,1)} %collective-permute-done.14.refs_2_, bf16[128,1024]{1,0:T(8,128)(2,1)} %collective-permute-done.15.refs_3_, bf16[1024,128]{1,0:T(8,128)(2,1)} %copy-done.16, ...), custom_call_target="tpu_custom_call" | custom-call | flops 5637144576 | bytes 1310720 | tf_op jit(solution)/shard_map/attend/pallas_call | solution.py:269
  112.5 1.2 fusion
  113.7 0.1 collective-permute-start.16
  113.8 1.5 collective-permute-start.17
  115.3 9.7 %attend.6 = (f32[1,1024,128]{2,1,0:T(8,128)}, f32[1,1024,128]{2,1,0:T(8,128)}, f32[1,1024,128]{2,1,0:T(8,128)}) custom-call(s32[16]{0:T(128)} %refs_0_.11, bf16[128,1024]{1,0:T(8,128)(2,1)} %refs_1_.5, bf16[2048,128]{1,0:T(8,128)(2,1)} %refs_4_.3, bf16[2048,128]{1,0:T(8,128)(2,1)} %copy-done.13, bf16[2048,128]{1,0:T(8,128)(2,1)} %refs_6_.1, ...), custom_call_target="tpu_custom_call" | custom-call | flops 3006477056 | bytes 2097152 | tf_op jit(solution)/shard_map/attend/pallas_call | solution.py:269
  125.0 0.1 collective-permute-start.18
  125.1 7.1 %attend.7 = (f32[1,1024,128]{2,1,0:T(8,128)}, f32[1,1024,128]{2,1,0:T(8,128)}, f32[1,1024,128]{2,1,0:T(8,128)}) custom-call(s32[16]{0:T(128)} %refs_0_.11, bf16[128,1024]{1,0:T(8,128)(2,1)} %refs_1_.5, bf16[1024,128]{1,0:T(8,128)(2,1)} %copy-done.17, bf16[1024,128]{1,0:T(8,128)(2,1)} %copy-done.21, bf16[1024,128]{1,0:T(8,128)(2,1)} %copy-done.15, ...), custom_call_target="tpu_custom_call" | custom-call | flops 1503238528 | bytes 1048576 | tf_op jit(solution)/shard_map/attend/pallas_call | solution.py:269
  132.2 7.3 %attend.8.refs_0_ = bf16[1,128,1152]{2,1,0:T(8,128)(2,1)} custom-call(s32[16]{0:T(128)} %refs_0_.11, bf16[128,1024]{1,0:T(8,128)(2,1)} %refs_1_.5, bf16[1024,128]{1,0:T(8,128)(2,1)} %copy-done.16, bf16[1024,128]{1,0:T(8,128)(2,1)} %copy-done.20, bf16[1024,128]{1,0:T(8,128)(2,1)} %copy-done.18, bf16[1024,128]{1,0:T(8,128)(2,1)} %copy-done.22, ...), custom_call_target="tpu_custom_call" | custom-call | flops 1879048192 | bytes 1310720 | tf_op jit(solution)/shard_map/attend/pallas_call | solution.py:269
  139.5 0.0 collective-permute-done.20.refs_2_
  139.5 0.0 copy-start.7
  139.5 0.0 collective-permute-done.21.refs_3_
  139.5 0.7 copy-done.7
  140.2 0.7 copy-done.8
  140.9 2.9 %pages.1 = bf16[256,256]{1,0:T(8,128)(2,1)} custom-call(s32[64]{0:T(128)} %owner_ref.1, s32[64]{0:T(128)} %slot_ref.1, bf16[512,256]{1,0:T(8,128)(2,1)} %copy-done, bf16[512,256]{1,0:T(8,128)(2,1)} %copy-done.6, bf16[512,256]{1,0:T(8,128)(2,1)} %copy-done.7, bf16[512,256]{1,0:T(8,128)(2,1)} %copy-done.8), custom_call_target="tpu_custom_call" | custom-call | tf_op jit(solution)/shard_map/pages/pallas_call | solution.py:347
  143.8 0.0 collective-permute-done.18.refs_3_
  143.8 0.7 copy-done.3
  144.5 0.1 copy-done.4
  144.6 0.7 copy-done.5
  145.3 2.8 %merge.1 = bf16[128,1024]{1,0:T(8,128)(2,1)} custom-call(bf16[1,128,1152]{2,1,0:T(8,128)(2,1)} %attend.8.refs_0_, bf16[1,128,1152]{2,1,0:T(8,128)(2,1)} %copy-done.3, bf16[1,128,1152]{2,1,0:T(8,128)(2,1)} %copy-done.4, bf16[1,128,1152]{2,1,0:T(8,128)(2,1)} %copy-done.5), custom_call_target="tpu_custom_call" | custom-call | tf_op jit(solution)/shard_map/merge/pallas_call | solution.py:311
  (42 shorter events, 0.2 us)
Async XLA Ops:
  0.6 20.6 %copy-start.2 = (bf16[2048,128]{1,0:T(8,128)(2,1)S(1)}, bf16[2048,128]{1,0:T(8,128)(2,1)}, u32[]{:S(2)}) copy-start(bf16[2048,128]{1,0:T(8,128)(2,1)} %refs_6_.1) | copy-start | bytes 1572868
  0.6 23.5 %collective-permute-start.13 = (bf16[128,1024]{1,0:T(8,128)(2,1)}, bf16[128,1024]{1,0:T(8,128)(2,1)}, u32[]{:S(2)}, u32[]{:S(2)}) collective-permute-start(bf16[128,1024]{1,0:T(8,128)(2,1)} %refs_1_.5), channel_id=1, source_target_pairs={{0,32},{8,40},{16,48},{24,56},{32,64},{40,72},{48,80},{56,88},{64,... | collective-permute-start | bytes 786440 | tf_op jit(solution)/shard_map/ppermute | solution.py:362
  2.8 27.1 %collective-permute-start.14 = (bf16[128,1024]{1,0:T(8,128)(2,1)}, bf16[128,1024]{1,0:T(8,128)(2,1)}, u32[]{:S(2)}, u32[]{:S(2)}) collective-permute-start(bf16[128,1024]{1,0:T(8,128)(2,1)} %refs_1_.5), channel_id=1, source_target_pairs={{0,96},{8,104},{16,112},{24,120},{32,0},{40,8},{48,16},{56,24},{64... | collective-permute-start | bytes 786440 | tf_op jit(solution)/shard_map/ppermute | solution.py:362
  4.4 29.7 %collective-permute-start.15 = (bf16[128,1024]{1,0:T(8,128)(2,1)}, bf16[128,1024]{1,0:T(8,128)(2,1)}, u32[]{:S(2)}, u32[]{:S(2)}) collective-permute-start(bf16[128,1024]{1,0:T(8,128)(2,1)} %refs_1_.5), channel_id=1, source_target_pairs={{0,64},{8,72},{16,80},{24,88},{32,96},{40,104},{48,112},{56,120},{... | collective-permute-start | bytes 786440 | tf_op jit(solution)/shard_map/ppermute | solution.py:362
  13.7 8.3 %copy-start.1 = (bf16[2048,128]{1,0:T(8,128)(2,1)S(1)}, bf16[2048,128]{1,0:T(8,128)(2,1)}, u32[]{:S(2)}) copy-start(bf16[2048,128]{1,0:T(8,128)(2,1)} %refs_4_.3) | copy-start | bytes 1572868
  13.7 16.1 %all-to-all-start = ((bf16[8,128,256]{2,1,0:T(8,128)(2,1)}), bf16[8,128,256]{2,1,0:T(8,128)(2,1)S(1)}, u32[]{:S(2)}, u32[]{:S(2)}) async-start(bf16[8,128,256]{2,1,0:T(8,128)(2,1)} %project.1), calls=%async_computation | async-start | bytes 1048576 | tf_op jit(solution)/shard_map/all_to_all | solution.py:378
  21.3 13.6 %collective-permute-start.9 = (bf16[1024,128]{1,0:T(8,128)(2,1)S(1)}, bf16[1024,128]{1,0:T(8,128)(2,1)S(1)}, u32[]{:S(2)}, u32[]{:S(2)}) collective-permute-start(bf16[1024,128]{1,0:T(8,128)(2,1)S(1)} %get-tuple-element.29), channel_id=1, source_target_pairs={{0,16},{8,24},{16,0},{24,8},{32,48},{40,56},{48,32},{56,40},{64,80... | collective-permute-start | bytes 786440 | tf_op jit(solution)/shard_map/ppermute | solution.py:358
  22.1 34.8 %collective-permute-start.11 = (bf16[2048,128]{1,0:T(8,128)(2,1)S(1)}, bf16[2048,128]{1,0:T(8,128)(2,1)S(1)}, u32[]{:S(2)}, u32[]{:S(2)}) collective-permute-start(bf16[2048,128]{1,0:T(8,128)(2,1)S(1)} %copy-done.1), channel_id=1, source_target_pairs={{0,8},{8,0},{16,24},{24,16},{32,40},{40,32},{48,56},{56,48},{64,72... | collective-permute-start | bytes 1572872 | tf_op jit(solution)/shard_map/ppermute | solution.py:358
  24.2 32.8 %collective-permute-start.12 = (bf16[2048,128]{1,0:T(8,128)(2,1)S(1)}, bf16[2048,128]{1,0:T(8,128)(2,1)S(1)}, u32[]{:S(2)}, u32[]{:S(2)}) collective-permute-start(bf16[2048,128]{1,0:T(8,128)(2,1)S(1)} %copy-done.2), channel_id=1, source_target_pairs={{0,8},{8,0},{16,24},{24,16},{32,40},{40,32},{48,56},{56,48},{64,72... | collective-permute-start | bytes 1572872 | tf_op jit(solution)/shard_map/ppermute | solution.py:358
  29.9 50.2 %copy-start.9 = (bf16[128,256]{1,0:T(8,128)(2,1)}, bf16[128,256]{1,0:T(8,128)(2,1)S(1)}, u32[]{:S(2)}) copy-start(bf16[128,256]{1,0:T(8,128)(2,1)S(1)} %reduce_sum.12.refs_6_.refs_8_) | copy-start | bytes 196612
  29.9 5.9 %collective-permute-start.4 = (bf16[128,256]{1,0:T(8,128)(2,1)S(1)}, bf16[128,256]{1,0:T(8,128)(2,1)S(1)}, u32[]{:S(2)}, u32[]{:S(2)}) collective-permute-start(bf16[128,256]{1,0:T(8,128)(2,1)S(1)} %reduce_sum.12.refs_6_.refs_8_), channel_id=1, source_target_pairs={{0,8},{8,0},{16,24},{24,16},{32,40},{40,32},{48,56},{56,48},{64,72... | collective-permute-start | bytes 196616 | tf_op jit(solution)/shard_map/ppermute | solution.py:358
  34.1 3.7 %collective-permute-start.5 = (bf16[128,256]{1,0:T(8,128)(2,1)S(1)}, bf16[128,256]{1,0:T(8,128)(2,1)S(1)}, u32[]{:S(2)}, u32[]{:S(2)}) collective-permute-start(bf16[128,256]{1,0:T(8,128)(2,1)S(1)} %reduce_sum.12.refs_6_.refs_8_), channel_id=1, source_target_pairs={{0,16},{8,24},{16,0},{24,8},{32,48},{40,56},{48,32},{56,40},{64,80... | collective-permute-start | bytes 196616 | tf_op jit(solution)/shard_map/ppermute | solution.py:358
  34.9 45.2 %copy-start.15 = (bf16[1024,128]{1,0:T(8,128)(2,1)}, bf16[1024,128]{1,0:T(8,128)(2,1)S(1)}, u32[]{:S(2)}) copy-start(bf16[1024,128]{1,0:T(8,128)(2,1)S(1)} %collective-permute-done.9.refs_4_.refs_6_) | copy-start | bytes 786436
  34.9 4.8 %collective-permute-start.6 = (bf16[128,256]{1,0:T(8,128)(2,1)S(1)}, bf16[128,256]{1,0:T(8,128)(2,1)S(1)}, u32[]{:S(2)}, u32[]{:S(2)}) collective-permute-start(bf16[128,256]{1,0:T(8,128)(2,1)S(1)} %reduce_sum.12.refs_6_.refs_8_), channel_id=1, source_target_pairs={{0,24},{8,16},{16,8},{24,0},{32,56},{40,48},{48,40},{56,32},{64,88... | collective-permute-start | bytes 196616 | tf_op jit(solution)/shard_map/ppermute | solution.py:358
  35.9 44.3 %copy-start.10 = (bf16[128,256]{1,0:T(8,128)(2,1)}, bf16[128,256]{1,0:T(8,128)(2,1)S(1)}, u32[]{:S(2)}) copy-start(bf16[128,256]{1,0:T(8,128)(2,1)S(1)} %collective-permute-done.4.refs_7_.refs_9_) | copy-start | bytes 196612
  35.9 8.9 %collective-permute-start.7 = (bf16[1024,128]{1,0:T(8,128)(2,1)S(1)}, bf16[1024,128]{1,0:T(8,128)(2,1)S(1)}, u32[]{:S(2)}, u32[]{:S(2)}) collective-permute-start(bf16[1024,128]{1,0:T(8,128)(2,1)S(1)} %get-tuple-element.31), channel_id=1, source_target_pairs={{0,16},{8,24},{16,0},{24,8},{32,48},{40,56},{48,32},{56,40},{64,80... | collective-permute-start | bytes 786440 | tf_op jit(solution)/shard_map/ppermute | solution.py:358
  37.7 42.4 %copy-start.11 = (bf16[128,256]{1,0:T(8,128)(2,1)}, bf16[128,256]{1,0:T(8,128)(2,1)S(1)}, u32[]{:S(2)}) copy-start(bf16[128,256]{1,0:T(8,128)(2,1)S(1)} %collective-permute-done.5.refs_8_.refs_10_) | copy-start | bytes 196612
  37.7 12.7 %collective-permute-start = (bf16[1024,128]{1,0:T(8,128)(2,1)S(1)}, bf16[1024,128]{1,0:T(8,128)(2,1)S(1)}, u32[]{:S(2)}, u32[]{:S(2)}) collective-permute-start(bf16[1024,128]{1,0:T(8,128)(2,1)S(1)} %get-tuple-element.32), channel_id=1, source_target_pairs={{0,16},{8,24},{16,0},{24,8},{32,48},{40,56},{48,32},{56,40},{64,80... | collective-permute-start | bytes 786440 | tf_op jit(solution)/shard_map/ppermute | solution.py:358
  39.7 40.4 %copy-start.12 = (bf16[128,256]{1,0:T(8,128)(2,1)}, bf16[128,256]{1,0:T(8,128)(2,1)S(1)}, u32[]{:S(2)}) copy-start(bf16[128,256]{1,0:T(8,128)(2,1)S(1)} %collective-permute-done.6.refs_9_.refs_11_) | copy-start | bytes 196612
  39.7 16.3 %collective-permute-start.2 = (bf16[1024,128]{1,0:T(8,128)(2,1)S(1)}, bf16[1024,128]{1,0:T(8,128)(2,1)S(1)}, u32[]{:S(2)}, u32[]{:S(2)}) collective-permute-start(bf16[1024,128]{1,0:T(8,128)(2,1)S(1)} %get-tuple-element.30), channel_id=1, source_target_pairs={{0,16},{8,24},{16,0},{24,8},{32,48},{40,56},{48,32},{56,40},{64,80... | collective-permute-start | bytes 786440 | tf_op jit(solution)/shard_map/ppermute | solution.py:358
  40.6 39.7 %copy-start = (bf16[512,256]{1,0:T(8,128)(2,1)}, bf16[512,256]{1,0:T(8,128)(2,1)S(1)}, u32[]{:S(2)}) copy-start(bf16[512,256]{1,0:T(8,128)(2,1)S(1)} %pad_maximum_fusion.refs_0_) | copy-start | bytes 786436
  44.8 35.4 %copy-start.17 = (bf16[1024,128]{1,0:T(8,128)(2,1)}, bf16[1024,128]{1,0:T(8,128)(2,1)S(1)}, u32[]{:S(2)}) copy-start(bf16[1024,128]{1,0:T(8,128)(2,1)S(1)} %collective-permute-done.7.refs_2_.refs_4_) | copy-start | bytes 786436
  44.8 35.4 %collective-permute-start.10 = (bf16[1024,128]{1,0:T(8,128)(2,1)S(1)}, bf16[1024,128]{1,0:T(8,128)(2,1)S(1)}, u32[]{:S(2)}, u32[]{:S(2)}) collective-permute-start(bf16[1024,128]{1,0:T(8,128)(2,1)S(1)} %collective-permute-done.9.refs_4_.refs_6_), channel_id=1, source_target_pairs={{0,8},{8,0},{16,24},{24,16},{32,40},{40,32},{48,56},{56,48},{64,72... | collective-permute-start | bytes 786440 | tf_op jit(solution)/shard_map/ppermute | solution.py:358
  50.4 29.7 %copy-start.16 = (bf16[1024,128]{1,0:T(8,128)(2,1)}, bf16[1024,128]{1,0:T(8,128)(2,1)S(1)}, u32[]{:S(2)}) copy-start(bf16[1024,128]{1,0:T(8,128)(2,1)S(1)} %collective-permute-done.refs_2_.refs_4_) | copy-start | bytes 786436
  50.4 29.9 %collective-permute-start.8 = (bf16[1024,128]{1,0:T(8,128)(2,1)S(1)}, bf16[1024,128]{1,0:T(8,128)(2,1)S(1)}, u32[]{:S(2)}, u32[]{:S(2)}) collective-permute-start(bf16[1024,128]{1,0:T(8,128)(2,1)S(1)} %collective-permute-done.7.refs_2_.refs_4_), channel_id=1, source_target_pairs={{0,8},{8,0},{16,24},{24,16},{32,40},{40,32},{48,56},{56,48},{64,72... | collective-permute-start | bytes 786440 | tf_op jit(solution)/shard_map/ppermute | solution.py:358
  56.0 24.1 %copy-start.18 = (bf16[1024,128]{1,0:T(8,128)(2,1)}, bf16[1024,128]{1,0:T(8,128)(2,1)S(1)}, u32[]{:S(2)}) copy-start(bf16[1024,128]{1,0:T(8,128)(2,1)S(1)} %collective-permute-done.2.refs_4_.refs_6_) | copy-start | bytes 786436
  56.0 40.5 %collective-permute-start.1 = (bf16[1024,128]{1,0:T(8,128)(2,1)S(1)}, bf16[1024,128]{1,0:T(8,128)(2,1)S(1)}, u32[]{:S(2)}, u32[]{:S(2)}) collective-permute-start(bf16[1024,128]{1,0:T(8,128)(2,1)S(1)} %collective-permute-done.refs_2_.refs_4_), channel_id=1, source_target_pairs={{0,8},{8,0},{16,24},{24,16},{32,40},{40,32},{48,56},{56,48},{64,72... | collective-permute-start | bytes 786440 | tf_op jit(solution)/shard_map/ppermute | solution.py:358
  56.9 0.8 copy-start.13
  56.9 39.7 %collective-permute-start.3 = (bf16[1024,128]{1,0:T(8,128)(2,1)S(1)}, bf16[1024,128]{1,0:T(8,128)(2,1)S(1)}, u32[]{:S(2)}, u32[]{:S(2)}) collective-permute-start(bf16[1024,128]{1,0:T(8,128)(2,1)S(1)} %collective-permute-done.2.refs_4_.refs_6_), channel_id=1, source_target_pairs={{0,8},{8,0},{16,24},{24,16},{32,40},{40,32},{48,56},{56,48},{64,72... | collective-permute-start | bytes 786440 | tf_op jit(solution)/shard_map/ppermute | solution.py:358
  57.0 0.9 copy-start.14
  57.0 68.0 %collective-permute-start.19 = (bf16[512,256]{1,0:T(8,128)(2,1)S(1)}, bf16[512,256]{1,0:T(8,128)(2,1)S(1)}, u32[]{:S(2)}, u32[]{:S(2)}) collective-permute-start(bf16[512,256]{1,0:T(8,128)(2,1)S(1)} %pad_maximum_fusion.refs_0_), channel_id=1, source_target_pairs={{0,32},{8,40},{16,48},{24,56},{32,64},{40,72},{48,80},{56,88},{64,... | collective-permute-start | bytes 786440 | tf_op jit(solution)/shard_map/ppermute | solution.py:362
  80.2 1.8 %copy-start.19 = (bf16[1024,128]{1,0:T(8,128)(2,1)}, bf16[1024,128]{1,0:T(8,128)(2,1)S(1)}, u32[]{:S(2)}) copy-start(bf16[1024,128]{1,0:T(8,128)(2,1)S(1)} %collective-permute-done.10.refs_5_.refs_7_) | copy-start | bytes 786436
  80.2 59.3 %collective-permute-start.20 = (bf16[512,256]{1,0:T(8,128)(2,1)S(1)}, bf16[512,256]{1,0:T(8,128)(2,1)S(1)}, u32[]{:S(2)}, u32[]{:S(2)}) collective-permute-start(bf16[512,256]{1,0:T(8,128)(2,1)S(1)} %pad_maximum_fusion.refs_0_), channel_id=1, source_target_pairs={{0,64},{8,72},{16,80},{24,88},{32,96},{40,104},{48,112},{56,120},{... | collective-permute-start | bytes 786440 | tf_op jit(solution)/shard_map/ppermute | solution.py:362
  80.3 1.6 %copy-start.21 = (bf16[1024,128]{1,0:T(8,128)(2,1)}, bf16[1024,128]{1,0:T(8,128)(2,1)S(1)}, u32[]{:S(2)}) copy-start(bf16[1024,128]{1,0:T(8,128)(2,1)S(1)} %collective-permute-done.8.refs_3_.refs_5_) | copy-start | bytes 786436
  80.3 59.2 %collective-permute-start.21 = (bf16[512,256]{1,0:T(8,128)(2,1)S(1)}, bf16[512,256]{1,0:T(8,128)(2,1)S(1)}, u32[]{:S(2)}, u32[]{:S(2)}) collective-permute-start(bf16[512,256]{1,0:T(8,128)(2,1)S(1)} %pad_maximum_fusion.refs_0_), channel_id=1, source_target_pairs={{0,96},{8,104},{16,112},{24,120},{32,0},{40,8},{48,16},{56,24},{64... | collective-permute-start | bytes 786440 | tf_op jit(solution)/shard_map/ppermute | solution.py:362
  96.6 0.7 copy-start.20
  96.6 0.8 copy-start.22
  113.7 30.0 %collective-permute-start.16 = (bf16[1,128,1152]{2,1,0:T(8,128)(2,1)S(1)}, bf16[1,128,1152]{2,1,0:T(8,128)(2,1)S(1)}, u32[]{:S(2)}, u32[]{:S(2)}) collective-permute-start(bf16[1,128,1152]{2,1,0:T(8,128)(2,1)S(1)} %get-tuple-element.28), channel_id=1, source_target_pairs={{0,96},{8,104},{16,112},{24,120},{32,0},{40,8},{48,16},{56,24},{64... | collective-permute-start | bytes 884744 | tf_op jit(solution)/shard_map/ppermute | solution.py:362
  113.8 30.0 %collective-permute-start.17 = (bf16[1,128,1152]{2,1,0:T(8,128)(2,1)S(1)}, bf16[1,128,1152]{2,1,0:T(8,128)(2,1)S(1)}, u32[]{:S(2)}, u32[]{:S(2)}) collective-permute-start(bf16[1,128,1152]{2,1,0:T(8,128)(2,1)S(1)} %get-tuple-element.27), channel_id=1, source_target_pairs={{0,32},{8,40},{16,48},{24,56},{32,64},{40,72},{48,80},{56,88},{64,... | collective-permute-start | bytes 884744 | tf_op jit(solution)/shard_map/ppermute | solution.py:362
  125.0 7.2 %copy-start.6 = (bf16[512,256]{1,0:T(8,128)(2,1)}, bf16[512,256]{1,0:T(8,128)(2,1)S(1)}, u32[]{:S(2)}) copy-start(bf16[512,256]{1,0:T(8,128)(2,1)S(1)} %collective-permute-done.19.refs_1_) | copy-start | bytes 786436
  125.0 18.8 %collective-permute-start.18 = (bf16[1,128,1152]{2,1,0:T(8,128)(2,1)S(1)}, bf16[1,128,1152]{2,1,0:T(8,128)(2,1)S(1)}, u32[]{:S(2)}, u32[]{:S(2)}) collective-permute-start(bf16[1,128,1152]{2,1,0:T(8,128)(2,1)S(1)} %get-tuple-element.26), channel_id=1, source_target_pairs={{0,64},{8,72},{16,80},{24,88},{32,96},{40,104},{48,112},{56,120},{... | collective-permute-start | bytes 884744 | tf_op jit(solution)/shard_map/ppermute | solution.py:362
  139.5 0.7 copy-start.7
  140.2 0.7 copy-start.8
  143.8 0.7 copy-start.3
  143.8 0.8 copy-start.4
  144.6 0.7 copy-start.5

commit v2 on v1

v2 whole, which is shorter than its diff:
```python
import functools

import jax
import jax.numpy as jnp
from jax import lax
from jax.experimental import pallas as pl
from jax.experimental.pallas import tpu as pltpu
from jax.sharding import PartitionSpec as P

PAGE = 32
HD = 128
LOG2E = 1.4426950408889634
SCALE = LOG2E / HD**0.5
BIG = 2.0**100
F32 = jnp.float32
BF16 = jnp.bfloat16
VMEM_LIMIT = 56 * 2**20
SMALL = pl.CostEstimate(flops=1000, bytes_accessed=1000, transcendentals=0)


def nt_dot(a, b):
    return lax.dot_general(a, b, (((1,), (1,)), ((), ())), preferred_element_type=F32)


def nn_dot(a, b):
    return lax.dot_general(a, b, (((1,), (0,)), ((), ())), preferred_element_type=F32)


def vmem_spec():
    return pl.BlockSpec(memory_space=pltpu.VMEM)


def smem_spec():
    return pl.BlockSpec(memory_space=pltpu.SMEM)


def project_kernel(tok_ref, w_ref, out_ref):
    out_ref[0] = nn_dot(tok_ref[...], w_ref[...]).astype(BF16)


def project(tokens, kv_weight):
    rows, depth = tokens.shape
    heads = kv_weight.shape[1] // (2 * HD)
    return pl.pallas_call(
        project_kernel,
        grid=(heads,),
        in_specs=[
            pl.BlockSpec((rows, depth), lambda h: (0, 0)),
            pl.BlockSpec((depth, 2 * HD), lambda h: (0, h)),
        ],
        out_specs=pl.BlockSpec((1, rows, 2 * HD), lambda h: (h, 0, 0)),
        out_shape=jax.ShapeDtypeStruct((heads, rows, 2 * HD), BF16),
        compiler_params=pltpu.CompilerParams(vmem_limit_bytes=VMEM_LIMIT),
        cost_estimate=SMALL,
        name="project",
    )(tokens, kv_weight)


def attend_kernel(cfg, *refs):
    nq, nseg, seg, owner_xor, state_in, fresh = cfg
    refs = list(refs)
    take = lambda n: [refs.pop(0) for _ in range(n)]
    (len_ref,) = take(1)
    q_refs = take(nq)
    kv_refs = take(nseg)
    f_refs = take(1) if fresh else []
    st_refs = take(nq) if state_in else []
    out, qb, kb, acc, ll, mm, st, sems = refs
    me = lax.axis_index("ctx")
    step = pl.program_id(0)
    rows = qb.shape[0]
    groups = rows // 128
    nsegs = nseg + len(f_refs)

    copies = [
        pltpu.make_async_copy(r, kb.at[pl.ds(s * seg, seg)], sems.at[s])
        for s, r in enumerate(kv_refs + f_refs)
    ]

    @pl.when(step == 0)
    def _():
        for c in copies:
            c.start()

    for i in range(nq):

        @pl.when(step == i)
        def _():
            for g in range(groups):
                qb[g * 128 : (g + 1) * 128, :] = q_refs[i][:, g * 128 : (g + 1) * 128]
            if state_in:
                st[...] = st_refs[i][0]

    @pl.when(step == 0)
    def _():
        copies[0].wait()

    if state_in:
        side_in = st[:, groups * 128 :].astype(F32)
        for g in range(groups):
            mm[g * 128 : (g + 1) * 128, :] = jnp.broadcast_to(side_in[:, g : g + 1], (128, 128))
    else:
        top = jnp.max(nt_dot(qb[...], kb[:256, :HD]), axis=-1, keepdims=True) * SCALE
        mm[...] = jnp.broadcast_to(top.astype(BF16).astype(F32), mm.shape)

    def masked(vals, size, limit, slope, fill):
        col = lax.broadcasted_iota(jnp.int32, (rows, size), 1)
        row = lax.rem(lax.broadcasted_iota(jnp.int32, (rows, size), 0), 128)
        return jnp.where(col <= limit + row * slope, vals, fill)

    def accumulate(at, size, limit=None, slope=None):
        at = pl.ds(pl.multiple_of(at, 128), size)
        s = nt_dot(qb[...], kb[at, :HD])
        tops = jnp.concatenate([mm[...]] * (size // 128), axis=1)
        p = jnp.exp2(s * SCALE - tops)
        if limit is not None:
            p = masked(p, size, limit, slope, 0.0)
        acc[...] += nn_dot(p.astype(BF16), kb[at, HD:])
        total = ll[...]
        for g in range(size // 128):
            total = total + p[:, g * 128 : (g + 1) * 128]
        ll[...] = total

    def segment(s):
        owner = me ^ owner_xor[0]
        for i in range(1, nseg):
            owner = jnp.where(s == i, me ^ owner_xor[i], owner)
        length = jnp.clip(len_ref[owner], 0, seg)
        whole = length // 512 * 512
        rest = length - whole
        limit = rest - 1
        slope = 0
        if fresh:
            is_fresh = s == nseg
            before = me * 128
            whole = jnp.where(is_fresh, before // 512 * 512, whole)
            rest = jnp.where(is_fresh, before - whole + 128, rest)
            limit = jnp.where(is_fresh, before - whole, limit)
            slope = jnp.where(is_fresh, 1, 0)
        return s * seg, whole, rest, limit, slope

    def sweep(turn):
        acc[...] = jnp.zeros_like(acc)
        ll[...] = jnp.zeros_like(ll)

        def one(s, carry):
            start, whole, rest, limit, slope = segment(s)

            for i in range(1, nsegs):

                @pl.when((s == i) & (step == 0) & (turn == 0))
                def _():
                    copies[i].wait()

            wide = whole // 1024

            def wide_step(j, c):
                accumulate(start + j * 1024, 1024)
                return c

            lax.fori_loop(0, wide, wide_step, 0)

            @pl.when(whole > wide * 1024)
            def _():
                accumulate(start + wide * 1024, 512)

            @pl.when(rest > 256)
            def _():
                accumulate(start + whole, 512, limit, slope)

            @pl.when((rest > 0) & (rest <= 256))
            def _():
                accumulate(start + whole, 256, limit, slope)

            return carry

        lax.fori_loop(0, nsegs, one, 0)

    def raise_tops():
        def one(s, carry):
            start, whole, rest, limit, slope = segment(s)

            def part(j, c):
                at = pl.ds(pl.multiple_of(start + j * 128, 128), 128)
                s_now = nt_dot(qb[...], kb[at, :HD]) * SCALE
                edge = jnp.where(j * 128 < whole, 128, limit - (j * 128 - whole))
                tilt = jnp.where(j * 128 < whole, 0, slope)
                s_now = masked(s_now, 128, edge, tilt, -3.0e38)
                top = jnp.max(s_now, axis=-1, keepdims=True)
                mm[...] = jnp.maximum(mm[...], top.astype(BF16).astype(F32))
                return c

            return lax.fori_loop(0, (whole + rest + 127) // 128, part, carry)

        lax.fori_loop(0, nsegs, one, 0)

    def attempt(turn):
        @pl.when(turn == 1)
        def _():
            raise_tops()

        sweep(turn)
        fits = jnp.max(ll[...]) < BIG
        return jnp.where((turn == 0) & jnp.logical_not(fits), 1, 2)

    lax.while_loop(lambda turn: turn < 2, attempt, 0)

    lane = lax.broadcasted_iota(jnp.int32, (128, 128), 1)
    side = jnp.zeros((128, 128), F32)
    for g in range(groups):
        part = slice(g * 128, (g + 1) * 128)
        mixed = acc[part, :]
        total = jnp.sum(ll[part, :], axis=-1, keepdims=True)
        top = mm[part, :]
        if state_in:
            decay = jnp.exp2(side_in[:, g : g + 1] - top)
            mixed = mixed + st[:, part].astype(F32) * decay
            total = total + (side_in[:, 8 + g : 9 + g] + side_in[:, 16 + g : 17 + g]) * decay
        out[0, :, part] = mixed.astype(BF16)
        high = total.astype(BF16).astype(F32)
        side = jnp.where(lane == g, top, side)
        side = jnp.where(lane == 8 + g, high, side)
        side = jnp.where(lane == 16 + g, total - high, side)
    out[0, :, groups * 128 :] = side.astype(BF16)


def attend(lengths, qs, kvs, owner_xor, state=None, fresh=None, flops=1000):
    nq, nseg, seg = len(qs), len(kvs), kvs[0].shape[0]
    width = qs[0].shape[1]
    rows = width
    cfg = (nq, nseg, seg, owner_xor, state is not None, fresh is not None)
    packed = pl.BlockSpec((1, 128, width + 128), lambda i: (i, 0, 0))
    any_spec = pl.BlockSpec(memory_space=pl.ANY)
    args = [lengths, *qs, *kvs]
    in_specs = [smem_spec()] + [vmem_spec()] * nq + [any_spec] * nseg
    if fresh is not None:
        args.append(fresh)
        in_specs.append(any_spec)
    if state is not None:
        args += [array for array, _ in state]
        in_specs += [
            pl.BlockSpec((1, 128, width + 128), functools.partial(lambda at, i: (at, 0, 0), at))
            for _, at in state
        ]
    nsegs = nseg + (fresh is not None)
    return pl.pallas_call(
        functools.partial(attend_kernel, cfg),
        grid=(nq,),
        in_specs=in_specs,
        out_specs=packed,
        out_shape=jax.ShapeDtypeStruct((nq, 128, width + 128), BF16),
        scratch_shapes=[
            pltpu.VMEM((rows, HD), BF16),
            pltpu.VMEM((nsegs * seg, 2 * HD), BF16),
            pltpu.VMEM((rows, HD), F32),
            pltpu.VMEM((rows, HD), F32),
            pltpu.VMEM((rows, HD), F32),
            pltpu.VMEM((128, width + 128), BF16),
            pltpu.SemaphoreType.DMA((nsegs,)),
        ],
        compiler_params=pltpu.CompilerParams(vmem_limit_bytes=VMEM_LIMIT),
        cost_estimate=pl.CostEstimate(flops=flops, bytes_accessed=1000, transcendentals=0),
        name="attend",
    )(*args)


def merge_kernel(*refs):
    parts, out = refs[:-1], refs[-1]
    groups = out.shape[1] // 128
    sides = [r[0, :, groups * 128 :].astype(F32) for r in parts]
    top = functools.reduce(jnp.maximum, sides)
    scales = [jnp.exp2(s - top) for s in sides]
    total = jnp.zeros_like(top)
    for w, s in zip(scales, sides):
        total = total + w * (pltpu.roll(s, 120, 1) + pltpu.roll(s, 112, 1))
    scales = [w / total for w in scales]
    for g in range(groups):
        part = slice(g * 128, (g + 1) * 128)
        mixed = sum(w[:, g : g + 1] * r[0, :, part].astype(F32) for w, r in zip(scales, parts))
        out[:, part] = mixed.astype(BF16)


def merge(parts):
    rows, width = parts[0][1].shape[1:]
    return pl.pallas_call(
        merge_kernel,
        grid=(1,),
        in_specs=[
            pl.BlockSpec((1, rows, width), functools.partial(lambda at, i: (at, 0, 0), at))
            for at, _ in parts
        ],
        out_specs=pl.BlockSpec((rows, width - 128), lambda i: (0, 0)),
        out_shape=jax.ShapeDtypeStruct((rows, width - 128), BF16),
        compiler_params=pltpu.CompilerParams(vmem_limit_bytes=VMEM_LIMIT),
        cost_estimate=SMALL,
        name="merge",
    )(*[p for _, p in parts])


def pages_kernel(owner_ref, slot_ref, fresh_ref, out):
    me = lax.axis_index("ctx")
    out[...] = jnp.zeros_like(out)

    def one(page, carry):
        @pl.when(owner_ref[page] == me)
        def _():
            src = pl.ds(pl.multiple_of(page * PAGE, PAGE), PAGE)
            dst = pl.ds(pl.multiple_of(slot_ref[page] * PAGE, PAGE), PAGE)
            out[dst, :] = fresh_ref[src, :]

        return carry

    lax.fori_loop(0, owner_ref.shape[0], one, 0)


def pick_pages(page_owner, page_slot, fresh):
    return pl.pallas_call(
        pages_kernel,
        in_specs=[smem_spec()] * 2 + [vmem_spec()],
        out_specs=vmem_spec(),
        out_shape=jax.ShapeDtypeStruct((8 * PAGE, 2 * HD), BF16),
        compiler_params=pltpu.CompilerParams(vmem_limit_bytes=VMEM_LIMIT),
        cost_estimate=SMALL,
        name="pages",
    )(page_owner, page_slot, fresh)


def flip(x, bits):
    return lax.ppermute(x, "ctx", [(i, i ^ bits) for i in range(16)])


def turn(x, k):
    return lax.ppermute(x, "ctx", [(i, (i + 4 * k) % 16) for i in range(16)])


def body(
    tokens, kv_weight, queries, cache_keys, cache_values, cache_lengths, page_owner, page_slot
):
    order = (1, 3, 2)
    others = [turn(queries, k) for k in order]
    own_kv = jnp.concatenate([cache_keys, cache_values], axis=1)
    far_kv = flip(own_kv, 2)
    core_kv = flip(own_kv, 1)

    partial = project(tokens, kv_weight)
    gathered = lax.all_to_all(partial, "tp", 0, 0, tiled=True)

    near, far = (0, 1), (2, 3)
    lengths, _ = lax.optimization_barrier((cache_lengths, partial))
    near0 = attend(lengths, [queries], (own_kv, core_kv), near)
    lengths, gathered, _ = lax.optimization_barrier((lengths, gathered, near0))
    fresh = jnp.sum(gathered.astype(F32), axis=0).astype(BF16)
    spread = jnp.broadcast_to(fresh[None], (16, *fresh.shape))
    fresh = lax.all_to_all(spread, "ctx", 0, 0, tiled=True).reshape(16 * 128, 2 * HD)
    kv_pages = pick_pages(page_owner, page_slot, fresh)
    near1 = attend(lengths, others[:2], (own_kv, core_kv), near)
    lengths, far_kv, _ = lax.optimization_barrier((lengths, far_kv, near1))
    both_kv = flip(far_kv, 1)
    near2 = attend(lengths, others[2:], (own_kv, core_kv), near, flops=2 * 10**10)
    sent = attend(
        lengths, others, (far_kv, both_kv), far, state=[(near1, 0), (near1, 1), (near2, 0)]
    )
    back = [turn(sent[i : i + 1], 4 - k) for i, k in enumerate(order)]
    lengths, _ = lax.optimization_barrier((lengths, sent))
    mine = attend(
        lengths, [queries], (far_kv, both_kv), far, state=[(near0, 0)], fresh=fresh
    )
    attended = merge([(0, mine), *[(0, b) for b in back]])
    return (attended, kv_pages)


def solution(mesh):
    placed = (
        P("ctx", "tp"),
        P("tp", None),
        P("ctx", "tp"),
        P("ctx", "tp"),
        P("ctx", "tp"),
        P(),
        P(),
        P(),
    )
    return jax.shard_map(
        body,
        mesh=mesh,
        in_specs=placed,
        out_specs=(P("ctx", "tp"), P("ctx", "tp")),
        check_vma=False,
    )
```

time: 150 us -> 120 us (0.80)
  Pallas kernels: 89.6 us -> 61.3 us
  waiting for transfers between devices: 20.8 us -> 7.74 us
  starting transfers between devices: 31.2 us -> 37.9 us
  local copies, waits for them, and re-layouts: 5.48 us -> 10.4 us
    pallas_call x6 -> x5, Pallas kernels: 76.1 us -> 47.9 us  [attend(): pl.pallas_call(functools.partial(attend_kernel, cfg), grid=(nq,), in_spec...]
    ppermute x13 -> x3, waiting for transfers between devices: 15.1 us -> 0.01 us  [flip(): return lax.ppermute(x, 'ctx', [(i, i ^ bits) for i in range(16)])]
    ppermute x13 -> x3, starting transfers between devices: 14.7 us -> 4.18 us  [flip(): return lax.ppermute(x, 'ctx', [(i, i ^ bits) for i in range(16)])]
    ppermute x9 -> x6, starting transfers between devices: 9.01 us -> 18.3 us  [turn(): return lax.ppermute(x, 'ctx', [(i, (i + 4 * k) % 16) for i in range(16)])]
    all_to_all x0 -> x1, starting transfers between devices: none -> 8.38 us  [body(): lax.all_to_all(spread, 'ctx', 0, 0, tiled=True).reshape(16 * 128, 2 * HD)]
    ppermute x9 -> x6, waiting for transfers between devices: 0.02 us -> 2.95 us  [turn(): return lax.ppermute(x, 'ctx', [(i, (i + 4 * k) % 16) for i in range(16)])]
    unnamed x46 -> x21, local copies, waits for them, and re-layouts: 4.2 us -> 6.94 us
  transfers between devices with their start and end apart: 23 -> 11, of which waited for: 6 -> 2; matrix products, arithmetic and copies ran while one was open for 1% -> 2% of each run, Pallas kernels for 59% -> 50%
where the time goes in v2:
time: 120 us; the launch traced here: 118 us
  Pallas kernels  61.3 us (51%)
  starting transfers between devices  37.9 us (32%)
  local copies, waits for them, and re-layouts  10.4 us (9%)
  waiting for transfers between devices  7.74 us (6%)
    pallas_call x5, Pallas kernels, attend(): pl.pallas_call(functools.partial(attend_kernel, cfg), grid=(nq,), in_spec...  47.9 us
    ppermute x6, starting transfers between devices, turn(): return lax.ppermute(x, 'ctx', [(i, (i + 4 * k) % 16) for i in range(16)])  18.3 us
    all_to_all x1, starting transfers between devices, body(): lax.all_to_all(spread, 'ctx', 0, 0, tiled=True).reshape(16 * 128, 2 * HD)  8.38 us
    pallas_call x1, Pallas kernels, project(): pl.pallas_call(project_kernel, grid=(heads,), in_specs=[pl.BlockSpec((row...  7.83 us
    all_to_all x1, starting transfers between devices, body(): gathered = lax.all_to_all(partial, 'tp', 0, 0, tiled=True)  7.04 us
    unnamed x21, local copies, waits for them, and re-layouts  6.94 us
    all_to_all x1, waiting for transfers between devices, body(): gathered = lax.all_to_all(partial, 'tp', 0, 0, tiled=True)  4.78 us
    ppermute x3, starting transfers between devices, flip(): return lax.ppermute(x, 'ctx', [(i, i ^ bits) for i in range(16)])  4.18 us
  transfers between devices with their start and end apart: 11, of which 2 were waited for; matrix products, arithmetic and copies ran while one was open for 2% of the time, Pallas kernels for 50%

profile of v2, /device:TPU:1, one launch (start us, length us, event | category | flops | bytes accessed | tf_op | source)
XLA Modules:
  0.0 118.1 jit_solution(17365348232221851271)
XLA Ops:
  0.6 0.0 copy-start.4
  0.6 1.2 constant_dynamic-update-slice_fusion.1
  1.8 1.2 constant_dynamic-update-slice_fusion.refs_2_.refs_3_
  3.0 0.0 copy-start.1
  3.0 1.5 %collective-permute-start = (bf16[2048,256]{1,0:T(8,128)(2,1)S(1)}, bf16[2048,256]{1,0:T(8,128)(2,1)S(1)}, u32[]{:S(2)}, u32[]{:S(2)}) collective-permute-start(bf16[2048,256]{1,0:T(8,128)(2,1)S(1)} %constant_dynamic-update-slice_fusion.refs_2_.refs_3_), channel_id=1, source_target_pairs={{0,8},{8,0},{16,24},{24,16},{32,40},{40,32},{48,56},{56,48},{64,72... | collective-permute-start | bytes 3145736 | tf_op jit(solution)/shard_map/ppermute | solution.py:329
  4.5 1.7 %collective-permute-start.1 = (bf16[2048,256]{1,0:T(8,128)(2,1)S(1)}, bf16[2048,256]{1,0:T(8,128)(2,1)}, u32[]{:S(2)}, u32[]{:S(2)}) collective-permute-start(bf16[2048,256]{1,0:T(8,128)(2,1)S(1)} %constant_dynamic-update-slice_fusion.refs_2_.refs_3_), channel_id=1, source_target_pairs={{0,16},{8,24},{16,0},{24,8},{32,48},{40,56},{48,32},{56,40},{64,80... | collective-permute-start | bytes 3145736 | tf_op jit(solution)/shard_map/ppermute | solution.py:329
  6.2 7.8 %project.1 = bf16[8,128,256]{2,1,0:T(8,128)(2,1)} custom-call(bf16[128,2048]{1,0:T(8,128)(2,1)} %tok_ref.1, bf16[2048,2048]{1,0:T(8,128)(2,1)} %w_ref.1), custom_call_target="tpu_custom_call" | custom-call | flops 1000 | bytes 1000 | tf_op jit(solution)/shard_map/project/pallas_call | solution.py:44
  14.1 7.0 %all-to-all-start = ((bf16[8,128,256]{2,1,0:T(8,128)(2,1)}), bf16[8,128,256]{2,1,0:T(8,128)(2,1)S(1)}, u32[]{:S(2)}, u32[]{:S(2)}) async-start(bf16[8,128,256]{2,1,0:T(8,128)(2,1)} %project.1), calls=%async_computation | async-start | bytes 1048576 | tf_op jit(solution)/shard_map/all_to_all | solution.py:346
  21.1 0.0 copy-done.4
  21.1 1.4 %collective-permute-start.2 = (bf16[128,1024]{1,0:T(8,128)(2,1)S(1)}, bf16[128,1024]{1,0:T(8,128)(2,1)S(1)}, u32[]{:S(2)}, u32[]{:S(2)}) collective-permute-start(bf16[128,1024]{1,0:T(8,128)(2,1)S(1)} %copy-done.4), channel_id=1, source_target_pairs={{0,32},{8,40},{16,48},{24,56},{32,64},{40,72},{48,80},{56,88},{64,... | collective-permute-start | bytes 786440 | tf_op jit(solution)/shard_map/ppermute | solution.py:333
  22.5 1.5 %collective-permute-start.3 = (bf16[128,1024]{1,0:T(8,128)(2,1)S(1)}, bf16[128,1024]{1,0:T(8,128)(2,1)S(1)}, u32[]{:S(2)}, u32[]{:S(2)}) collective-permute-start(bf16[128,1024]{1,0:T(8,128)(2,1)S(1)} %copy-done.4), channel_id=1, source_target_pairs={{0,96},{8,104},{16,112},{24,120},{32,0},{40,8},{48,16},{56,24},{64... | collective-permute-start | bytes 786440 | tf_op jit(solution)/shard_map/ppermute | solution.py:333
  24.0 1.6 %collective-permute-start.4 = (bf16[128,1024]{1,0:T(8,128)(2,1)S(1)}, bf16[128,1024]{1,0:T(8,128)(2,1)}, u32[]{:S(2)}, u32[]{:S(2)}) collective-permute-start(bf16[128,1024]{1,0:T(8,128)(2,1)S(1)} %copy-done.4), channel_id=1, source_target_pairs={{0,64},{8,72},{16,80},{24,88},{32,96},{40,104},{48,112},{56,120},{... | collective-permute-start | bytes 786440 | tf_op jit(solution)/shard_map/ppermute | solution.py:333
  25.6 0.0 collective-permute-done.refs_3_.refs_4_
  25.6 0.0 copy-done.1
  25.6 0.0 copy-start.2
  25.6 1.0 copy-done.2
  26.5 7.1 %attend.5.refs_5_ = bf16[1,128,1152]{2,1,0:T(8,128)(2,1)} custom-call(s32[16]{0:T(128)} %refs_0_.4, bf16[128,1024]{1,0:T(8,128)(2,1)} %refs_1_.3, bf16[2048,256]{1,0:T(8,128)(2,1)} %copy-done.1, bf16[2048,256]{1,0:T(8,128)(2,1)} %copy-done.2), custom_call_target="tpu_custom_call" | custom-call | flops 1000 | bytes 1000 | tf_op jit(solution)/shard_map/attend/pallas_call | solution.py:246
  33.6 4.8 %all-to-all-done = bf16[8,128,256]{2,1,0:T(8,128)(2,1)S(1)} async-done(((bf16[8,128,256]{2,1,0:T(8,128)(2,1)}), bf16[8,128,256]{2,1,0:T(8,128)(2,1)S(1)}, u32[]{:S(2)}, u32[]{:S(2)}) %all-to-all-start) | async-done | bytes 524320 | tf_op jit(solution)/shard_map/all_to_all | solution.py:346
  38.4 0.0 collective-permute-done.2.refs_1_
  38.4 0.0 copy-start.5
  38.4 0.0 collective-permute-done.3.refs_2_
  38.4 0.7 copy-done.5
  39.1 0.0 copy-start.6
  39.1 0.7 copy-done.6
  39.8 11.4 %attend.6.refs_6_.refs_7_ = bf16[2,128,1152]{2,1,0:T(8,128)(2,1)} custom-call(s32[16]{0:T(128)} %refs_0_.4, bf16[128,1024]{1,0:T(8,128)(2,1)} %copy-done.5, bf16[128,1024]{1,0:T(8,128)(2,1)} %copy-done.6, bf16[2048,256]{1,0:T(8,128)(2,1)} %copy-done.1, bf16[2048,256]{1,0:T(8,128)(2,1)} %copy-done.2), custom_call_target="tpu_custom_call" | custom-call | flops 1000 | bytes 1000 | tf_op jit(solution)/shard_map/attend/pallas_call | solution.py:246
  51.2 0.0 collective-permute-done.1.refs_4_.refs_2_
  51.2 0.9 collective-permute-start.5
  52.2 0.1 reduce_sum.12
  52.3 1.1 broadcast_in_dim.2
  53.3 8.4 %all-to-all-start.1 = ((bf16[16,128,256]{2,1,0:T(8,128)(2,1)}), bf16[16,128,256]{2,1,0:T(8,128)(2,1)S(1)}, u32[]{:S(2)}, u32[]{:S(2)}) async-start(bf16[16,128,256]{2,1,0:T(8,128)(2,1)} %broadcast_in_dim.2), calls=%async_computation.1 | async-start | bytes 2097152 | tf_op jit(solution)/shard_map/all_to_all | solution.py:354
  61.7 0.0 collective-permute-done.4.refs_1_.refs_3_
  61.7 7.1 %attend.7.refs_8_ = bf16[1,128,1152]{2,1,0:T(8,128)(2,1)} custom-call(s32[16]{0:T(128)} %refs_0_.4, bf16[128,1024]{1,0:T(8,128)(2,1)} %collective-permute-done.4.refs_1_.refs_3_, bf16[2048,256]{1,0:T(8,128)(2,1)} %copy-done.1, bf16[2048,256]{1,0:T(8,128)(2,1)} %copy-done.2), custom_call_target="tpu_custom_call" | custom-call | flops 20000000000 | bytes 1000 | tf_op jit(solution)/shard_map/attend/pallas_call | solution.py:246
  68.8 0.0 collective-permute-done.5.refs_5_.refs_3_
  68.8 0.0 copy-start.3
  68.8 1.0 copy-done.3
  69.8 14.9 %attend.8 = bf16[3,128,1152]{2,1,0:T(8,128)(2,1)} custom-call(s32[16]{0:T(128)} %refs_0_.4, bf16[128,1024]{1,0:T(8,128)(2,1)} %copy-done.5, bf16[128,1024]{1,0:T(8,128)(2,1)} %copy-done.6, bf16[128,1024]{1,0:T(8,128)(2,1)} %collective-permute-done.4.refs_1_.refs_3_, bf16[2048,256]{1,0:T(8,128)(2,1)} %collective-permute-done.1.refs_4_.refs_2_, ...), custom_call_target="tpu_custom_call" | custom-call | flops 1000 | bytes 1000 | tf_op jit(solution)/shard_map/attend/pallas_call | solution.py:246
  84.7 1.2 %fusion = (bf16[1,128,1152]{2,1,0:T(8,128)(2,1)S(1)}, bf16[1,128,1152]{2,1,0:T(8,128)(2,1)S(1)}, bf16[1,128,1152]{2,1,0:T(8,128)(2,1)S(1)}) fusion(bf16[3,128,1152]{2,1,0:T(8,128)(2,1)} %attend.8), kind=kLoop, calls=%fused_computation.2 | loop fusion | bytes 1769472 | tf_op jit(solution)/shard_map/slice | solution.py:363
  86.0 12.6 %collective-permute-start.6 = (bf16[1,128,1152]{2,1,0:T(8,128)(2,1)S(1)}, bf16[1,128,1152]{2,1,0:T(8,128)(2,1)S(1)}, u32[]{:S(2)}, u32[]{:S(2)}) collective-permute-start(bf16[1,128,1152]{2,1,0:T(8,128)(2,1)S(1)} %get-tuple-element.16), channel_id=1, source_target_pairs={{0,96},{8,104},{16,112},{24,120},{32,0},{40,8},{48,16},{56,24},{64... | collective-permute-start | bytes 884744 | tf_op jit(solution)/shard_map/ppermute | solution.py:333
  98.5 0.0 collective-permute-start.7
  98.5 1.3 %collective-permute-start.8 = (bf16[1,128,1152]{2,1,0:T(8,128)(2,1)S(1)}, bf16[1,128,1152]{2,1,0:T(8,128)(2,1)S(1)}, u32[]{:S(2)}, u32[]{:S(2)}) collective-permute-start(bf16[1,128,1152]{2,1,0:T(8,128)(2,1)S(1)} %get-tuple-element.14), channel_id=1, source_target_pairs={{0,64},{8,72},{16,80},{24,88},{32,96},{40,104},{48,112},{56,120},{... | collective-permute-start | bytes 884744 | tf_op jit(solution)/shard_map/ppermute | solution.py:333
  99.8 0.0 all-to-all-done.1
  99.8 0.0 copy-start
  99.8 1.0 copy-done
  100.8 2.8 %pages.1 = bf16[256,256]{1,0:T(8,128)(2,1)} custom-call(s32[64]{0:T(128)} %owner_ref.1, s32[64]{0:T(128)} %slot_ref.1, bf16[2048,256]{1,0:T(8,128)(2,1)} %bitcast.1), custom_call_target="tpu_custom_call" | custom-call | flops 1000 | bytes 1000 | tf_op jit(solution)/shard_map/pages/pallas_call | solution.py:317
  103.6 7.4 %attend.9.refs_0_ = bf16[1,128,1152]{2,1,0:T(8,128)(2,1)} custom-call(s32[16]{0:T(128)} %refs_0_.4, bf16[128,1024]{1,0:T(8,128)(2,1)} %refs_1_.3, bf16[2048,256]{1,0:T(8,128)(2,1)} %collective-permute-done.1.refs_4_.refs_2_, bf16[2048,256]{1,0:T(8,128)(2,1)} %copy-done.3, bf16[2048,256]{1,0:T(8,128)(2,1)} %bitcast.2, bf16[1,128,1152]{2,1,0:T(8,128)(2,1)} %attend.5.refs_5_), custom_call_target="tpu_custom_call" | custom-call | flops 1000 | bytes 1000 | tf_op jit(solution)/shard_map/attend/pallas_call | solution.py:246
  111.0 0.0 collective-permute-done.6.refs_1_
  111.0 0.0 copy-start.7
  111.0 2.9 %collective-permute-done.7.refs_2_ = bf16[1,128,1152]{2,1,0:T(8,128)(2,1)S(1)} collective-permute-done((bf16[1,128,1152]{2,1,0:T(8,128)(2,1)S(1)}, bf16[1,128,1152]{2,1,0:T(8,128)(2,1)S(1)}, u32[]{:S(2)}, u32[]{:S(2)}) %collective-permute-start.7) | collective-permute-done | bytes 294944 | tf_op jit(solution)/shard_map/ppermute | solution.py:333
  114.0 0.0 copy-start.8
  114.0 0.0 collective-permute-done.8.refs_3_
  114.0 0.0 copy-done.7
  114.0 0.7 copy-done.8
  114.7 0.0 copy-start.9
  114.7 0.7 copy-done.9
  115.4 2.7 %merge.1 = bf16[128,1024]{1,0:T(8,128)(2,1)} custom-call(bf16[1,128,1152]{2,1,0:T(8,128)(2,1)} %attend.9.refs_0_, bf16[1,128,1152]{2,1,0:T(8,128)(2,1)} %copy-done.7, bf16[1,128,1152]{2,1,0:T(8,128)(2,1)} %copy-done.8, bf16[1,128,1152]{2,1,0:T(8,128)(2,1)} %copy-done.9), custom_call_target="tpu_custom_call" | custom-call | flops 1000 | bytes 1000 | tf_op jit(solution)/shard_map/merge/pallas_call | solution.py:285
Async XLA Ops:
  0.6 20.5 %copy-start.4 = (bf16[128,1024]{1,0:T(8,128)(2,1)S(1)}, bf16[128,1024]{1,0:T(8,128)(2,1)}, u32[]{:S(2)}) copy-start(bf16[128,1024]{1,0:T(8,128)(2,1)} %refs_1_.3) | copy-start | bytes 786436
  3.0 22.6 %copy-start.1 = (bf16[2048,256]{1,0:T(8,128)(2,1)}, bf16[2048,256]{1,0:T(8,128)(2,1)S(1)}, u32[]{:S(2)}) copy-start(bf16[2048,256]{1,0:T(8,128)(2,1)S(1)} %constant_dynamic-update-slice_fusion.refs_2_.refs_3_) | copy-start | bytes 3145732
  3.0 22.6 %collective-permute-start = (bf16[2048,256]{1,0:T(8,128)(2,1)S(1)}, bf16[2048,256]{1,0:T(8,128)(2,1)S(1)}, u32[]{:S(2)}, u32[]{:S(2)}) collective-permute-start(bf16[2048,256]{1,0:T(8,128)(2,1)S(1)} %constant_dynamic-update-slice_fusion.refs_2_.refs_3_), channel_id=1, source_target_pairs={{0,8},{8,0},{16,24},{24,16},{32,40},{40,32},{48,56},{56,48},{64,72... | collective-permute-start | bytes 3145736 | tf_op jit(solution)/shard_map/ppermute | solution.py:329
  4.5 46.7 %collective-permute-start.1 = (bf16[2048,256]{1,0:T(8,128)(2,1)S(1)}, bf16[2048,256]{1,0:T(8,128)(2,1)}, u32[]{:S(2)}, u32[]{:S(2)}) collective-permute-start(bf16[2048,256]{1,0:T(8,128)(2,1)S(1)} %constant_dynamic-update-slice_fusion.refs_2_.refs_3_), channel_id=1, source_target_pairs={{0,16},{8,24},{16,0},{24,8},{32,48},{40,56},{48,32},{56,40},{64,80... | collective-permute-start | bytes 3145736 | tf_op jit(solution)/shard_map/ppermute | solution.py:329
  14.1 24.3 %all-to-all-start = ((bf16[8,128,256]{2,1,0:T(8,128)(2,1)}), bf16[8,128,256]{2,1,0:T(8,128)(2,1)S(1)}, u32[]{:S(2)}, u32[]{:S(2)}) async-start(bf16[8,128,256]{2,1,0:T(8,128)(2,1)} %project.1), calls=%async_computation | async-start | bytes 1048576 | tf_op jit(solution)/shard_map/all_to_all | solution.py:346
  21.1 17.3 %collective-permute-start.2 = (bf16[128,1024]{1,0:T(8,128)(2,1)S(1)}, bf16[128,1024]{1,0:T(8,128)(2,1)S(1)}, u32[]{:S(2)}, u32[]{:S(2)}) collective-permute-start(bf16[128,1024]{1,0:T(8,128)(2,1)S(1)} %copy-done.4), channel_id=1, source_target_pairs={{0,32},{8,40},{16,48},{24,56},{32,64},{40,72},{48,80},{56,88},{64,... | collective-permute-start | bytes 786440 | tf_op jit(solution)/shard_map/ppermute | solution.py:333
  22.5 15.9 %collective-permute-start.3 = (bf16[128,1024]{1,0:T(8,128)(2,1)S(1)}, bf16[128,1024]{1,0:T(8,128)(2,1)S(1)}, u32[]{:S(2)}, u32[]{:S(2)}) collective-permute-start(bf16[128,1024]{1,0:T(8,128)(2,1)S(1)} %copy-done.4), channel_id=1, source_target_pairs={{0,96},{8,104},{16,112},{24,120},{32,0},{40,8},{48,16},{56,24},{64... | collective-permute-start | bytes 786440 | tf_op jit(solution)/shard_map/ppermute | solution.py:333
  24.0 37.7 %collective-permute-start.4 = (bf16[128,1024]{1,0:T(8,128)(2,1)S(1)}, bf16[128,1024]{1,0:T(8,128)(2,1)}, u32[]{:S(2)}, u32[]{:S(2)}) collective-permute-start(bf16[128,1024]{1,0:T(8,128)(2,1)S(1)} %copy-done.4), channel_id=1, source_target_pairs={{0,64},{8,72},{16,80},{24,88},{32,96},{40,104},{48,112},{56,120},{... | collective-permute-start | bytes 786440 | tf_op jit(solution)/shard_map/ppermute | solution.py:333
  25.6 1.0 copy-start.2
  38.4 0.7 copy-start.5
  39.1 0.7 copy-start.6
  51.2 17.6 %collective-permute-start.5 = (bf16[2048,256]{1,0:T(8,128)(2,1)}, bf16[2048,256]{1,0:T(8,128)(2,1)S(1)}, u32[]{:S(2)}, u32[]{:S(2)}) collective-permute-start(bf16[2048,256]{1,0:T(8,128)(2,1)} %collective-permute-done.1.refs_4_.refs_2_), channel_id=1, source_target_pairs={{0,8},{8,0},{16,24},{24,16},{32,40},{40,32},{48,56},{56,48},{64,72... | collective-permute-start | bytes 3145736 | tf_op jit(solution)/shard_map/ppermute | solution.py:329
  53.3 46.5 %all-to-all-start.1 = ((bf16[16,128,256]{2,1,0:T(8,128)(2,1)}), bf16[16,128,256]{2,1,0:T(8,128)(2,1)S(1)}, u32[]{:S(2)}, u32[]{:S(2)}) async-start(bf16[16,128,256]{2,1,0:T(8,128)(2,1)} %broadcast_in_dim.2), calls=%async_computation.1 | async-start | bytes 2097152 | tf_op jit(solution)/shard_map/all_to_all | solution.py:354
  68.8 1.0 copy-start.3
  86.0 25.1 %collective-permute-start.6 = (bf16[1,128,1152]{2,1,0:T(8,128)(2,1)S(1)}, bf16[1,128,1152]{2,1,0:T(8,128)(2,1)S(1)}, u32[]{:S(2)}, u32[]{:S(2)}) collective-permute-start(bf16[1,128,1152]{2,1,0:T(8,128)(2,1)S(1)} %get-tuple-element.16), channel_id=1, source_target_pairs={{0,96},{8,104},{16,112},{24,120},{32,0},{40,8},{48,16},{56,24},{64... | collective-permute-start | bytes 884744 | tf_op jit(solution)/shard_map/ppermute | solution.py:333
  98.5 15.5 %collective-permute-start.7 = (bf16[1,128,1152]{2,1,0:T(8,128)(2,1)S(1)}, bf16[1,128,1152]{2,1,0:T(8,128)(2,1)S(1)}, u32[]{:S(2)}, u32[]{:S(2)}) collective-permute-start(bf16[1,128,1152]{2,1,0:T(8,128)(2,1)S(1)} %get-tuple-element.15), channel_id=1, source_target_pairs={{0,32},{8,40},{16,48},{24,56},{32,64},{40,72},{48,80},{56,88},{64,... | collective-permute-start | bytes 884744 | tf_op jit(solution)/shard_map/ppermute | solution.py:333
  98.5 15.5 %collective-permute-start.8 = (bf16[1,128,1152]{2,1,0:T(8,128)(2,1)S(1)}, bf16[1,128,1152]{2,1,0:T(8,128)(2,1)S(1)}, u32[]{:S(2)}, u32[]{:S(2)}) collective-permute-start(bf16[1,128,1152]{2,1,0:T(8,128)(2,1)S(1)} %get-tuple-element.14), channel_id=1, source_target_pairs={{0,64},{8,72},{16,80},{24,88},{32,96},{40,104},{48,112},{56,120},{... | collective-permute-start | bytes 884744 | tf_op jit(solution)/shard_map/ppermute | solution.py:333
  99.8 1.0 copy-start
  111.0 3.0 %copy-start.7 = (bf16[1,128,1152]{2,1,0:T(8,128)(2,1)}, bf16[1,128,1152]{2,1,0:T(8,128)(2,1)S(1)}, u32[]{:S(2)}) copy-start(bf16[1,128,1152]{2,1,0:T(8,128)(2,1)S(1)} %collective-permute-done.6.refs_1_) | copy-start | bytes 884740
  114.0 0.7 copy-start.8
  114.7 0.7 copy-start.9

commit v3 on v2

--- a/solution.py
+++ b/solution.py
@@ -14,7 +14,7 @@
 BIG = 2.0**100
 F32 = jnp.float32
 BF16 = jnp.bfloat16
-VMEM_LIMIT = 56 * 2**20
+VMEM_LIMIT = 63 * 2**20 + 2**19 + 2**18 + 2**17
 SMALL = pl.CostEstimate(flops=1000, bytes_accessed=1000, transcendentals=0)
 
 
@@ -35,20 +35,23 @@
 
 
 def project_kernel(tok_ref, w_ref, out_ref):
-    out_ref[0] = nn_dot(tok_ref[...], w_ref[...]).astype(BF16)
+    result = nn_dot(tok_ref[...], w_ref[...]).astype(BF16)
+    for h in range(out_ref.shape[0]):
+        out_ref[h] = result[:, h * 2 * HD : (h + 1) * 2 * HD]
 
 
 def project(tokens, kv_weight):
     rows, depth = tokens.shape
     heads = kv_weight.shape[1] // (2 * HD)
+    at_once = 2
     return pl.pallas_call(
         project_kernel,
-        grid=(heads,),
+        grid=(heads // at_once,),
         in_specs=[
             pl.BlockSpec((rows, depth), lambda h: (0, 0)),
-            pl.BlockSpec((depth, 2 * HD), lambda h: (0, h)),
+            pl.BlockSpec((depth, at_once * 2 * HD), lambda h: (0, h)),
         ],
-        out_specs=pl.BlockSpec((1, rows, 2 * HD), lambda h: (h, 0, 0)),
+        out_specs=pl.BlockSpec((at_once, rows, 2 * HD), lambda h: (h, 0, 0)),
         out_shape=jax.ShapeDtypeStruct((heads, rows, 2 * HD), BF16),
         compiler_params=pltpu.CompilerParams(vmem_limit_bytes=VMEM_LIMIT),
         cost_estimate=SMALL,
@@ -64,8 +67,11 @@
     q_refs = take(nq)
     kv_refs = take(nseg)
     f_refs = take(1) if fresh else []
+    page_refs = take(2) if fresh else []
     st_refs = take(nq) if state_in else []
-    out, qb, kb, acc, ll, mm, st, sems = refs
+    outs = take(nq)
+    pages_out = take(1) if fresh else []
+    qs, qb, kb, acc, ll, mm, st, sems, q_sems, st_sems = refs
     me = lax.axis_index("ctx")
     step = pl.program_id(0)
     rows = qb.shape[0]
@@ -77,26 +83,36 @@
         for s, r in enumerate(kv_refs + f_refs)
     ]
 
+    q_copies = [
+        pltpu.make_async_copy(r, qs.at[i], q_sems.at[i]) for i, r in enumerate(q_refs)
+    ]
+    st_copies = [
+        pltpu.make_async_copy(r, st.at[i], st_sems.at[i]) for i, r in enumerate(st_refs)
+    ]
+
     @pl.when(step == 0)
     def _():
-        for c in copies:
+        q_copies[0].start()
+        for c in copies[:1] + q_copies[1:] + st_copies + copies[1:]:
             c.start()
 
     for i in range(nq):
 
         @pl.when(step == i)
         def _():
-            for g in range(groups):
-                qb[g * 128 : (g + 1) * 128, :] = q_refs[i][:, g * 128 : (g + 1) * 128]
+            q_copies[i].wait()
             if state_in:
-                st[...] = st_refs[i][0]
+                st_copies[i].wait()
+
+    for g in range(groups):
+        qb[g * 128 : (g + 1) * 128, :] = qs[step, :, g * 128 : (g + 1) * 128]
 
     @pl.when(step == 0)
     def _():
         copies[0].wait()
 
     if state_in:
-        side_in = st[:, groups * 128 :].astype(F32)
+        side_in = st[step, :, groups * 128 :].astype(F32)
         for g in range(groups):
             mm[g * 128 : (g + 1) * 128, :] = jnp.broadcast_to(side_in[:, g : g + 1], (128, 128))
     else:
@@ -206,57 +222,84 @@
     lax.while_loop(lambda turn: turn < 2, attempt, 0)
 
     lane = lax.broadcasted_iota(jnp.int32, (128, 128), 1)
-    side = jnp.zeros((128, 128), F32)
-    for g in range(groups):
-        part = slice(g * 128, (g + 1) * 128)
-        mixed = acc[part, :]
-        total = jnp.sum(ll[part, :], axis=-1, keepdims=True)
-        top = mm[part, :]
-        if state_in:
-            decay = jnp.exp2(side_in[:, g : g + 1] - top)
-            mixed = mixed + st[:, part].astype(F32) * decay
-            total = total + (side_in[:, 8 + g : 9 + g] + side_in[:, 16 + g : 17 + g]) * decay
-        out[0, :, part] = mixed.astype(BF16)
-        high = total.astype(BF16).astype(F32)
-        side = jnp.where(lane == g, top, side)
-        side = jnp.where(lane == 8 + g, high, side)
-        side = jnp.where(lane == 16 + g, total - high, side)
-    out[0, :, groups * 128 :] = side.astype(BF16)
-
-
-def attend(lengths, qs, kvs, owner_xor, state=None, fresh=None, flops=1000):
+
+    def finish(out):
+        side = jnp.zeros((128, 128), F32)
+        for g in range(groups):
+            part = slice(g * 128, (g + 1) * 128)
+            mixed = acc[part, :]
+            total = jnp.sum(ll[part, :], axis=-1, keepdims=True)
+            top = mm[part, :]
+            if state_in:
+                decay = jnp.exp2(side_in[:, g : g + 1] - top)
+                mixed = mixed + st[step, :, part].astype(F32) * decay
+                total = total + (side_in[:, 8 + g : 9 + g] + side_in[:, 16 + g : 17 + g]) * decay
+            out[:, part] = mixed.astype(BF16)
+            high = total.astype(BF16).astype(F32)
+            side = jnp.where(lane == g, top, side)
+            side = jnp.where(lane == 8 + g, high, side)
+            side = jnp.where(lane == 16 + g, total - high, side)
+        out[:, groups * 128 :] = side.astype(BF16)
+
+    for i in range(nq):
+
+        @pl.when(step == i)
+        def _():
+            finish(outs[i])
+
+    if fresh:
+        owner_ref, slot_ref = page_refs
+        (pages,) = pages_out
+        pages[...] = jnp.zeros_like(pages)
+
+        def one_page(page, carry):
+            @pl.when(owner_ref[page] == me)
+            def _():
+                src = pl.ds(pl.multiple_of(nseg * seg + page * PAGE, PAGE), PAGE)
+                dst = pl.ds(pl.multiple_of(slot_ref[page] * PAGE, PAGE), PAGE)
+                pages[dst, :] = kb[src, :]
+
+            return carry
+
+        lax.fori_loop(0, owner_ref.shape[0], one_page, 0)
+
+
+def attend(lengths, qs, kvs, owner_xor, state=None, fresh=None, pages=None, flops=1000):
     nq, nseg, seg = len(qs), len(kvs), kvs[0].shape[0]
     width = qs[0].shape[1]
     rows = width
     cfg = (nq, nseg, seg, owner_xor, state is not None, fresh is not None)
-    packed = pl.BlockSpec((1, 128, width + 128), lambda i: (i, 0, 0))
     any_spec = pl.BlockSpec(memory_space=pl.ANY)
     args = [lengths, *qs, *kvs]
-    in_specs = [smem_spec()] + [vmem_spec()] * nq + [any_spec] * nseg
+    in_specs = [smem_spec()] + [any_spec] * (nq + nseg)
+    out_specs = [pl.BlockSpec((128, width + 128), lambda i: (0, 0))] * nq
+    out_shape = [jax.ShapeDtypeStruct((128, width + 128), BF16)] * nq
     if fresh is not None:
-        args.append(fresh)
-        in_specs.append(any_spec)
+        args += [fresh, *pages]
+        in_specs += [any_spec, smem_spec(), smem_spec()]
+        out_specs.append(pl.BlockSpec((8 * PAGE, 2 * HD), lambda i: (0, 0)))
+        out_shape.append(jax.ShapeDtypeStruct((8 * PAGE, 2 * HD), BF16))
     if state is not None:
-        args += [array for array, _ in state]
-        in_specs += [
-            pl.BlockSpec((1, 128, width + 128), functools.partial(lambda at, i: (at, 0, 0), at))
-            for _, at in state
-        ]
+        args += state
+        in_specs += [any_spec] * nq
     nsegs = nseg + (fresh is not None)
     return pl.pallas_call(
         functools.partial(attend_kernel, cfg),
         grid=(nq,),
         in_specs=in_specs,
-        out_specs=packed,
-        out_shape=jax.ShapeDtypeStruct((nq, 128, width + 128), BF16),
+        out_specs=out_specs,
+        out_shape=out_shape,
         scratch_shapes=[
+            pltpu.VMEM((nq, 128, width), BF16),
             pltpu.VMEM((rows, HD), BF16),
             pltpu.VMEM((nsegs * seg, 2 * HD), BF16),
             pltpu.VMEM((rows, HD), F32),
             pltpu.VMEM((rows, HD), F32),
             pltpu.VMEM((rows, HD), F32),
-            pltpu.VMEM((128, width + 128), BF16),
+            pltpu.VMEM((nq, 128, width + 128), BF16),
             pltpu.SemaphoreType.DMA((nsegs,)),
+            pltpu.SemaphoreType.DMA((nq,)),
+            pltpu.SemaphoreType.DMA((nq,)),
         ],
         compiler_params=pltpu.CompilerParams(vmem_limit_bytes=VMEM_LIMIT),
         cost_estimate=pl.CostEstimate(flops=flops, bytes_accessed=1000, transcendentals=0),
@@ -267,7 +310,7 @@
 def merge_kernel(*refs):
     parts, out = refs[:-1], refs[-1]
     groups = out.shape[1] // 128
-    sides = [r[0, :, groups * 128 :].astype(F32) for r in parts]
+    sides = [r[:, groups * 128 :].astype(F32) for r in parts]
     top = functools.reduce(jnp.maximum, sides)
     scales = [jnp.exp2(s - top) for s in sides]
     total = jnp.zeros_like(top)
@@ -276,53 +319,22 @@
     scales = [w / total for w in scales]
     for g in range(groups):
         part = slice(g * 128, (g + 1) * 128)
-        mixed = sum(w[:, g : g + 1] * r[0, :, part].astype(F32) for w, r in zip(scales, parts))
+        mixed = sum(w[:, g : g + 1] * r[:, part].astype(F32) for w, r in zip(scales, parts))
         out[:, part] = mixed.astype(BF16)
 
 
 def merge(parts):
-    rows, width = parts[0][1].shape[1:]
+    rows, width = parts[0].shape
     return pl.pallas_call(
         merge_kernel,
-        grid=(1,),
-        in_specs=[
-            pl.BlockSpec((1, rows, width), functools.partial(lambda at, i: (at, 0, 0), at))
-            for at, _ in parts
-        ],
-        out_specs=pl.BlockSpec((rows, width - 128), lambda i: (0, 0)),
+        grid=(2,),
+        in_specs=[pl.BlockSpec((rows // 2, width), lambda i: (i, 0))] * len(parts),
+        out_specs=pl.BlockSpec((rows // 2, width - 128), lambda i: (i, 0)),
         out_shape=jax.ShapeDtypeStruct((rows, width - 128), BF16),
         compiler_params=pltpu.CompilerParams(vmem_limit_bytes=VMEM_LIMIT),
         cost_estimate=SMALL,
         name="merge",
-    )(*[p for _, p in parts])
-
-
-def pages_kernel(owner_ref, slot_ref, fresh_ref, out):
-    me = lax.axis_index("ctx")
-    out[...] = jnp.zeros_like(out)
-
-    def one(page, carry):
-        @pl.when(owner_ref[page] == me)
-        def _():
-            src = pl.ds(pl.multiple_of(page * PAGE, PAGE), PAGE)
-            dst = pl.ds(pl.multiple_of(slot_ref[page] * PAGE, PAGE), PAGE)
-            out[dst, :] = fresh_ref[src, :]
-
-        return carry
-
-    lax.fori_loop(0, owner_ref.shape[0], one, 0)
-
-
-def pick_pages(page_owner, page_slot, fresh):
-    return pl.pallas_call(
-        pages_kernel,
-        in_specs=[smem_spec()] * 2 + [vmem_spec()],
-        out_specs=vmem_spec(),
-        out_shape=jax.ShapeDtypeStruct((8 * PAGE, 2 * HD), BF16),
-        compiler_params=pltpu.CompilerParams(vmem_limit_bytes=VMEM_LIMIT),
-        cost_estimate=SMALL,
-        name="pages",
-    )(page_owner, page_slot, fresh)
+    )(*parts)
 
 
 def flip(x, bits):
@@ -347,25 +359,24 @@
 
     near, far = (0, 1), (2, 3)
     lengths, _ = lax.optimization_barrier((cache_lengths, partial))
-    near0 = attend(lengths, [queries], (own_kv, core_kv), near)
-    lengths, gathered, _ = lax.optimization_barrier((lengths, gathered, near0))
+    near0, near1 = attend(
+        lengths, [queries, others[0]], (own_kv, core_kv), near, flops=2 * 10**10
+    )
+    lengths, gathered, far_kv, _ = lax.optimization_barrier((lengths, gathered, far_kv, near0))
     fresh = jnp.sum(gathered.astype(F32), axis=0).astype(BF16)
-    spread = jnp.broadcast_to(fresh[None], (16, *fresh.shape))
-    fresh = lax.all_to_all(spread, "ctx", 0, 0, tiled=True).reshape(16 * 128, 2 * HD)
-    kv_pages = pick_pages(page_owner, page_slot, fresh)
-    near1 = attend(lengths, others[:2], (own_kv, core_kv), near)
-    lengths, far_kv, _ = lax.optimization_barrier((lengths, far_kv, near1))
+    fresh = lax.all_gather(fresh, "ctx", axis=0, tiled=True)
     both_kv = flip(far_kv, 1)
-    near2 = attend(lengths, others[2:], (own_kv, core_kv), near, flops=2 * 10**10)
+    near2, near3 = attend(lengths, others[1:], (own_kv, core_kv), near, flops=2 * 10**10)
     sent = attend(
-        lengths, others, (far_kv, both_kv), far, state=[(near1, 0), (near1, 1), (near2, 0)]
+        lengths, others, (far_kv, both_kv), far, state=[near1, near2, near3], flops=2 * 10**10
     )
-    back = [turn(sent[i : i + 1], 4 - k) for i, k in enumerate(order)]
-    lengths, _ = lax.optimization_barrier((lengths, sent))
-    mine = attend(
-        lengths, [queries], (far_kv, both_kv), far, state=[(near0, 0)], fresh=fresh
+    back = [turn(part, 4 - k) for part, k in zip(sent, order)]
+    lengths, _ = lax.optimization_barrier((lengths, sent[0]))
+    mine, kv_pages = attend(
+        lengths, [queries], (far_kv, both_kv), far, state=[near0], fresh=fresh,
+        pages=(page_owner, page_slot),
     )
-    attended = merge([(0, mine), *[(0, b) for b in back]])
+    attended = merge([mine, *back])
     return (attended, kv_pages)
 
 

time: 120 us -> 115 us (0.958); the launches traced: 118 us -> 116 us
  starting transfers between devices: 37.9 us -> 22 us
  between operations: 0.77 us -> 14.1 us
  Pallas kernels: 61.3 us -> 69.1 us
  local copies, waits for them, and re-layouts: 10.4 us -> 3.83 us
  waiting for transfers between devices: 7.74 us -> 4.94 us
  other arithmetic: 0.07 us -> 1.76 us
    pallas_call x5 -> x4, Pallas kernels: 47.9 us -> 60.6 us  [attend(): pl.pallas_call(functools.partial(attend_kernel, cfg), grid=(nq,), in_spec...]
    all_to_all x1 -> x0, starting transfers between devices: 8.38 us -> none  [body(): lax.all_to_all(spread, 'ctx', 0, 0, tiled=True).reshape(16 * 128, 2 * HD)]
    ppermute x6, starting transfers between devices: 18.3 us -> 10.4 us  [turn(): return lax.ppermute(x, 'ctx', [(i, (i + 4 * k) % 16) for i in range(16)])]
    unnamed x21 -> x1, local copies, waits for them, and re-layouts: 6.94 us -> 1.91 us
    pallas_call x3 -> x2, Pallas kernels: 13.3 us -> 8.48 us  [the longest x1 5.74 us: project(): pl.pallas_call(project_kernel, grid=(heads // at_once,), in_specs=[pl.Blo...]
    all_to_all x1, waiting for transfers between devices: 4.78 us -> 2.66 us  [body(): gathered = lax.all_to_all(partial, 'tp', 0, 0, tiled=True)]
    reduce_sum x1, other arithmetic: 0.07 us -> 1.76 us  [body(): fresh = jnp.sum(gathered.astype(F32), axis=0).astype(BF16)]
    slice x1 -> x0, local copies, waits for them, and re-layouts: 1.21 us -> none  [body(): back = [turn(sent[i:i + 1], 4 - k) for i, k in enumerate(order)]]
  transfers between devices with their start and end apart: 11 -> 11, of which waited for: 2 -> 2; matrix products, arithmetic and copies ran while one was open for 2% -> 2% of each run, Pallas kernels for 50% -> 57%
where the time goes in v3:
time: 115 us; the launch traced here: 116 us
  Pallas kernels  69.1 us (60%)
  starting transfers between devices  22 us (19%)
  between operations  14.1 us (12%)
  waiting for transfers between devices  4.94 us (4%)
  local copies, waits for them, and re-layouts  3.83 us (3%)
  other arithmetic  1.76 us (2%)
    pallas_call x4, Pallas kernels, attend(): pl.pallas_call(functools.partial(attend_kernel, cfg), grid=(nq,), in_spec...  60.6 us
    ppermute x6, starting transfers between devices, turn(): return lax.ppermute(x, 'ctx', [(i, (i + 4 * k) % 16) for i in range(16)])  10.4 us
    all_to_all x1, starting transfers between devices, body(): gathered = lax.all_to_all(partial, 'tp', 0, 0, tiled=True)  7.04 us
    pallas_call x1, Pallas kernels, project(): pl.pallas_call(project_kernel, grid=(heads // at_once,), in_specs=[pl.Blo...  5.74 us
    ppermute x3, starting transfers between devices, flip(): return lax.ppermute(x, 'ctx', [(i, i ^ bits) for i in range(16)])  4.46 us
    pallas_call x1, Pallas kernels, merge(): pl.pallas_call(merge_kernel, grid=(2,), in_specs=[pl.BlockSpec((rows // 2...  2.74 us
    all_to_all x1, waiting for transfers between devices, body(): gathered = lax.all_to_all(partial, 'tp', 0, 0, tiled=True)  2.66 us
  transfers between devices with their start and end apart: 11, of which 2 were waited for; matrix products, arithmetic and copies ran while one was open for 2% of the time, Pallas kernels for 57%

profile of v3, /device:TPU:1, one launch (start us, length us, event | category | flops | bytes accessed | tf_op | source)
XLA Modules:
  0.0 115.7 jit_solution(7357554672616865342)
XLA Ops:
  7.2 1.9 %constant_dynamic-update-slice_fusion.1 = bf16[2048,256]{1,0:T(8,128)(2,1)} fusion(bf16[2048,128]{1,0:T(8,128)(2,1)} %param.11), kind=kLoop, calls=%fused_computation.1 | loop fusion | bytes 1048576
  9.1 1.9 %constant_dynamic-update-slice_fusion.refs_3_ = bf16[2048,256]{1,0:T(8,128)(2,1)} fusion(bf16[2048,256]{1,0:T(8,128)(2,1)} %constant_dynamic-update-slice_fusion.1, bf16[2048,128]{1,0:T(8,128)(2,1)} %param.12), kind=kLoop, calls=%fused_computation | loop fusion | bytes 1048576 | tf_op jit(solution)/shard_map/concatenate | solution.py:353
  11.0 1.4 %collective-permute-start.2 = (bf16[2048,256]{1,0:T(8,128)(2,1)}, bf16[2048,256]{1,0:T(8,128)(2,1)}, u32[]{:S(2)}, u32[]{:S(2)}) collective-permute-start(bf16[2048,256]{1,0:T(8,128)(2,1)} %constant_dynamic-update-slice_fusion.refs_3_), channel_id=1, source_target_pairs={{0,8},{8,0},{16,24},{24,16},{32,40},{40,32},{48,56},{56,48},{64,72... | collective-permute-start | bytes 3145736 | tf_op jit(solution)/shard_map/ppermute | solution.py:341
  12.4 1.4 %collective-permute-start.1 = (bf16[128,1024]{1,0:T(8,128)(2,1)}, bf16[128,1024]{1,0:T(8,128)(2,1)}, u32[]{:S(2)}, u32[]{:S(2)}) collective-permute-start(bf16[128,1024]{1,0:T(8,128)(2,1)} %refs_1_.3), channel_id=1, source_target_pairs={{0,32},{8,40},{16,48},{24,56},{32,64},{40,72},{48,80},{56,88},{64,... | collective-permute-start | bytes 786440 | tf_op jit(solution)/shard_map/ppermute | solution.py:345
  13.8 1.6 %collective-permute-start = (bf16[2048,256]{1,0:T(8,128)(2,1)}, bf16[2048,256]{1,0:T(8,128)(2,1)}, u32[]{:S(2)}, u32[]{:S(2)}) collective-permute-start(bf16[2048,256]{1,0:T(8,128)(2,1)} %constant_dynamic-update-slice_fusion.refs_3_), channel_id=1, source_target_pairs={{0,16},{8,24},{16,0},{24,8},{32,48},{40,56},{48,32},{56,40},{64,80... | collective-permute-start | bytes 3145736 | tf_op jit(solution)/shard_map/ppermute | solution.py:341
  15.4 1.4 %collective-permute-start.3 = (bf16[128,1024]{1,0:T(8,128)(2,1)}, bf16[128,1024]{1,0:T(8,128)(2,1)}, u32[]{:S(2)}, u32[]{:S(2)}) collective-permute-start(bf16[128,1024]{1,0:T(8,128)(2,1)} %refs_1_.3), channel_id=1, source_target_pairs={{0,96},{8,104},{16,112},{24,120},{32,0},{40,8},{48,16},{56,24},{64... | collective-permute-start | bytes 786440 | tf_op jit(solution)/shard_map/ppermute | solution.py:345
  16.9 1.6 %collective-permute-start.4 = (bf16[128,1024]{1,0:T(8,128)(2,1)}, bf16[128,1024]{1,0:T(8,128)(2,1)}, u32[]{:S(2)}, u32[]{:S(2)}) collective-permute-start(bf16[128,1024]{1,0:T(8,128)(2,1)} %refs_1_.3), channel_id=1, source_target_pairs={{0,64},{8,72},{16,80},{24,88},{32,96},{40,104},{48,112},{56,120},{... | collective-permute-start | bytes 786440 | tf_op jit(solution)/shard_map/ppermute | solution.py:345
  18.5 5.7 %project.1 = bf16[8,128,256]{2,1,0:T(8,128)(2,1)} custom-call(bf16[128,2048]{1,0:T(8,128)(2,1)} %tok_ref.1, bf16[2048,2048]{1,0:T(8,128)(2,1)} %w_ref.1), custom_call_target="tpu_custom_call" | custom-call | flops 1000 | bytes 1000 | tf_op jit(solution)/shard_map/project/pallas_call | solution.py:47
  24.3 7.0 %all-to-all-start = ((bf16[8,128,256]{2,1,0:T(8,128)(2,1)}), bf16[8,128,256]{2,1,0:T(8,128)(2,1)}, u32[]{:S(2)}, u32[]{:S(2)}) async-start(bf16[8,128,256]{2,1,0:T(8,128)(2,1)} %project.1), calls=%async_computation | async-start | bytes 1048576 | tf_op jit(solution)/shard_map/all_to_all | solution.py:358
  31.3 0.0 all-gather.2.cloned.1.call-start
  31.3 0.0 collective-permute-done.1.refs_2_.refs_1_
  31.3 0.0 collective-permute-done.2.refs_4_
  31.4 13.4 %attend.4 = (bf16[128,1152]{1,0:T(8,128)(2,1)}, bf16[128,1152]{1,0:T(8,128)(2,1)}) custom-call(s32[16]{0:T(128)} %refs_0_.3, bf16[128,1024]{1,0:T(8,128)(2,1)} %refs_1_.3, bf16[128,1024]{1,0:T(8,128)(2,1)} %collective-permute-done.1.refs_2_.refs_1_, bf16[2048,256]{1,0:T(8,128)(2,1)} %constant_dynamic-update-slice_fusion.refs_3_, ...), custom_call_target="tpu_custom_call" | custom-call | flops 20000000000 | bytes 1000 | tf_op jit(solution)/shard_map/attend/pallas_call | solution.py:286
  44.7 2.7 %all-to-all-done = bf16[8,128,256]{2,1,0:T(8,128)(2,1)} async-done(((bf16[8,128,256]{2,1,0:T(8,128)(2,1)}), bf16[8,128,256]{2,1,0:T(8,128)(2,1)}, u32[]{:S(2)}, u32[]{:S(2)}) %all-to-all-start) | async-done | bytes 524320 | tf_op jit(solution)/shard_map/all_to_all | solution.py:358
  47.4 0.0 collective-permute-done.refs_4_.refs_2_
  47.4 1.4 %collective-permute-start.5 = (bf16[2048,256]{1,0:T(8,128)(2,1)}, bf16[2048,256]{1,0:T(8,128)(2,1)}, u32[]{:S(2)}, u32[]{:S(2)}) collective-permute-start(bf16[2048,256]{1,0:T(8,128)(2,1)} %collective-permute-done.refs_4_.refs_2_), channel_id=1, source_target_pairs={{0,8},{8,0},{16,24},{24,16},{32,40},{40,32},{48,56},{56,48},{64,72... | collective-permute-start | bytes 3145736 | tf_op jit(solution)/shard_map/ppermute | solution.py:341
  48.8 1.8 %reduce_sum.12 = bf16[128,256]{1,0:T(8,128)(2,1)} reduce(bf16[8,128,256]{2,1,0:T(8,128)(2,1)} %all-to-all-done, bf16[]{:T(256)} %constant.2.clone.1), dimensions={0}, to_apply=%region_0.0 | reduce | flops 229376 | bytes 589826 | tf_op jit(solution)/shard_map/reduce_sum | solution.py:366
  50.5 0.0 all-gather.2.cloned.1.call-update
  50.6 0.0 collective-permute-done.3.refs_1_.refs_2_
  50.6 0.0 collective-permute-done.4.refs_2_.refs_3_
  50.6 13.3 %attend.5 = (bf16[128,1152]{1,0:T(8,128)(2,1)}, bf16[128,1152]{1,0:T(8,128)(2,1)}) custom-call(s32[16]{0:T(128)} %refs_0_.3, bf16[128,1024]{1,0:T(8,128)(2,1)} %collective-permute-done.3.refs_1_.refs_2_, bf16[128,1024]{1,0:T(8,128)(2,1)} %collective-permute-done.4.refs_2_.refs_3_, bf16[2048,256]{1,0:T(8,128)(2,1)} %constant_dynamic-update-slice_fusion.refs_3_, ...), custom_call_target="tpu_custom_call" | custom-call | flops 20000000000 | bytes 1000 | tf_op jit(solution)/shard_map/attend/pallas_call | solution.py:286
  63.9 0.0 collective-permute-done.5.refs_5_.refs_3_
  63.9 22.7 %attend.6 = (bf16[128,1152]{1,0:T(8,128)(2,1)}, bf16[128,1152]{1,0:T(8,128)(2,1)}, bf16[128,1152]{1,0:T(8,128)(2,1)}) custom-call(s32[16]{0:T(128)} %refs_0_.3, bf16[128,1024]{1,0:T(8,128)(2,1)} %collective-permute-done.1.refs_2_.refs_1_, bf16[128,1024]{1,0:T(8,128)(2,1)} %collective-permute-done.3.refs_1_.refs_2_, ...), custom_call_target="tpu_custom_call" | custom-call | flops 20000000000 | bytes 1000 | tf_op jit(solution)/shard_map/attend/pallas_call | solution.py:286
  86.7 0.1 collective-permute-start.6
  86.7 1.5 %collective-permute-start.7 = (bf16[128,1152]{1,0:T(8,128)(2,1)}, bf16[128,1152]{1,0:T(8,128)(2,1)}, u32[]{:S(2)}, u32[]{:S(2)}) collective-permute-start(bf16[128,1152]{1,0:T(8,128)(2,1)} %get-tuple-element.27), channel_id=1, source_target_pairs={{0,32},{8,40},{16,48},{24,56},{32,64},{40,72},{48,80},{56,88},{64,... | collective-permute-start | bytes 884744 | tf_op jit(solution)/shard_map/ppermute | solution.py:345
  88.2 4.4 %collective-permute-start.8 = (bf16[128,1152]{1,0:T(8,128)(2,1)}, bf16[128,1152]{1,0:T(8,128)(2,1)}, u32[]{:S(2)}, u32[]{:S(2)}) collective-permute-start(bf16[128,1152]{1,0:T(8,128)(2,1)} %get-tuple-element.28), channel_id=1, source_target_pairs={{0,64},{8,72},{16,80},{24,88},{32,96},{40,104},{48,112},{56,120},{... | collective-permute-start | bytes 884744 | tf_op jit(solution)/shard_map/ppermute | solution.py:345
  92.6 0.0 all-gather.2.cloned.1.call-done.refs_4_
  92.6 11.2 %attend.7 = (bf16[128,1152]{1,0:T(8,128)(2,1)}, bf16[256,256]{1,0:T(8,128)(2,1)}) custom-call(s32[16]{0:T(128)} %refs_0_.3, bf16[128,1024]{1,0:T(8,128)(2,1)} %refs_1_.3, bf16[2048,256]{1,0:T(8,128)(2,1)} %collective-permute-done.refs_4_.refs_2_, bf16[2048,256]{1,0:T(8,128)(2,1)} %collective-permute-done.5.refs_5_.refs_3_, ...), custom_call_target="tpu_custom_call" | custom-call | flops 1000 | bytes 1000 | tf_op jit(solution)/shard_map/attend/pallas_call | solution.py:286
  103.8 0.0 collective-permute-done.6.refs_1_
  103.9 0.0 collective-permute-done.7.refs_2_
  103.9 2.2 %collective-permute-done.8.refs_3_ = bf16[128,1152]{1,0:T(8,128)(2,1)} collective-permute-done((bf16[128,1152]{1,0:T(8,128)(2,1)}, bf16[128,1152]{1,0:T(8,128)(2,1)}, u32[]{:S(2)}, u32[]{:S(2)}) %collective-permute-start.8) | collective-permute-done | bytes 294944 | tf_op jit(solution)/shard_map/ppermute | solution.py:345
  106.1 2.7 %merge.1 = bf16[128,1024]{1,0:T(8,128)(2,1)} custom-call(bf16[128,1152]{1,0:T(8,128)(2,1)} %get-tuple-element.26.refs_0_, bf16[128,1152]{1,0:T(8,128)(2,1)} %collective-permute-done.6.refs_1_, bf16[128,1152]{1,0:T(8,128)(2,1)} %collective-permute-done.7.refs_2_, bf16[128,1152]{1,0:T(8,128)(2,1)} %collective-permute-done.8.refs_3_), custom_call_target="tpu_custom_call" | custom-call | flops 1000 | bytes 1000 | tf_op jit(solution)/shard_map/merge/pallas_call | solution.py:328
Async XLA Ops:
  11.0 20.4 %collective-permute-start.2 = (bf16[2048,256]{1,0:T(8,128)(2,1)}, bf16[2048,256]{1,0:T(8,128)(2,1)}, u32[]{:S(2)}, u32[]{:S(2)}) collective-permute-start(bf16[2048,256]{1,0:T(8,128)(2,1)} %constant_dynamic-update-slice_fusion.refs_3_), channel_id=1, source_target_pairs={{0,8},{8,0},{16,24},{24,16},{32,40},{40,32},{48,56},{56,48},{64,72... | collective-permute-start | bytes 3145736 | tf_op jit(solution)/shard_map/ppermute | solution.py:341
  12.4 18.9 %collective-permute-start.1 = (bf16[128,1024]{1,0:T(8,128)(2,1)}, bf16[128,1024]{1,0:T(8,128)(2,1)}, u32[]{:S(2)}, u32[]{:S(2)}) collective-permute-start(bf16[128,1024]{1,0:T(8,128)(2,1)} %refs_1_.3), channel_id=1, source_target_pairs={{0,32},{8,40},{16,48},{24,56},{32,64},{40,72},{48,80},{56,88},{64,... | collective-permute-start | bytes 786440 | tf_op jit(solution)/shard_map/ppermute | solution.py:345
  13.8 33.6 %collective-permute-start = (bf16[2048,256]{1,0:T(8,128)(2,1)}, bf16[2048,256]{1,0:T(8,128)(2,1)}, u32[]{:S(2)}, u32[]{:S(2)}) collective-permute-start(bf16[2048,256]{1,0:T(8,128)(2,1)} %constant_dynamic-update-slice_fusion.refs_3_), channel_id=1, source_target_pairs={{0,16},{8,24},{16,0},{24,8},{32,48},{40,56},{48,32},{56,40},{64,80... | collective-permute-start | bytes 3145736 | tf_op jit(solution)/shard_map/ppermute | solution.py:341
  15.4 35.1 %collective-permute-start.3 = (bf16[128,1024]{1,0:T(8,128)(2,1)}, bf16[128,1024]{1,0:T(8,128)(2,1)}, u32[]{:S(2)}, u32[]{:S(2)}) collective-permute-start(bf16[128,1024]{1,0:T(8,128)(2,1)} %refs_1_.3), channel_id=1, source_target_pairs={{0,96},{8,104},{16,112},{24,120},{32,0},{40,8},{48,16},{56,24},{64... | collective-permute-start | bytes 786440 | tf_op jit(solution)/shard_map/ppermute | solution.py:345
  16.9 33.7 %collective-permute-start.4 = (bf16[128,1024]{1,0:T(8,128)(2,1)}, bf16[128,1024]{1,0:T(8,128)(2,1)}, u32[]{:S(2)}, u32[]{:S(2)}) collective-permute-start(bf16[128,1024]{1,0:T(8,128)(2,1)} %refs_1_.3), channel_id=1, source_target_pairs={{0,64},{8,72},{16,80},{24,88},{32,96},{40,104},{48,112},{56,120},{... | collective-permute-start | bytes 786440 | tf_op jit(solution)/shard_map/ppermute | solution.py:345
  24.3 23.1 %all-to-all-start = ((bf16[8,128,256]{2,1,0:T(8,128)(2,1)}), bf16[8,128,256]{2,1,0:T(8,128)(2,1)}, u32[]{:S(2)}, u32[]{:S(2)}) async-start(bf16[8,128,256]{2,1,0:T(8,128)(2,1)} %project.1), calls=%async_computation | async-start | bytes 1048576 | tf_op jit(solution)/shard_map/all_to_all | solution.py:358
  31.3 61.3 %all-gather.2.cloned.1.call-start = ((), (), s32[]{:S(2)}) async-start(), calls=%async_computation.1 | async-start | bytes 1114112 | tf_op jit(solution)/shard_map/all_gather | solution.py:367
  47.4 16.5 %collective-permute-start.5 = (bf16[2048,256]{1,0:T(8,128)(2,1)}, bf16[2048,256]{1,0:T(8,128)(2,1)}, u32[]{:S(2)}, u32[]{:S(2)}) collective-permute-start(bf16[2048,256]{1,0:T(8,128)(2,1)} %collective-permute-done.refs_4_.refs_2_), channel_id=1, source_target_pairs={{0,8},{8,0},{16,24},{24,16},{32,40},{40,32},{48,56},{56,48},{64,72... | collective-permute-start | bytes 3145736 | tf_op jit(solution)/shard_map/ppermute | solution.py:341
  86.7 17.2 %collective-permute-start.6 = (bf16[128,1152]{1,0:T(8,128)(2,1)}, bf16[128,1152]{1,0:T(8,128)(2,1)}, u32[]{:S(2)}, u32[]{:S(2)}) collective-permute-start(bf16[128,1152]{1,0:T(8,128)(2,1)} %get-tuple-element.23), channel_id=1, source_target_pairs={{0,96},{8,104},{16,112},{24,120},{32,0},{40,8},{48,16},{56,24},{64... | collective-permute-start | bytes 884744 | tf_op jit(solution)/shard_map/ppermute | solution.py:345
  86.7 17.1 %collective-permute-start.7 = (bf16[128,1152]{1,0:T(8,128)(2,1)}, bf16[128,1152]{1,0:T(8,128)(2,1)}, u32[]{:S(2)}, u32[]{:S(2)}) collective-permute-start(bf16[128,1152]{1,0:T(8,128)(2,1)} %get-tuple-element.27), channel_id=1, source_target_pairs={{0,32},{8,40},{16,48},{24,56},{32,64},{40,72},{48,80},{56,88},{64,... | collective-permute-start | bytes 884744 | tf_op jit(solution)/shard_map/ppermute | solution.py:345
  88.2 17.9 %collective-permute-start.8 = (bf16[128,1152]{1,0:T(8,128)(2,1)}, bf16[128,1152]{1,0:T(8,128)(2,1)}, u32[]{:S(2)}, u32[]{:S(2)}) collective-permute-start(bf16[128,1152]{1,0:T(8,128)(2,1)} %get-tuple-element.28), channel_id=1, source_target_pairs={{0,64},{8,72},{16,80},{24,88},{32,96},{40,104},{48,112},{56,120},{... | collective-permute-start | bytes 884744 | tf_op jit(solution)/shard_map/ppermute | solution.py:345
Sparse Core Ops, SparseCore 0:
  50.7 32.3 all-gather.1

commit v4 on v3

--- a/solution.py
+++ b/solution.py
@@ -60,7 +60,7 @@
 
 
 def attend_kernel(cfg, *refs):
-    nq, nseg, seg, owner_xor, state_in, fresh = cfg
+    nq, nseg, seg, owner_xor, state_in, fresh, relay = cfg
     refs = list(refs)
     take = lambda n: [refs.pop(0) for _ in range(n)]
     (len_ref,) = take(1)
@@ -68,9 +68,14 @@
     kv_refs = take(nseg)
     f_refs = take(1) if fresh else []
     page_refs = take(2) if fresh else []
+    part_refs = take(1) if relay else []
     st_refs = take(nq) if state_in else []
     outs = take(nq)
     pages_out = take(1) if fresh else []
+    spread_out = take(1) if relay else []
+    if relay:
+        parts, total_rows, part_sem, spread_sems = refs[-4:]
+        refs = refs[:-4]
     qs, qb, kb, acc, ll, mm, st, sems, q_sems, st_sems = refs
     me = lax.axis_index("ctx")
     step = pl.program_id(0)
@@ -90,8 +95,17 @@
         pltpu.make_async_copy(r, st.at[i], st_sems.at[i]) for i, r in enumerate(st_refs)
     ]
 
+    if relay:
+        part_copy = pltpu.make_async_copy(part_refs[0], parts, part_sem.at[0])
+        spread_copies = [
+            pltpu.make_async_copy(total_rows, spread_out[0].at[i], spread_sems.at[i])
+            for i in range(spread_out[0].shape[0])
+        ]
+
     @pl.when(step == 0)
     def _():
+        if relay:
+            part_copy.start()
         q_copies[0].start()
         for c in copies[:1] + q_copies[1:] + st_copies + copies[1:]:
             c.start()
@@ -118,6 +132,18 @@
     else:
         top = jnp.max(nt_dot(qb[...], kb[:256, :HD]), axis=-1, keepdims=True) * SCALE
         mm[...] = jnp.broadcast_to(top.astype(BF16).astype(F32), mm.shape)
+
+    if relay:
+
+        @pl.when(step == 0)
+        def _():
+            part_copy.wait()
+            added = parts[0].astype(F32)
+            for i in range(1, parts.shape[0]):
+                added = added + parts[i].astype(F32)
+            total_rows[...] = added.astype(BF16)
+            for c in spread_copies:
+                c.start()
 
     def masked(vals, size, limit, slope, fill):
         col = lax.broadcasted_iota(jnp.int32, (rows, size), 1)
@@ -263,12 +289,19 @@
 
         lax.fori_loop(0, owner_ref.shape[0], one_page, 0)
 
-
-def attend(lengths, qs, kvs, owner_xor, state=None, fresh=None, pages=None, flops=1000):
+    if relay:
+
+        @pl.when(step == nq - 1)
+        def _():
+            for c in spread_copies:
+                c.wait()
+
+
+def attend(lengths, qs, kvs, owner_xor, state=None, fresh=None, pages=None, parts=None):
     nq, nseg, seg = len(qs), len(kvs), kvs[0].shape[0]
     width = qs[0].shape[1]
     rows = width
-    cfg = (nq, nseg, seg, owner_xor, state is not None, fresh is not None)
+    cfg = (nq, nseg, seg, owner_xor, state is not None, fresh is not None, parts is not None)
     any_spec = pl.BlockSpec(memory_space=pl.ANY)
     args = [lengths, *qs, *kvs]
     in_specs = [smem_spec()] + [any_spec] * (nq + nseg)
@@ -279,6 +312,19 @@
         in_specs += [any_spec, smem_spec(), smem_spec()]
         out_specs.append(pl.BlockSpec((8 * PAGE, 2 * HD), lambda i: (0, 0)))
         out_shape.append(jax.ShapeDtypeStruct((8 * PAGE, 2 * HD), BF16))
+    scratch = []
+    if parts is not None:
+        args.append(parts)
+        in_specs.append(any_spec)
+        block = parts.shape[1:]
+        out_specs.append(any_spec)
+        out_shape.append(jax.ShapeDtypeStruct((16, *block), BF16))
+        scratch = [
+            pltpu.VMEM(parts.shape, BF16),
+            pltpu.VMEM(block, BF16),
+            pltpu.SemaphoreType.DMA((1,)),
+            pltpu.SemaphoreType.DMA((16,)),
+        ]
     if state is not None:
         args += state
         in_specs += [any_spec] * nq
@@ -300,9 +346,12 @@
             pltpu.SemaphoreType.DMA((nsegs,)),
             pltpu.SemaphoreType.DMA((nq,)),
             pltpu.SemaphoreType.DMA((nq,)),
+            *scratch,
         ],
         compiler_params=pltpu.CompilerParams(vmem_limit_bytes=VMEM_LIMIT),
-        cost_estimate=pl.CostEstimate(flops=flops, bytes_accessed=1000, transcendentals=0),
+        cost_estimate=pl.CostEstimate(
+            flops=2 * 10**10, bytes_accessed=1000, transcendentals=0
+        ),
         name="attend",
     )(*args)
 
@@ -337,6 +386,31 @@
     )(*parts)
 
 
+def pack_kernel(k_ref, v_ref, out_ref, sems):
+    copies = [
+        pltpu.make_async_copy(r, out_ref.at[:, pl.ds(i * HD, HD)], sems.at[i])
+        for i, r in enumerate((k_ref, v_ref))
+    ]
+    for c in copies:
+        c.start()
+    for c in copies:
+        c.wait()
+
+
+def pack(keys, values):
+    any_spec = pl.BlockSpec(memory_space=pl.ANY)
+    return pl.pallas_call(
+        pack_kernel,
+        in_specs=[any_spec] * 2,
+        out_specs=any_spec,
+        out_shape=jax.ShapeDtypeStruct((keys.shape[0], 2 * HD), BF16),
+        scratch_shapes=[pltpu.SemaphoreType.DMA((2,))],
+        compiler_params=pltpu.CompilerParams(vmem_limit_bytes=VMEM_LIMIT),
+        cost_estimate=SMALL,
+        name="pack",
+    )(keys, values)
+
+
 def flip(x, bits):
     return lax.ppermute(x, "ctx", [(i, i ^ bits) for i in range(16)])
 
@@ -350,7 +424,7 @@
 ):
     order = (1, 3, 2)
     others = [turn(queries, k) for k in order]
-    own_kv = jnp.concatenate([cache_keys, cache_values], axis=1)
+    own_kv = pack(cache_keys, cache_values)
     far_kv = flip(own_kv, 2)
     core_kv = flip(own_kv, 1)
 
@@ -359,21 +433,16 @@
 
     near, far = (0, 1), (2, 3)
     lengths, _ = lax.optimization_barrier((cache_lengths, partial))
-    near0, near1 = attend(
-        lengths, [queries, others[0]], (own_kv, core_kv), near, flops=2 * 10**10
-    )
-    lengths, gathered, far_kv, _ = lax.optimization_barrier((lengths, gathered, far_kv, near0))
-    fresh = jnp.sum(gathered.astype(F32), axis=0).astype(BF16)
-    fresh = lax.all_gather(fresh, "ctx", axis=0, tiled=True)
+    near1, near2 = attend(lengths, others[:2], (own_kv, core_kv), near)
+    lengths, gathered, far_kv, _ = lax.optimization_barrier((lengths, gathered, far_kv, near1))
     both_kv = flip(far_kv, 1)
-    near2, near3 = attend(lengths, others[1:], (own_kv, core_kv), near, flops=2 * 10**10)
-    sent = attend(
-        lengths, others, (far_kv, both_kv), far, state=[near1, near2, near3], flops=2 * 10**10
-    )
+    near3, spread = attend(lengths, others[2:], (own_kv, core_kv), near, parts=gathered)
+    fresh = lax.all_to_all(spread, "ctx", 0, 0, tiled=True).reshape(16 * 128, 2 * HD)
+    sent = attend(lengths, others, (far_kv, both_kv), far, state=[near1, near2, near3])
     back = [turn(part, 4 - k) for part, k in zip(sent, order)]
     lengths, _ = lax.optimization_barrier((lengths, sent[0]))
     mine, kv_pages = attend(
-        lengths, [queries], (far_kv, both_kv), far, state=[near0], fresh=fresh,
+        lengths, [queries], (own_kv, core_kv, far_kv, both_kv), near + far, fresh=fresh,
         pages=(page_owner, page_slot),
     )
     attended = merge([mine, *back])

time: 115 us -> 132 us (1.15)
  Pallas kernels: 69.1 us -> 100 us
  between operations: 14.1 us -> 0.74 us
  starting transfers between devices: 22 us -> 29.7 us
  local copies, waits for them, and re-layouts: 3.83 us -> 0 us
  waiting for transfers between devices: 4.94 us -> 2.34 us
  other arithmetic: 1.76 us -> 0 us
    pallas_call x0 -> x1, Pallas kernels: none -> 32.9 us  [pack(): pl.pallas_call(pack_kernel, in_specs=[any_spec] * 2, out_specs=any_spec,...]
    all_to_all x0 -> x1, starting transfers between devices: none -> 4.44 us  [body(): lax.all_to_all(spread, 'ctx', 0, 0, tiled=True).reshape(16 * 128, 2 * HD)]
    ppermute x6, starting transfers between devices: 10.4 us -> 13 us  [turn(): return lax.ppermute(x, 'ctx', [(i, (i + 4 * k) % 16) for i in range(16)])]
    ppermute x6, waiting for transfers between devices: 2.26 us -> 0.02 us  [turn(): return lax.ppermute(x, 'ctx', [(i, (i + 4 * k) % 16) for i in range(16)])]
    concatenate x1 -> x0, local copies, waits for them, and re-layouts: 1.92 us -> none  [body(): own_kv = jnp.concatenate([cache_keys, cache_values], axis=1)]
    unnamed x1 -> x0, local copies, waits for them, and re-layouts: 1.91 us -> none
    pallas_call x4, Pallas kernels: 60.6 us -> 58.7 us  [attend(): pl.pallas_call(functools.partial(attend_kernel, cfg), grid=(nq,), in_spec...]
    reduce_sum x1 -> x0, other arithmetic: 1.76 us -> none  [body(): fresh = jnp.sum(gathered.astype(F32), axis=0).astype(BF16)]
  transfers between devices with their start and end apart: 11 -> 11, of which waited for: 2 -> 1; matrix products, arithmetic and copies ran while one was open for 2% -> 0% of each run, Pallas kernels for 57% -> 49%
where the time goes in v4:
time: 132 us; the launch traced here: 133 us
  Pallas kernels  100 us (76%)
  starting transfers between devices  29.7 us (22%)
  waiting for transfers between devices  2.34 us (2%)
    pallas_call x4, Pallas kernels, attend(): pl.pallas_call(functools.partial(attend_kernel, cfg), grid=(nq,), in_spec...  58.7 us
    pallas_call x1, Pallas kernels, pack(): pl.pallas_call(pack_kernel, in_specs=[any_spec] * 2, out_specs=any_spec,...  32.9 us
    ppermute x6, starting transfers between devices, turn(): return lax.ppermute(x, 'ctx', [(i, (i + 4 * k) % 16) for i in range(16)])  13 us
    all_to_all x1, starting transfers between devices, body(): gathered = lax.all_to_all(partial, 'tp', 0, 0, tiled=True)  7.04 us
    pallas_call x1, Pallas kernels, project(): pl.pallas_call(project_kernel, grid=(heads // at_once,), in_specs=[pl.Blo...  5.74 us
    ppermute x3, starting transfers between devices, flip(): return lax.ppermute(x, 'ctx', [(i, i ^ bits) for i in range(16)])  5.25 us
    all_to_all x1, starting transfers between devices, body(): lax.all_to_all(spread, 'ctx', 0, 0, tiled=True).reshape(16 * 128, 2 * HD)  4.44 us
    pallas_call x1, Pallas kernels, merge(): pl.pallas_call(merge_kernel, grid=(2,), in_specs=[pl.BlockSpec((rows // 2...  2.75 us
  transfers between devices with their start and end apart: 11, of which 1 were waited for; matrix products, arithmetic and copies ran while one was open for 0% of the time, Pallas kernels for 49%

profile of v4, /device:TPU:1, one launch (start us, length us, event | category | flops | bytes accessed | tf_op | source)
XLA Modules:
  0.0 132.9 jit_solution(6214519781499040366)
XLA Ops:
  0.6 32.9 %pack.1.refs_3_.refs_2_ = bf16[2048,256]{1,0:T(8,128)(2,1)} custom-call(bf16[2048,128]{1,0:T(8,128)(2,1)} %k_ref.1, bf16[2048,128]{1,0:T(8,128)(2,1)} %v_ref.1), custom_call_target="tpu_custom_call" | custom-call | flops 1000 | bytes 1000 | tf_op jit(solution)/shard_map/pack/pallas_call | solution.py:402
  33.5 1.5 %collective-permute-start.3 = (bf16[2048,256]{1,0:T(8,128)(2,1)}, bf16[2048,256]{1,0:T(8,128)(2,1)}, u32[]{:S(2)}, u32[]{:S(2)}) collective-permute-start(bf16[2048,256]{1,0:T(8,128)(2,1)} %pack.1.refs_3_.refs_2_), channel_id=1, source_target_pairs={{0,8},{8,0},{16,24},{24,16},{32,40},{40,32},{48,56},{56,48},{64,72... | collective-permute-start | bytes 3145736 | tf_op jit(solution)/shard_map/ppermute | solution.py:415
  35.0 2.8 %collective-permute-start.2 = (bf16[128,1024]{1,0:T(8,128)(2,1)}, bf16[128,1024]{1,0:T(8,128)(2,1)}, u32[]{:S(2)}, u32[]{:S(2)}) collective-permute-start(bf16[128,1024]{1,0:T(8,128)(2,1)} %refs_1_.1), channel_id=1, source_target_pairs={{0,96},{8,104},{16,112},{24,120},{32,0},{40,8},{48,16},{56,24},{64... | collective-permute-start | bytes 786440 | tf_op jit(solution)/shard_map/ppermute | solution.py:419
  37.9 0.0 collective-permute-start.1
  37.9 1.6 %collective-permute-start.4 = (bf16[128,1024]{1,0:T(8,128)(2,1)}, bf16[128,1024]{1,0:T(8,128)(2,1)}, u32[]{:S(2)}, u32[]{:S(2)}) collective-permute-start(bf16[128,1024]{1,0:T(8,128)(2,1)} %refs_1_.1), channel_id=1, source_target_pairs={{0,64},{8,72},{16,80},{24,88},{32,96},{40,104},{48,112},{56,120},{... | collective-permute-start | bytes 786440 | tf_op jit(solution)/shard_map/ppermute | solution.py:419
  39.5 1.6 %collective-permute-start = (bf16[2048,256]{1,0:T(8,128)(2,1)}, bf16[2048,256]{1,0:T(8,128)(2,1)}, u32[]{:S(2)}, u32[]{:S(2)}) collective-permute-start(bf16[2048,256]{1,0:T(8,128)(2,1)} %pack.1.refs_3_.refs_2_), channel_id=1, source_target_pairs={{0,16},{8,24},{16,0},{24,8},{32,48},{40,56},{48,32},{56,40},{64,80... | collective-permute-start | bytes 3145736 | tf_op jit(solution)/shard_map/ppermute | solution.py:415
  41.1 5.7 %project.1 = bf16[8,128,256]{2,1,0:T(8,128)(2,1)} custom-call(bf16[128,2048]{1,0:T(8,128)(2,1)} %tok_ref.1, bf16[2048,2048]{1,0:T(8,128)(2,1)} %w_ref.1), custom_call_target="tpu_custom_call" | custom-call | flops 1000 | bytes 1000 | tf_op jit(solution)/shard_map/project/pallas_call | solution.py:47
  46.9 7.0 %all-to-all-start = ((bf16[8,128,256]{2,1,0:T(8,128)(2,1)}), bf16[8,128,256]{2,1,0:T(8,128)(2,1)}, u32[]{:S(2)}, u32[]{:S(2)}) async-start(bf16[8,128,256]{2,1,0:T(8,128)(2,1)} %project.1), calls=%async_computation | async-start | bytes 1048576 | tf_op jit(solution)/shard_map/all_to_all | solution.py:432
  53.9 0.0 collective-permute-done.2.refs_2_
  53.9 0.0 collective-permute-done.1.refs_1_
  53.9 0.0 collective-permute-done.3.refs_4_.refs_3_
  53.9 16.1 %attend.4 = (bf16[128,1152]{1,0:T(8,128)(2,1)}, bf16[128,1152]{1,0:T(8,128)(2,1)}) custom-call(s32[16]{0:T(128)} %refs_0_.3, bf16[128,1024]{1,0:T(8,128)(2,1)} %collective-permute-done.1.refs_1_, bf16[128,1024]{1,0:T(8,128)(2,1)} %collective-permute-done.2.refs_2_, bf16[2048,256]{1,0:T(8,128)(2,1)} %pack.1.refs_3_.refs_2_, ...), custom_call_target="tpu_custom_call" | custom-call | flops 20000000000 | bytes 1000 | tf_op jit(solution)/shard_map/attend/pallas_call | solution.py:332
  70.1 2.3 %all-to-all-done.refs_4_ = bf16[8,128,256]{2,1,0:T(8,128)(2,1)} async-done(((bf16[8,128,256]{2,1,0:T(8,128)(2,1)}), bf16[8,128,256]{2,1,0:T(8,128)(2,1)}, u32[]{:S(2)}, u32[]{:S(2)}) %all-to-all-start) | async-done | bytes 524320 | tf_op jit(solution)/shard_map/all_to_all | solution.py:432
  72.4 0.0 collective-permute-done.refs_4_
  72.4 2.1 %collective-permute-start.5 = (bf16[2048,256]{1,0:T(8,128)(2,1)}, bf16[2048,256]{1,0:T(8,128)(2,1)}, u32[]{:S(2)}, u32[]{:S(2)}) collective-permute-start(bf16[2048,256]{1,0:T(8,128)(2,1)} %collective-permute-done.refs_4_), channel_id=1, source_target_pairs={{0,8},{8,0},{16,24},{24,16},{32,40},{40,32},{48,56},{56,48},{64,72... | collective-permute-start | bytes 3145736 | tf_op jit(solution)/shard_map/ppermute | solution.py:415
  74.5 0.0 collective-permute-done.4.refs_1_.refs_3_
  74.5 9.7 %attend.5 = (bf16[128,1152]{1,0:T(8,128)(2,1)}, bf16[16,128,256]{2,1,0:T(8,128)(2,1)}) custom-call(s32[16]{0:T(128)} %refs_0_.3, bf16[128,1024]{1,0:T(8,128)(2,1)} %collective-permute-done.4.refs_1_.refs_3_, bf16[2048,256]{1,0:T(8,128)(2,1)} %pack.1.refs_3_.refs_2_, bf16[2048,256]{1,0:T(8,128)(2,1)} %collective-permute-done.3.refs_4_.refs_3_, ...), custom_call_target="tpu_custom_call" | custom-call | flops 20000000000 | bytes 1000 | tf_op jit(solution)/shard_map/attend/pallas_call | solution.py:332
  84.2 4.4 %all-to-all-start.1 = ((bf16[16,128,256]{2,1,0:T(8,128)(2,1)}), bf16[16,128,256]{2,1,0:T(8,128)(2,1)}, u32[]{:S(2)}, u32[]{:S(2)}) async-start(bf16[16,128,256]{2,1,0:T(8,128)(2,1)} %get-tuple-element.25), calls=%async_computation.1 | async-start | bytes 2097152 | tf_op jit(solution)/shard_map/all_to_all | solution.py:440
  88.7 0.0 collective-permute-done.5.refs_5_
  88.7 17.3 %attend.6 = (bf16[128,1152]{1,0:T(8,128)(2,1)}, bf16[128,1152]{1,0:T(8,128)(2,1)}, bf16[128,1152]{1,0:T(8,128)(2,1)}) custom-call(s32[16]{0:T(128)} %refs_0_.3, bf16[128,1024]{1,0:T(8,128)(2,1)} %collective-permute-done.1.refs_1_, bf16[128,1024]{1,0:T(8,128)(2,1)} %collective-permute-done.2.refs_2_, ...), custom_call_target="tpu_custom_call" | custom-call | flops 20000000000 | bytes 1000 | tf_op jit(solution)/shard_map/attend/pallas_call | solution.py:332
  106.1 7.2 %collective-permute-start.6 = (bf16[128,1152]{1,0:T(8,128)(2,1)}, bf16[128,1152]{1,0:T(8,128)(2,1)}, u32[]{:S(2)}, u32[]{:S(2)}) collective-permute-start(bf16[128,1152]{1,0:T(8,128)(2,1)} %get-tuple-element.23), channel_id=1, source_target_pairs={{0,96},{8,104},{16,112},{24,120},{32,0},{40,8},{48,16},{56,24},{64... | collective-permute-start | bytes 884744 | tf_op jit(solution)/shard_map/ppermute | solution.py:419
  113.3 0.0 collective-permute-start.7
  113.3 1.3 collective-permute-start.8
  114.5 0.0 all-to-all-done.1
  114.5 15.6 %attend.7 = (bf16[128,1152]{1,0:T(8,128)(2,1)}, bf16[256,256]{1,0:T(8,128)(2,1)}) custom-call(s32[16]{0:T(128)} %refs_0_.3, bf16[128,1024]{1,0:T(8,128)(2,1)} %refs_1_.1, bf16[2048,256]{1,0:T(8,128)(2,1)} %pack.1.refs_3_.refs_2_, bf16[2048,256]{1,0:T(8,128)(2,1)} %collective-permute-done.3.refs_4_.refs_3_, bf16[2048,256]{1,0:T(8,128)(2,1)} %collective-permute-done.refs_4_, ...), custom_call_target="tpu_custom_call" | custom-call | flops 20000000000 | bytes 1000 | tf_op jit(solution)/shard_map/attend/pallas_call | solution.py:332
  130.1 0.0 collective-permute-done.7.refs_2_
  130.1 0.0 collective-permute-done.8.refs_3_
  130.1 0.0 collective-permute-done.6.refs_1_
  130.1 2.8 %merge.1 = bf16[128,1024]{1,0:T(8,128)(2,1)} custom-call(bf16[128,1152]{1,0:T(8,128)(2,1)} %get-tuple-element.26.refs_0_, bf16[128,1152]{1,0:T(8,128)(2,1)} %collective-permute-done.6.refs_1_, bf16[128,1152]{1,0:T(8,128)(2,1)} %collective-permute-done.7.refs_2_, bf16[128,1152]{1,0:T(8,128)(2,1)} %collective-permute-done.8.refs_3_), custom_call_target="tpu_custom_call" | custom-call | flops 1000 | bytes 1000 | tf_op jit(solution)/shard_map/merge/pallas_call | solution.py:377
Async XLA Ops:
  33.5 20.4 %collective-permute-start.3 = (bf16[2048,256]{1,0:T(8,128)(2,1)}, bf16[2048,256]{1,0:T(8,128)(2,1)}, u32[]{:S(2)}, u32[]{:S(2)}) collective-permute-start(bf16[2048,256]{1,0:T(8,128)(2,1)} %pack.1.refs_3_.refs_2_), channel_id=1, source_target_pairs={{0,8},{8,0},{16,24},{24,16},{32,40},{40,32},{48,56},{56,48},{64,72... | collective-permute-start | bytes 3145736 | tf_op jit(solution)/shard_map/ppermute | solution.py:415
  35.0 18.9 %collective-permute-start.2 = (bf16[128,1024]{1,0:T(8,128)(2,1)}, bf16[128,1024]{1,0:T(8,128)(2,1)}, u32[]{:S(2)}, u32[]{:S(2)}) collective-permute-start(bf16[128,1024]{1,0:T(8,128)(2,1)} %refs_1_.1), channel_id=1, source_target_pairs={{0,96},{8,104},{16,112},{24,120},{32,0},{40,8},{48,16},{56,24},{64... | collective-permute-start | bytes 786440 | tf_op jit(solution)/shard_map/ppermute | solution.py:419
  37.9 16.1 %collective-permute-start.1 = (bf16[128,1024]{1,0:T(8,128)(2,1)}, bf16[128,1024]{1,0:T(8,128)(2,1)}, u32[]{:S(2)}, u32[]{:S(2)}) collective-permute-start(bf16[128,1024]{1,0:T(8,128)(2,1)} %refs_1_.1), channel_id=1, source_target_pairs={{0,32},{8,40},{16,48},{24,56},{32,64},{40,72},{48,80},{56,88},{64,... | collective-permute-start | bytes 786440 | tf_op jit(solution)/shard_map/ppermute | solution.py:419
  37.9 36.6 %collective-permute-start.4 = (bf16[128,1024]{1,0:T(8,128)(2,1)}, bf16[128,1024]{1,0:T(8,128)(2,1)}, u32[]{:S(2)}, u32[]{:S(2)}) collective-permute-start(bf16[128,1024]{1,0:T(8,128)(2,1)} %refs_1_.1), channel_id=1, source_target_pairs={{0,64},{8,72},{16,80},{24,88},{32,96},{40,104},{48,112},{56,120},{... | collective-permute-start | bytes 786440 | tf_op jit(solution)/shard_map/ppermute | solution.py:419
  39.5 32.9 %collective-permute-start = (bf16[2048,256]{1,0:T(8,128)(2,1)}, bf16[2048,256]{1,0:T(8,128)(2,1)}, u32[]{:S(2)}, u32[]{:S(2)}) collective-permute-start(bf16[2048,256]{1,0:T(8,128)(2,1)} %pack.1.refs_3_.refs_2_), channel_id=1, source_target_pairs={{0,16},{8,24},{16,0},{24,8},{32,48},{40,56},{48,32},{56,40},{64,80... | collective-permute-start | bytes 3145736 | tf_op jit(solution)/shard_map/ppermute | solution.py:415
  46.9 25.5 %all-to-all-start = ((bf16[8,128,256]{2,1,0:T(8,128)(2,1)}), bf16[8,128,256]{2,1,0:T(8,128)(2,1)}, u32[]{:S(2)}, u32[]{:S(2)}) async-start(bf16[8,128,256]{2,1,0:T(8,128)(2,1)} %project.1), calls=%async_computation | async-start | bytes 1048576 | tf_op jit(solution)/shard_map/all_to_all | solution.py:432
  72.4 16.3 %collective-permute-start.5 = (bf16[2048,256]{1,0:T(8,128)(2,1)}, bf16[2048,256]{1,0:T(8,128)(2,1)}, u32[]{:S(2)}, u32[]{:S(2)}) collective-permute-start(bf16[2048,256]{1,0:T(8,128)(2,1)} %collective-permute-done.refs_4_), channel_id=1, source_target_pairs={{0,8},{8,0},{16,24},{24,16},{32,40},{40,32},{48,56},{56,48},{64,72... | collective-permute-start | bytes 3145736 | tf_op jit(solution)/shard_map/ppermute | solution.py:415
  84.2 30.3 %all-to-all-start.1 = ((bf16[16,128,256]{2,1,0:T(8,128)(2,1)}), bf16[16,128,256]{2,1,0:T(8,128)(2,1)}, u32[]{:S(2)}, u32[]{:S(2)}) async-start(bf16[16,128,256]{2,1,0:T(8,128)(2,1)} %get-tuple-element.25), calls=%async_computation.1 | async-start | bytes 2097152 | tf_op jit(solution)/shard_map/all_to_all | solution.py:440
  106.1 24.1 %collective-permute-start.6 = (bf16[128,1152]{1,0:T(8,128)(2,1)}, bf16[128,1152]{1,0:T(8,128)(2,1)}, u32[]{:S(2)}, u32[]{:S(2)}) collective-permute-start(bf16[128,1152]{1,0:T(8,128)(2,1)} %get-tuple-element.23), channel_id=1, source_target_pairs={{0,96},{8,104},{16,112},{24,120},{32,0},{40,8},{48,16},{56,24},{64... | collective-permute-start | bytes 884744 | tf_op jit(solution)/shard_map/ppermute | solution.py:419
  113.3 16.8 %collective-permute-start.7 = (bf16[128,1152]{1,0:T(8,128)(2,1)}, bf16[128,1152]{1,0:T(8,128)(2,1)}, u32[]{:S(2)}, u32[]{:S(2)}) collective-permute-start(bf16[128,1152]{1,0:T(8,128)(2,1)} %get-tuple-element.27), channel_id=1, source_target_pairs={{0,32},{8,40},{16,48},{24,56},{32,64},{40,72},{48,80},{56,88},{64,... | collective-permute-start | bytes 884744 | tf_op jit(solution)/shard_map/ppermute | solution.py:419
  113.3 16.8 %collective-permute-start.8 = (bf16[128,1152]{1,0:T(8,128)(2,1)}, bf16[128,1152]{1,0:T(8,128)(2,1)}, u32[]{:S(2)}, u32[]{:S(2)}) collective-permute-start(bf16[128,1152]{1,0:T(8,128)(2,1)} %get-tuple-element.28), channel_id=1, source_target_pairs={{0,64},{8,72},{16,80},{24,88},{32,96},{40,104},{48,112},{56,120},{... | collective-permute-start | bytes 884744 | tf_op jit(solution)/shard_map/ppermute | solution.py:419

commit v5 on v4

--- a/solution.py
+++ b/solution.py
@@ -78,9 +78,8 @@
         refs = refs[:-4]
     qs, qb, kb, acc, ll, mm, st, sems, q_sems, st_sems = refs
     me = lax.axis_index("ctx")
-    step = pl.program_id(0)
     rows = qb.shape[0]
-    groups = rows // 128
+    groups = qs.shape[2] // 128
     nsegs = nseg + len(f_refs)
 
     copies = [
@@ -102,48 +101,38 @@
             for i in range(spread_out[0].shape[0])
         ]
 
-    @pl.when(step == 0)
-    def _():
-        if relay:
-            part_copy.start()
-        q_copies[0].start()
-        for c in copies[:1] + q_copies[1:] + st_copies + copies[1:]:
-            c.start()
-
+    if relay:
+        part_copy.start()
+    q_copies[0].start()
+    for c in copies[:1] + q_copies[1:] + st_copies + copies[1:]:
+        c.start()
     for i in range(nq):
-
-        @pl.when(step == i)
-        def _():
-            q_copies[i].wait()
-            if state_in:
-                st_copies[i].wait()
-
-    for g in range(groups):
-        qb[g * 128 : (g + 1) * 128, :] = qs[step, :, g * 128 : (g + 1) * 128]
-
-    @pl.when(step == 0)
-    def _():
-        copies[0].wait()
+        q_copies[i].wait()
+        for g in range(groups):
+            at = (i * groups + g) * 128
+            qb[at : at + 128, :] = qs[i, :, g * 128 : (g + 1) * 128]
+    copies[0].wait()
 
     if state_in:
-        side_in = st[step, :, groups * 128 :].astype(F32)
-        for g in range(groups):
-            mm[g * 128 : (g + 1) * 128, :] = jnp.broadcast_to(side_in[:, g : g + 1], (128, 128))
+        sides = []
+        for i in range(nq):
+            st_copies[i].wait()
+            sides.append(st[i, :, groups * 128 :].astype(F32))
+            for g in range(groups):
+                at = (i * groups + g) * 128
+                mm[at : at + 128, :] = jnp.broadcast_to(sides[i][:, g : g + 1], (128, 128))
     else:
         top = jnp.max(nt_dot(qb[...], kb[:256, :HD]), axis=-1, keepdims=True) * SCALE
         mm[...] = jnp.broadcast_to(top.astype(BF16).astype(F32), mm.shape)
 
     if relay:
-
-        @pl.when(step == 0)
-        def _():
-            part_copy.wait()
-            added = parts[0].astype(F32)
-            for i in range(1, parts.shape[0]):
-                added = added + parts[i].astype(F32)
-            total_rows[...] = added.astype(BF16)
-            for c in spread_copies:
-                c.start()
+        part_copy.wait()
+        added = parts[0].astype(F32)
+        for i in range(1, parts.shape[0]):
+            added = added + parts[i].astype(F32)
+        total_rows[...] = added.astype(BF16)
+        for c in spread_copies:
+            c.start()
 
     def masked(vals, size, limit, slope, fill):
         col = lax.broadcasted_iota(jnp.int32, (rows, size), 1)
@@ -190,7 +179,7 @@
 
             for i in range(1, nsegs):
 
-                @pl.when((s == i) & (step == 0) & (turn == 0))
+                @pl.when((s == i) & (turn == 0))
                 def _():
                     copies[i].wait()
 
@@ -249,17 +238,20 @@
 
     lane = lax.broadcasted_iota(jnp.int32, (128, 128), 1)
 
-    def finish(out):
+    for i in range(nq):
+        out = outs[i]
         side = jnp.zeros((128, 128), F32)
         for g in range(groups):
+            rows_at = slice((i * groups + g) * 128, (i * groups + g + 1) * 128)
             part = slice(g * 128, (g + 1) * 128)
-            mixed = acc[part, :]
-            total = jnp.sum(ll[part, :], axis=-1, keepdims=True)
-            top = mm[part, :]
+            mixed = acc[rows_at, :]
+            total = jnp.sum(ll[rows_at, :], axis=-1, keepdims=True)
+            top = mm[rows_at, :]
             if state_in:
-                decay = jnp.exp2(side_in[:, g : g + 1] - top)
-                mixed = mixed + st[step, :, part].astype(F32) * decay
-                total = total + (side_in[:, 8 + g : 9 + g] + side_in[:, 16 + g : 17 + g]) * decay
+                before = sides[i]
+                decay = jnp.exp2(before[:, g : g + 1] - top)
+                mixed = mixed + st[i, :, part].astype(F32) * decay
+                total = total + (before[:, 8 + g : 9 + g] + before[:, 16 + g : 17 + g]) * decay
             out[:, part] = mixed.astype(BF16)
             high = total.astype(BF16).astype(F32)
             side = jnp.where(lane == g, top, side)
@@ -267,12 +259,6 @@
             side = jnp.where(lane == 16 + g, total - high, side)
         out[:, groups * 128 :] = side.astype(BF16)
 
-    for i in range(nq):
-
-        @pl.when(step == i)
-        def _():
-            finish(outs[i])
-
     if fresh:
         owner_ref, slot_ref = page_refs
         (pages,) = pages_out
@@ -290,17 +276,14 @@
         lax.fori_loop(0, owner_ref.shape[0], one_page, 0)
 
     if relay:
-
-        @pl.when(step == nq - 1)
-        def _():
-            for c in spread_copies:
-                c.wait()
+        for c in spread_copies:
+            c.wait()
 
 
 def attend(lengths, qs, kvs, owner_xor, state=None, fresh=None, pages=None, parts=None):
     nq, nseg, seg = len(qs), len(kvs), kvs[0].shape[0]
     width = qs[0].shape[1]
-    rows = width
+    rows = nq * width
     cfg = (nq, nseg, seg, owner_xor, state is not None, fresh is not None, parts is not None)
     any_spec = pl.BlockSpec(memory_space=pl.ANY)
     args = [lengths, *qs, *kvs]
@@ -331,7 +314,7 @@
     nsegs = nseg + (fresh is not None)
     return pl.pallas_call(
         functools.partial(attend_kernel, cfg),
-        grid=(nq,),
+        grid=(1,),
         in_specs=in_specs,
         out_specs=out_specs,
         out_shape=out_shape,
@@ -386,31 +369,6 @@
     )(*parts)
 
 
-def pack_kernel(k_ref, v_ref, out_ref, sems):
-    copies = [
-        pltpu.make_async_copy(r, out_ref.at[:, pl.ds(i * HD, HD)], sems.at[i])
-        for i, r in enumerate((k_ref, v_ref))
-    ]
-    for c in copies:
-        c.start()
-    for c in copies:
-        c.wait()
-
-
-def pack(keys, values):
-    any_spec = pl.BlockSpec(memory_space=pl.ANY)
-    return pl.pallas_call(
-        pack_kernel,
-        in_specs=[any_spec] * 2,
-        out_specs=any_spec,
-        out_shape=jax.ShapeDtypeStruct((keys.shape[0], 2 * HD), BF16),
-        scratch_shapes=[pltpu.SemaphoreType.DMA((2,))],
-        compiler_params=pltpu.CompilerParams(vmem_limit_bytes=VMEM_LIMIT),
-        cost_estimate=SMALL,
-        name="pack",
-    )(keys, values)
-
-
 def flip(x, bits):
     return lax.ppermute(x, "ctx", [(i, i ^ bits) for i in range(16)])
 
@@ -424,7 +382,7 @@
 ):
     order = (1, 3, 2)
     others = [turn(queries, k) for k in order]
-    own_kv = pack(cache_keys, cache_values)
+    own_kv = jnp.concatenate([cache_keys, cache_values], axis=1)
     far_kv = flip(own_kv, 2)
     core_kv = flip(own_kv, 1)
 

time: 132 us -> 101 us (0.77)
  the two profiles are of different devices: /device:TPU:1 before, /device:TPU:44 now
where the time goes in v5:
time: 101 us
  Pallas kernels  68.1 us (67%)
  starting transfers between devices  22.2 us (22%)
  waiting for transfers between devices  6.35 us (6%)
  local copies, waits for them, and re-layouts  3.84 us (4%)
    pallas_call x4, Pallas kernels, attend(): pl.pallas_call(functools.partial(attend_kernel, cfg), grid=(1,), in_specs...  59.6 us
    ppermute x6, starting transfers between devices, turn(): return lax.ppermute(x, 'ctx', [(i, (i + 4 * k) % 16) for i in range(16)])  8.33 us
    all_to_all x1, starting transfers between devices, body(): gathered = lax.all_to_all(partial, 'tp', 0, 0, tiled=True)  7.51 us
    all_to_all x1, waiting for transfers between devices, body(): gathered = lax.all_to_all(partial, 'tp', 0, 0, tiled=True)  6.32 us
    all_to_all x1, starting transfers between devices, body(): lax.all_to_all(spread, 'ctx', 0, 0, tiled=True).reshape(16 * 128, 2 * HD)  6.2 us
    pallas_call x1, Pallas kernels, project(): pl.pallas_call(project_kernel, grid=(heads // at_once,), in_specs=[pl.Blo...  5.74 us
    pallas_call x1, Pallas kernels, merge(): pl.pallas_call(merge_kernel, grid=(2,), in_specs=[pl.BlockSpec((rows // 2...  2.75 us
  transfers between devices with their start and end apart: 11, of which 1 were waited for; matrix products, arithmetic and copies ran while one was open for 0% of the time, Pallas kernels for 65%

profile of v5, /device:TPU:44, one launch (start us, length us, event | category | flops | bytes accessed | tf_op | source)
XLA Modules:
  0.0 101.1 jit_solution(16412219399115766796)
XLA Ops:
  0.6 1.9 %constant_dynamic-update-slice_fusion.1 = bf16[2048,256]{1,0:T(8,128)(2,1)} fusion(bf16[2048,128]{1,0:T(8,128)(2,1)} %param.11), kind=kLoop, calls=%fused_computation.1 | loop fusion | bytes 1048576
  2.6 1.9 %constant_dynamic-update-slice_fusion.refs_3_.refs_2_ = bf16[2048,256]{1,0:T(8,128)(2,1)} fusion(bf16[2048,256]{1,0:T(8,128)(2,1)} %constant_dynamic-update-slice_fusion.1, bf16[2048,128]{1,0:T(8,128)(2,1)} %param.12), kind=kLoop, calls=%fused_computation | loop fusion | bytes 1048576 | tf_op jit(solution)/shard_map/concatenate | solution.py:385
  4.5 0.0 collective-permute-start.3
  4.5 0.4 collective-permute-start.2
  4.9 1.6 %collective-permute-start.1 = (bf16[128,1024]{1,0:T(8,128)(2,1)}, bf16[128,1024]{1,0:T(8,128)(2,1)}, u32[]{:S(2)}, u32[]{:S(2)}) collective-permute-start(bf16[128,1024]{1,0:T(8,128)(2,1)} %refs_1_.1), channel_id=1, source_target_pairs={{0,32},{8,40},{16,48},{24,56},{32,64},{40,72},{48,80},{56,88},{64,... | collective-permute-start | bytes 786440 | tf_op jit(solution)/shard_map/ppermute | solution.py:377
  6.5 3.5 %collective-permute-start.4 = (bf16[128,1024]{1,0:T(8,128)(2,1)}, bf16[128,1024]{1,0:T(8,128)(2,1)}, u32[]{:S(2)}, u32[]{:S(2)}) collective-permute-start(bf16[128,1024]{1,0:T(8,128)(2,1)} %refs_1_.1), channel_id=1, source_target_pairs={{0,64},{8,72},{16,80},{24,88},{32,96},{40,104},{48,112},{56,120},{... | collective-permute-start | bytes 786440 | tf_op jit(solution)/shard_map/ppermute | solution.py:377
  10.0 0.1 collective-permute-start
  10.1 5.7 %project.1 = bf16[8,128,256]{2,1,0:T(8,128)(2,1)} custom-call(bf16[128,2048]{1,0:T(8,128)(2,1)} %tok_ref.1, bf16[2048,2048]{1,0:T(8,128)(2,1)} %w_ref.1), custom_call_target="tpu_custom_call" | custom-call | flops 1000 | bytes 1000 | tf_op jit(solution)/shard_map/project/pallas_call | solution.py:47
  15.9 7.5 %all-to-all-start = ((bf16[8,128,256]{2,1,0:T(8,128)(2,1)}), bf16[8,128,256]{2,1,0:T(8,128)(2,1)}, u32[]{:S(2)}, u32[]{:S(2)}) async-start(bf16[8,128,256]{2,1,0:T(8,128)(2,1)} %project.1), calls=%async_computation | async-start | bytes 1048576 | tf_op jit(solution)/shard_map/all_to_all | solution.py:390
  23.4 0.0 collective-permute-done.2.refs_2_
  23.4 0.0 collective-permute-done.1.refs_1_
  23.4 0.0 collective-permute-done.3.refs_4_.refs_3_
  23.4 12.3 %attend.4 = (bf16[128,1152]{1,0:T(8,128)(2,1)}, bf16[128,1152]{1,0:T(8,128)(2,1)}) custom-call(s32[16]{0:T(128)} %refs_0_.3, bf16[128,1024]{1,0:T(8,128)(2,1)} %collective-permute-done.1.refs_1_, bf16[128,1024]{1,0:T(8,128)(2,1)} %collective-permute-done.2.refs_2_, bf16[2048,256]{1,0:T(8,128)(2,1)} %constant_dynamic-update-slice_fusion.refs_3_.refs_2_, ...), custom_call_target="tpu_custom_call" | custom-call | flops 20000000000 | bytes 1000 | tf_op jit(solution)/shard_map/attend/pallas_call | solution.py:315
  35.7 6.3 %all-to-all-done.refs_4_ = bf16[8,128,256]{2,1,0:T(8,128)(2,1)} async-done(((bf16[8,128,256]{2,1,0:T(8,128)(2,1)}), bf16[8,128,256]{2,1,0:T(8,128)(2,1)}, u32[]{:S(2)}, u32[]{:S(2)}) %all-to-all-start) | async-done | bytes 524320 | tf_op jit(solution)/shard_map/all_to_all | solution.py:390
  42.0 0.0 collective-permute-done.refs_4_
  42.0 0.0 collective-permute-start.5
  42.0 0.0 collective-permute-done.4.refs_1_.refs_3_
  42.0 8.6 %attend.5 = (bf16[128,1152]{1,0:T(8,128)(2,1)}, bf16[16,128,256]{2,1,0:T(8,128)(2,1)}) custom-call(s32[16]{0:T(128)} %refs_0_.3, bf16[128,1024]{1,0:T(8,128)(2,1)} %collective-permute-done.4.refs_1_.refs_3_, bf16[2048,256]{1,0:T(8,128)(2,1)} %constant_dynamic-update-slice_fusion.refs_3_.refs_2_, bf16[2048,256]{1,0:T(8,128)(2,1)} %collective-permute-done.3.refs_4_.refs_3_, ...), custom_call_target="tpu_custom_call" | custom-call | flops 20000000000 | bytes 1000 | tf_op jit(solution)/shard_map/attend/pallas_call | solution.py:315
  50.7 6.2 %all-to-all-start.1 = ((bf16[16,128,256]{2,1,0:T(8,128)(2,1)}), bf16[16,128,256]{2,1,0:T(8,128)(2,1)}, u32[]{:S(2)}, u32[]{:S(2)}) async-start(bf16[16,128,256]{2,1,0:T(8,128)(2,1)} %get-tuple-element.25), calls=%async_computation.1 | async-start | bytes 2097152 | tf_op jit(solution)/shard_map/all_to_all | solution.py:398
  56.9 0.0 collective-permute-done.5.refs_5_
  56.9 21.0 %attend.6 = (bf16[128,1152]{1,0:T(8,128)(2,1)}, bf16[128,1152]{1,0:T(8,128)(2,1)}, bf16[128,1152]{1,0:T(8,128)(2,1)}) custom-call(s32[16]{0:T(128)} %refs_0_.3, bf16[128,1024]{1,0:T(8,128)(2,1)} %collective-permute-done.1.refs_1_, bf16[128,1024]{1,0:T(8,128)(2,1)} %collective-permute-done.2.refs_2_, ...), custom_call_target="tpu_custom_call" | custom-call | flops 20000000000 | bytes 1000 | tf_op jit(solution)/shard_map/attend/pallas_call | solution.py:315
  77.9 0.1 collective-permute-start.6
  78.0 2.0 %collective-permute-start.7 = (bf16[128,1152]{1,0:T(8,128)(2,1)}, bf16[128,1152]{1,0:T(8,128)(2,1)}, u32[]{:S(2)}, u32[]{:S(2)}) collective-permute-start(bf16[128,1152]{1,0:T(8,128)(2,1)} %get-tuple-element.27), channel_id=1, source_target_pairs={{0,32},{8,40},{16,48},{24,56},{32,64},{40,72},{48,80},{56,88},{64,... | collective-permute-start | bytes 884744 | tf_op jit(solution)/shard_map/ppermute | solution.py:377
  80.0 0.7 collective-permute-start.8
  80.7 0.0 all-to-all-done.1
  80.7 17.6 %attend.7 = (bf16[128,1152]{1,0:T(8,128)(2,1)}, bf16[256,256]{1,0:T(8,128)(2,1)}) custom-call(s32[16]{0:T(128)} %refs_0_.3, bf16[128,1024]{1,0:T(8,128)(2,1)} %refs_1_.1, bf16[2048,256]{1,0:T(8,128)(2,1)} %constant_dynamic-update-slice_fusion.refs_3_.refs_2_, bf16[2048,256]{1,0:T(8,128)(2,1)} %collective-permute-done.3.refs_4_.refs_3_, ...), custom_call_target="tpu_custom_call" | custom-call | flops 20000000000 | bytes 1000 | tf_op jit(solution)/shard_map/attend/pallas_call | solution.py:315
  98.3 0.0 collective-permute-done.7.refs_2_
  98.3 0.0 collective-permute-done.8.refs_3_
  98.4 0.0 collective-permute-done.6.refs_1_
  98.4 2.8 %merge.1 = bf16[128,1024]{1,0:T(8,128)(2,1)} custom-call(bf16[128,1152]{1,0:T(8,128)(2,1)} %get-tuple-element.26.refs_0_, bf16[128,1152]{1,0:T(8,128)(2,1)} %collective-permute-done.6.refs_1_, bf16[128,1152]{1,0:T(8,128)(2,1)} %collective-permute-done.7.refs_2_, bf16[128,1152]{1,0:T(8,128)(2,1)} %collective-permute-done.8.refs_3_), custom_call_target="tpu_custom_call" | custom-call | flops 1000 | bytes 1000 | tf_op jit(solution)/shard_map/merge/pallas_call | solution.py:360
Async XLA Ops:
  4.5 18.9 %collective-permute-start.3 = (bf16[2048,256]{1,0:T(8,128)(2,1)}, bf16[2048,256]{1,0:T(8,128)(2,1)}, u32[]{:S(2)}, u32[]{:S(2)}) collective-permute-start(bf16[2048,256]{1,0:T(8,128)(2,1)} %constant_dynamic-update-slice_fusion.refs_3_.refs_2_), channel_id=1, source_target_pairs={{0,8},{8,0},{16,24},{24,16},{32,40},{40,32},{48,56},{56,48},{64,72... | collective-permute-start | bytes 3145736 | tf_op jit(solution)/shard_map/ppermute | solution.py:373
  4.5 18.9 %collective-permute-start.2 = (bf16[128,1024]{1,0:T(8,128)(2,1)}, bf16[128,1024]{1,0:T(8,128)(2,1)}, u32[]{:S(2)}, u32[]{:S(2)}) collective-permute-start(bf16[128,1024]{1,0:T(8,128)(2,1)} %refs_1_.1), channel_id=1, source_target_pairs={{0,96},{8,104},{16,112},{24,120},{32,0},{40,8},{48,16},{56,24},{64... | collective-permute-start | bytes 786440 | tf_op jit(solution)/shard_map/ppermute | solution.py:377
  4.9 18.4 %collective-permute-start.1 = (bf16[128,1024]{1,0:T(8,128)(2,1)}, bf16[128,1024]{1,0:T(8,128)(2,1)}, u32[]{:S(2)}, u32[]{:S(2)}) collective-permute-start(bf16[128,1024]{1,0:T(8,128)(2,1)} %refs_1_.1), channel_id=1, source_target_pairs={{0,32},{8,40},{16,48},{24,56},{32,64},{40,72},{48,80},{56,88},{64,... | collective-permute-start | bytes 786440 | tf_op jit(solution)/shard_map/ppermute | solution.py:377
  6.5 35.5 %collective-permute-start.4 = (bf16[128,1024]{1,0:T(8,128)(2,1)}, bf16[128,1024]{1,0:T(8,128)(2,1)}, u32[]{:S(2)}, u32[]{:S(2)}) collective-permute-start(bf16[128,1024]{1,0:T(8,128)(2,1)} %refs_1_.1), channel_id=1, source_target_pairs={{0,64},{8,72},{16,80},{24,88},{32,96},{40,104},{48,112},{56,120},{... | collective-permute-start | bytes 786440 | tf_op jit(solution)/shard_map/ppermute | solution.py:377
  10.0 32.0 %collective-permute-start = (bf16[2048,256]{1,0:T(8,128)(2,1)}, bf16[2048,256]{1,0:T(8,128)(2,1)}, u32[]{:S(2)}, u32[]{:S(2)}) collective-permute-start(bf16[2048,256]{1,0:T(8,128)(2,1)} %constant_dynamic-update-slice_fusion.refs_3_.refs_2_), channel_id=1, source_target_pairs={{0,16},{8,24},{16,0},{24,8},{32,48},{40,56},{48,32},{56,40},{64,80... | collective-permute-start | bytes 3145736 | tf_op jit(solution)/shard_map/ppermute | solution.py:373
  15.9 26.2 %all-to-all-start = ((bf16[8,128,256]{2,1,0:T(8,128)(2,1)}), bf16[8,128,256]{2,1,0:T(8,128)(2,1)}, u32[]{:S(2)}, u32[]{:S(2)}) async-start(bf16[8,128,256]{2,1,0:T(8,128)(2,1)} %project.1), calls=%async_computation | async-start | bytes 1048576 | tf_op jit(solution)/shard_map/all_to_all | solution.py:390
  42.0 14.9 %collective-permute-start.5 = (bf16[2048,256]{1,0:T(8,128)(2,1)}, bf16[2048,256]{1,0:T(8,128)(2,1)}, u32[]{:S(2)}, u32[]{:S(2)}) collective-permute-start(bf16[2048,256]{1,0:T(8,128)(2,1)} %collective-permute-done.refs_4_), channel_id=1, source_target_pairs={{0,8},{8,0},{16,24},{24,16},{32,40},{40,32},{48,56},{56,48},{64,72... | collective-permute-start | bytes 3145736 | tf_op jit(solution)/shard_map/ppermute | solution.py:373
  50.7 30.0 %all-to-all-start.1 = ((bf16[16,128,256]{2,1,0:T(8,128)(2,1)}), bf16[16,128,256]{2,1,0:T(8,128)(2,1)}, u32[]{:S(2)}, u32[]{:S(2)}) async-start(bf16[16,128,256]{2,1,0:T(8,128)(2,1)} %get-tuple-element.25), calls=%async_computation.1 | async-start | bytes 2097152 | tf_op jit(solution)/shard_map/all_to_all | solution.py:398
  77.9 20.5 %collective-permute-start.6 = (bf16[128,1152]{1,0:T(8,128)(2,1)}, bf16[128,1152]{1,0:T(8,128)(2,1)}, u32[]{:S(2)}, u32[]{:S(2)}) collective-permute-start(bf16[128,1152]{1,0:T(8,128)(2,1)} %get-tuple-element.23), channel_id=1, source_target_pairs={{0,96},{8,104},{16,112},{24,120},{32,0},{40,8},{48,16},{56,24},{64... | collective-permute-start | bytes 884744 | tf_op jit(solution)/shard_map/ppermute | solution.py:377
  78.0 20.4 %collective-permute-start.7 = (bf16[128,1152]{1,0:T(8,128)(2,1)}, bf16[128,1152]{1,0:T(8,128)(2,1)}, u32[]{:S(2)}, u32[]{:S(2)}) collective-permute-start(bf16[128,1152]{1,0:T(8,128)(2,1)} %get-tuple-element.27), channel_id=1, source_target_pairs={{0,32},{8,40},{16,48},{24,56},{32,64},{40,72},{48,80},{56,88},{64,... | collective-permute-start | bytes 884744 | tf_op jit(solution)/shard_map/ppermute | solution.py:377
  80.0 18.4 %collective-permute-start.8 = (bf16[128,1152]{1,0:T(8,128)(2,1)}, bf16[128,1152]{1,0:T(8,128)(2,1)}, u32[]{:S(2)}, u32[]{:S(2)}) collective-permute-start(bf16[128,1152]{1,0:T(8,128)(2,1)} %get-tuple-element.28), channel_id=1, source_target_pairs={{0,64},{8,72},{16,80},{24,88},{32,96},{40,104},{48,112},{56,120},{... | collective-permute-start | bytes 884744 | tf_op jit(solution)/shard_map/ppermute | solution.py:377

commit v6 on v5

--- a/solution.py
+++ b/solution.py
@@ -14,6 +14,7 @@
 BIG = 2.0**100
 F32 = jnp.float32
 BF16 = jnp.bfloat16
+FIRST = 4 * 10**9
 VMEM_LIMIT = 63 * 2**20 + 2**19 + 2**18 + 2**17
 SMALL = pl.CostEstimate(flops=1000, bytes_accessed=1000, transcendentals=0)
 
@@ -60,7 +61,7 @@
 
 
 def attend_kernel(cfg, *refs):
-    nq, nseg, seg, owner_xor, state_in, fresh, relay = cfg
+    nq, nseg, seg, owner_xor, state_in, fresh = cfg
     refs = list(refs)
     take = lambda n: [refs.pop(0) for _ in range(n)]
     (len_ref,) = take(1)
@@ -68,14 +69,9 @@
     kv_refs = take(nseg)
     f_refs = take(1) if fresh else []
     page_refs = take(2) if fresh else []
-    part_refs = take(1) if relay else []
     st_refs = take(nq) if state_in else []
     outs = take(nq)
     pages_out = take(1) if fresh else []
-    spread_out = take(1) if relay else []
-    if relay:
-        parts, total_rows, part_sem, spread_sems = refs[-4:]
-        refs = refs[:-4]
     qs, qb, kb, acc, ll, mm, st, sems, q_sems, st_sems = refs
     me = lax.axis_index("ctx")
     rows = qb.shape[0]
@@ -94,15 +90,6 @@
         pltpu.make_async_copy(r, st.at[i], st_sems.at[i]) for i, r in enumerate(st_refs)
     ]
 
-    if relay:
-        part_copy = pltpu.make_async_copy(part_refs[0], parts, part_sem.at[0])
-        spread_copies = [
-            pltpu.make_async_copy(total_rows, spread_out[0].at[i], spread_sems.at[i])
-            for i in range(spread_out[0].shape[0])
-        ]
-
-    if relay:
-        part_copy.start()
     q_copies[0].start()
     for c in copies[:1] + q_copies[1:] + st_copies + copies[1:]:
         c.start()
@@ -124,15 +111,6 @@
     else:
         top = jnp.max(nt_dot(qb[...], kb[:256, :HD]), axis=-1, keepdims=True) * SCALE
         mm[...] = jnp.broadcast_to(top.astype(BF16).astype(F32), mm.shape)
-
-    if relay:
-        part_copy.wait()
-        added = parts[0].astype(F32)
-        for i in range(1, parts.shape[0]):
-            added = added + parts[i].astype(F32)
-        total_rows[...] = added.astype(BF16)
-        for c in spread_copies:
-            c.start()
 
     def masked(vals, size, limit, slope, fill):
         col = lax.broadcasted_iota(jnp.int32, (rows, size), 1)
@@ -275,16 +253,14 @@
 
         lax.fori_loop(0, owner_ref.shape[0], one_page, 0)
 
-    if relay:
-        for c in spread_copies:
-            c.wait()
-
-
-def attend(lengths, qs, kvs, owner_xor, state=None, fresh=None, pages=None, parts=None):
+
+def attend(
+    lengths, qs, kvs, owner_xor, state=None, fresh=None, pages=None, flops=2 * 10**10
+):
     nq, nseg, seg = len(qs), len(kvs), kvs[0].shape[0]
     width = qs[0].shape[1]
     rows = nq * width
-    cfg = (nq, nseg, seg, owner_xor, state is not None, fresh is not None, parts is not None)
+    cfg = (nq, nseg, seg, owner_xor, state is not None, fresh is not None)
     any_spec = pl.BlockSpec(memory_space=pl.ANY)
     args = [lengths, *qs, *kvs]
     in_specs = [smem_spec()] + [any_spec] * (nq + nseg)
@@ -295,19 +271,6 @@
         in_specs += [any_spec, smem_spec(), smem_spec()]
         out_specs.append(pl.BlockSpec((8 * PAGE, 2 * HD), lambda i: (0, 0)))
         out_shape.append(jax.ShapeDtypeStruct((8 * PAGE, 2 * HD), BF16))
-    scratch = []
-    if parts is not None:
-        args.append(parts)
-        in_specs.append(any_spec)
-        block = parts.shape[1:]
-        out_specs.append(any_spec)
-        out_shape.append(jax.ShapeDtypeStruct((16, *block), BF16))
-        scratch = [
-            pltpu.VMEM(parts.shape, BF16),
-            pltpu.VMEM(block, BF16),
-            pltpu.SemaphoreType.DMA((1,)),
-            pltpu.SemaphoreType.DMA((16,)),
-        ]
     if state is not None:
         args += state
         in_specs += [any_spec] * nq
@@ -329,11 +292,10 @@
             pltpu.SemaphoreType.DMA((nsegs,)),
             pltpu.SemaphoreType.DMA((nq,)),
             pltpu.SemaphoreType.DMA((nq,)),
-            *scratch,
         ],
         compiler_params=pltpu.CompilerParams(vmem_limit_bytes=VMEM_LIMIT),
         cost_estimate=pl.CostEstimate(
-            flops=2 * 10**10, bytes_accessed=1000, transcendentals=0
+            flops=flops, bytes_accessed=1000, transcendentals=0
         ),
         name="attend",
     )(*args)
@@ -369,6 +331,36 @@
     )(*parts)
 
 
+def relay_kernel(parts, spread, total, sems):
+    added = parts[0].astype(F32)
+    for i in range(1, parts.shape[0]):
+        added = added + parts[i].astype(F32)
+    total[...] = added.astype(BF16)
+    copies = [
+        pltpu.make_async_copy(total, spread.at[i], sems.at[i]) for i in range(spread.shape[0])
+    ]
+    for c in copies:
+        c.start()
+    for c in copies:
+        c.wait()
+
+
+def relay(parts, count):
+    block = parts.shape[1:]
+    return pl.pallas_call(
+        relay_kernel,
+        in_specs=[vmem_spec()],
+        out_specs=pl.BlockSpec(memory_space=pl.ANY),
+        out_shape=jax.ShapeDtypeStruct((count, *block), BF16),
+        scratch_shapes=[pltpu.VMEM(block, BF16), pltpu.SemaphoreType.DMA((count,))],
+        compiler_params=pltpu.CompilerParams(vmem_limit_bytes=VMEM_LIMIT),
+        cost_estimate=pl.CostEstimate(
+            flops=2 * 10**10, bytes_accessed=1000, transcendentals=0
+        ),
+        name="relay",
+    )(parts)
+
+
 def flip(x, bits):
     return lax.ppermute(x, "ctx", [(i, i ^ bits) for i in range(16)])
 
@@ -391,12 +383,12 @@
 
     near, far = (0, 1), (2, 3)
     lengths, _ = lax.optimization_barrier((cache_lengths, partial))
-    near1, near2 = attend(lengths, others[:2], (own_kv, core_kv), near)
-    lengths, gathered, far_kv, _ = lax.optimization_barrier((lengths, gathered, far_kv, near1))
+    nears = attend(lengths, others, (own_kv, core_kv), near, flops=FIRST)
+    lengths, gathered, far_kv, _ = lax.optimization_barrier((lengths, gathered, far_kv, nears[0]))
     both_kv = flip(far_kv, 1)
-    near3, spread = attend(lengths, others[2:], (own_kv, core_kv), near, parts=gathered)
+    spread = relay(gathered, 16)
     fresh = lax.all_to_all(spread, "ctx", 0, 0, tiled=True).reshape(16 * 128, 2 * HD)
-    sent = attend(lengths, others, (far_kv, both_kv), far, state=[near1, near2, near3])
+    sent = attend(lengths, others, (far_kv, both_kv), far, state=list(nears))
     back = [turn(part, 4 - k) for part, k in zip(sent, order)]
     lengths, _ = lax.optimization_barrier((lengths, sent[0]))
     mine, kv_pages = attend(

time: 101 us -> 92.6 us (0.917)
  the two profiles are of different devices: /device:TPU:44 before, /device:TPU:1 now
where the time goes in v6:
time: 92.6 us; the launch traced here: 92.3 us
  Pallas kernels  56.7 us (61%)
  starting transfers between devices  31 us (33%)
  local copies, waits for them, and re-layouts  3.85 us (4%)
    pallas_call x3, Pallas kernels, attend(): pl.pallas_call(functools.partial(attend_kernel, cfg), grid=(1,), in_specs...  45.9 us
    ppermute x6, starting transfers between devices, turn(): return lax.ppermute(x, 'ctx', [(i, (i + 4 * k) % 16) for i in range(16)])  13.5 us
    all_to_all x1, starting transfers between devices, body(): gathered = lax.all_to_all(partial, 'tp', 0, 0, tiled=True)  7.04 us
    all_to_all x1, starting transfers between devices, body(): lax.all_to_all(spread, 'ctx', 0, 0, tiled=True).reshape(16 * 128, 2 * HD)  5.86 us
    pallas_call x1, Pallas kernels, project(): pl.pallas_call(project_kernel, grid=(heads // at_once,), in_specs=[pl.Blo...  5.74 us
    ppermute x3, starting transfers between devices, flip(): return lax.ppermute(x, 'ctx', [(i, i ^ bits) for i in range(16)])  4.62 us
    pallas_call x1, Pallas kernels, merge(): pl.pallas_call(merge_kernel, grid=(2,), in_specs=[pl.BlockSpec((rows // 2...  2.75 us
    pallas_call x1, Pallas kernels, relay(): pl.pallas_call(relay_kernel, in_specs=[vmem_spec()], out_specs=pl.BlockSp...  2.22 us
  transfers between devices with their start and end apart: 11, of which 0 were waited for; matrix products, arithmetic and copies ran while one was open for 0% of the time, Pallas kernels for 58%

profile of v6, /device:TPU:1, one launch (start us, length us, event | category | flops | bytes accessed | tf_op | source)
XLA Modules:
  0.0 92.3 jit_solution(15727704666543987227)
XLA Ops:
  0.6 1.9 %constant_dynamic-update-slice_fusion.1 = bf16[2048,256]{1,0:T(8,128)(2,1)} fusion(bf16[2048,128]{1,0:T(8,128)(2,1)} %param.11), kind=kLoop, calls=%fused_computation.1 | loop fusion | bytes 1048576
  2.6 1.9 %constant_dynamic-update-slice_fusion.refs_4_.refs_2_ = bf16[2048,256]{1,0:T(8,128)(2,1)} fusion(bf16[2048,256]{1,0:T(8,128)(2,1)} %constant_dynamic-update-slice_fusion.1, bf16[2048,128]{1,0:T(8,128)(2,1)} %param.12), kind=kLoop, calls=%fused_computation | loop fusion | bytes 1048576 | tf_op jit(solution)/shard_map/concatenate | solution.py:377
  4.5 1.4 %collective-permute-start.4 = (bf16[2048,256]{1,0:T(8,128)(2,1)}, bf16[2048,256]{1,0:T(8,128)(2,1)}, u32[]{:S(2)}, u32[]{:S(2)}) collective-permute-start(bf16[2048,256]{1,0:T(8,128)(2,1)} %constant_dynamic-update-slice_fusion.refs_4_.refs_2_), channel_id=1, source_target_pairs={{0,8},{8,0},{16,24},{24,16},{32,40},{40,32},{48,56},{56,48},{64,72... | collective-permute-start | bytes 3145736 | tf_op jit(solution)/shard_map/ppermute | solution.py:365
  5.9 1.7 %collective-permute-start = (bf16[2048,256]{1,0:T(8,128)(2,1)}, bf16[2048,256]{1,0:T(8,128)(2,1)}, u32[]{:S(2)}, u32[]{:S(2)}) collective-permute-start(bf16[2048,256]{1,0:T(8,128)(2,1)} %constant_dynamic-update-slice_fusion.refs_4_.refs_2_), channel_id=1, source_target_pairs={{0,16},{8,24},{16,0},{24,8},{32,48},{40,56},{48,32},{56,40},{64,80... | collective-permute-start | bytes 3145736 | tf_op jit(solution)/shard_map/ppermute | solution.py:365
  7.6 1.3 %collective-permute-start.1 = (bf16[128,1024]{1,0:T(8,128)(2,1)}, bf16[128,1024]{1,0:T(8,128)(2,1)}, u32[]{:S(2)}, u32[]{:S(2)}) collective-permute-start(bf16[128,1024]{1,0:T(8,128)(2,1)} %refs_1_.1), channel_id=1, source_target_pairs={{0,32},{8,40},{16,48},{24,56},{32,64},{40,72},{48,80},{56,88},{64,... | collective-permute-start | bytes 786440 | tf_op jit(solution)/shard_map/ppermute | solution.py:369
  8.9 1.4 %collective-permute-start.2 = (bf16[128,1024]{1,0:T(8,128)(2,1)}, bf16[128,1024]{1,0:T(8,128)(2,1)}, u32[]{:S(2)}, u32[]{:S(2)}) collective-permute-start(bf16[128,1024]{1,0:T(8,128)(2,1)} %refs_1_.1), channel_id=1, source_target_pairs={{0,96},{8,104},{16,112},{24,120},{32,0},{40,8},{48,16},{56,24},{64... | collective-permute-start | bytes 786440 | tf_op jit(solution)/shard_map/ppermute | solution.py:369
  10.4 1.6 %collective-permute-start.3 = (bf16[128,1024]{1,0:T(8,128)(2,1)}, bf16[128,1024]{1,0:T(8,128)(2,1)}, u32[]{:S(2)}, u32[]{:S(2)}) collective-permute-start(bf16[128,1024]{1,0:T(8,128)(2,1)} %refs_1_.1), channel_id=1, source_target_pairs={{0,64},{8,72},{16,80},{24,88},{32,96},{40,104},{48,112},{56,120},{... | collective-permute-start | bytes 786440 | tf_op jit(solution)/shard_map/ppermute | solution.py:369
  12.0 5.7 %project.1 = bf16[8,128,256]{2,1,0:T(8,128)(2,1)} custom-call(bf16[128,2048]{1,0:T(8,128)(2,1)} %tok_ref.1, bf16[2048,2048]{1,0:T(8,128)(2,1)} %w_ref.1), custom_call_target="tpu_custom_call" | custom-call | flops 1000 | bytes 1000 | tf_op jit(solution)/shard_map/project/pallas_call | solution.py:48
  17.7 7.0 %all-to-all-start = ((bf16[8,128,256]{2,1,0:T(8,128)(2,1)}), bf16[8,128,256]{2,1,0:T(8,128)(2,1)}, u32[]{:S(2)}, u32[]{:S(2)}) async-start(bf16[8,128,256]{2,1,0:T(8,128)(2,1)} %project.1), calls=%async_computation | async-start | bytes 1048576 | tf_op jit(solution)/shard_map/all_to_all | solution.py:382
  24.8 0.0 collective-permute-done.1.refs_1_
  24.8 0.0 collective-permute-done.2.refs_2_
  24.8 0.0 collective-permute-done.3.refs_3_
  24.8 0.0 collective-permute-done.4.refs_5_.refs_3_
  24.8 15.7 %attend.3 = (bf16[128,1152]{1,0:T(8,128)(2,1)}, bf16[128,1152]{1,0:T(8,128)(2,1)}, bf16[128,1152]{1,0:T(8,128)(2,1)}) custom-call(s32[16]{0:T(128)} %refs_0_.2, bf16[128,1024]{1,0:T(8,128)(2,1)} %collective-permute-done.1.refs_1_, bf16[128,1024]{1,0:T(8,128)(2,1)} %collective-permute-done.2.refs_2_, bf16[128,1024]{1,0:T(8,128)(2,1)} %collective-permute-done.3.refs_3_, ...), custom_call_target="tpu_custom_call" | custom-call | flops 4000000000 | bytes 1000 | tf_op jit(solution)/shard_map/attend/pallas_call | solution.py:278
  40.6 0.0 all-to-all-done.parts
  40.6 0.0 collective-permute-done.refs_4_
  40.6 1.5 %collective-permute-start.5 = (bf16[2048,256]{1,0:T(8,128)(2,1)}, bf16[2048,256]{1,0:T(8,128)(2,1)}, u32[]{:S(2)}, u32[]{:S(2)}) collective-permute-start(bf16[2048,256]{1,0:T(8,128)(2,1)} %collective-permute-done.refs_4_), channel_id=1, source_target_pairs={{0,8},{8,0},{16,24},{24,16},{32,40},{40,32},{48,56},{56,48},{64,72... | collective-permute-start | bytes 3145736 | tf_op jit(solution)/shard_map/ppermute | solution.py:365
  42.1 2.2 %relay.1 = bf16[16,128,256]{2,1,0:T(8,128)(2,1)} custom-call(bf16[8,128,256]{2,1,0:T(8,128)(2,1)} %all-to-all-done.parts), custom_call_target="tpu_custom_call" | custom-call | flops 20000000000 | bytes 1000 | tf_op jit(solution)/shard_map/relay/pallas_call | solution.py:350
  44.3 5.9 %all-to-all-start.1 = ((bf16[16,128,256]{2,1,0:T(8,128)(2,1)}), bf16[16,128,256]{2,1,0:T(8,128)(2,1)}, u32[]{:S(2)}, u32[]{:S(2)}) async-start(bf16[16,128,256]{2,1,0:T(8,128)(2,1)} %relay.1), calls=%async_computation.1 | async-start | bytes 2097152 | tf_op jit(solution)/shard_map/all_to_all | solution.py:390
  50.2 0.0 collective-permute-done.5.refs_5_
  50.2 15.6 %attend.4 = (bf16[128,1152]{1,0:T(8,128)(2,1)}, bf16[128,1152]{1,0:T(8,128)(2,1)}, bf16[128,1152]{1,0:T(8,128)(2,1)}) custom-call(s32[16]{0:T(128)} %refs_0_.2, bf16[128,1024]{1,0:T(8,128)(2,1)} %collective-permute-done.1.refs_1_, bf16[128,1024]{1,0:T(8,128)(2,1)} %collective-permute-done.2.refs_2_, bf16[128,1024]{1,0:T(8,128)(2,1)} %collective-permute-done.3.refs_3_, ...), custom_call_target="tpu_custom_call" | custom-call | flops 20000000000 | bytes 1000 | tf_op jit(solution)/shard_map/attend/pallas_call | solution.py:278
  65.8 1.1 %collective-permute-start.6 = (bf16[128,1152]{1,0:T(8,128)(2,1)}, bf16[128,1152]{1,0:T(8,128)(2,1)}, u32[]{:S(2)}, u32[]{:S(2)}) collective-permute-start(bf16[128,1152]{1,0:T(8,128)(2,1)} %get-tuple-element.21), channel_id=1, source_target_pairs={{0,96},{8,104},{16,112},{24,120},{32,0},{40,8},{48,16},{56,24},{64... | collective-permute-start | bytes 884744 | tf_op jit(solution)/shard_map/ppermute | solution.py:369
  66.9 5.3 %collective-permute-start.7 = (bf16[128,1152]{1,0:T(8,128)(2,1)}, bf16[128,1152]{1,0:T(8,128)(2,1)}, u32[]{:S(2)}, u32[]{:S(2)}) collective-permute-start(bf16[128,1152]{1,0:T(8,128)(2,1)} %get-tuple-element.25), channel_id=1, source_target_pairs={{0,32},{8,40},{16,48},{24,56},{32,64},{40,72},{48,80},{56,88},{64,... | collective-permute-start | bytes 884744 | tf_op jit(solution)/shard_map/ppermute | solution.py:369
  72.3 2.7 %collective-permute-start.8 = (bf16[128,1152]{1,0:T(8,128)(2,1)}, bf16[128,1152]{1,0:T(8,128)(2,1)}, u32[]{:S(2)}, u32[]{:S(2)}) collective-permute-start(bf16[128,1152]{1,0:T(8,128)(2,1)} %get-tuple-element.26), channel_id=1, source_target_pairs={{0,64},{8,72},{16,80},{24,88},{32,96},{40,104},{48,112},{56,120},{... | collective-permute-start | bytes 884744 | tf_op jit(solution)/shard_map/ppermute | solution.py:369
  74.9 0.0 all-to-all-done.1
  74.9 14.6 %attend.5 = (bf16[128,1152]{1,0:T(8,128)(2,1)}, bf16[256,256]{1,0:T(8,128)(2,1)}) custom-call(s32[16]{0:T(128)} %refs_0_.2, bf16[128,1024]{1,0:T(8,128)(2,1)} %refs_1_.1, bf16[2048,256]{1,0:T(8,128)(2,1)} %constant_dynamic-update-slice_fusion.refs_4_.refs_2_, bf16[2048,256]{1,0:T(8,128)(2,1)} %collective-permute-done.4.refs_5_.refs_3_, ...), custom_call_target="tpu_custom_call" | custom-call | flops 20000000000 | bytes 1000 | tf_op jit(solution)/shard_map/attend/pallas_call | solution.py:278
  89.5 0.0 collective-permute-done.6.refs_1_
  89.5 0.0 collective-permute-done.7.refs_2_
  89.5 0.0 collective-permute-done.8.refs_3_
  89.5 2.8 %merge.1 = bf16[128,1024]{1,0:T(8,128)(2,1)} custom-call(bf16[128,1152]{1,0:T(8,128)(2,1)} %get-tuple-element.24.refs_0_, bf16[128,1152]{1,0:T(8,128)(2,1)} %collective-permute-done.6.refs_1_, bf16[128,1152]{1,0:T(8,128)(2,1)} %collective-permute-done.7.refs_2_, bf16[128,1152]{1,0:T(8,128)(2,1)} %collective-permute-done.8.refs_3_), custom_call_target="tpu_custom_call" | custom-call | flops 1000 | bytes 1000 | tf_op jit(solution)/shard_map/merge/pallas_call | solution.py:322
Async XLA Ops:
  4.5 20.3 %collective-permute-start.4 = (bf16[2048,256]{1,0:T(8,128)(2,1)}, bf16[2048,256]{1,0:T(8,128)(2,1)}, u32[]{:S(2)}, u32[]{:S(2)}) collective-permute-start(bf16[2048,256]{1,0:T(8,128)(2,1)} %constant_dynamic-update-slice_fusion.refs_4_.refs_2_), channel_id=1, source_target_pairs={{0,8},{8,0},{16,24},{24,16},{32,40},{40,32},{48,56},{56,48},{64,72... | collective-permute-start | bytes 3145736 | tf_op jit(solution)/shard_map/ppermute | solution.py:365
  5.9 34.7 %collective-permute-start = (bf16[2048,256]{1,0:T(8,128)(2,1)}, bf16[2048,256]{1,0:T(8,128)(2,1)}, u32[]{:S(2)}, u32[]{:S(2)}) collective-permute-start(bf16[2048,256]{1,0:T(8,128)(2,1)} %constant_dynamic-update-slice_fusion.refs_4_.refs_2_), channel_id=1, source_target_pairs={{0,16},{8,24},{16,0},{24,8},{32,48},{40,56},{48,32},{56,40},{64,80... | collective-permute-start | bytes 3145736 | tf_op jit(solution)/shard_map/ppermute | solution.py:365
  7.6 17.2 %collective-permute-start.1 = (bf16[128,1024]{1,0:T(8,128)(2,1)}, bf16[128,1024]{1,0:T(8,128)(2,1)}, u32[]{:S(2)}, u32[]{:S(2)}) collective-permute-start(bf16[128,1024]{1,0:T(8,128)(2,1)} %refs_1_.1), channel_id=1, source_target_pairs={{0,32},{8,40},{16,48},{24,56},{32,64},{40,72},{48,80},{56,88},{64,... | collective-permute-start | bytes 786440 | tf_op jit(solution)/shard_map/ppermute | solution.py:369
  8.9 15.9 %collective-permute-start.2 = (bf16[128,1024]{1,0:T(8,128)(2,1)}, bf16[128,1024]{1,0:T(8,128)(2,1)}, u32[]{:S(2)}, u32[]{:S(2)}) collective-permute-start(bf16[128,1024]{1,0:T(8,128)(2,1)} %refs_1_.1), channel_id=1, source_target_pairs={{0,96},{8,104},{16,112},{24,120},{32,0},{40,8},{48,16},{56,24},{64... | collective-permute-start | bytes 786440 | tf_op jit(solution)/shard_map/ppermute | solution.py:369
  10.4 14.4 %collective-permute-start.3 = (bf16[128,1024]{1,0:T(8,128)(2,1)}, bf16[128,1024]{1,0:T(8,128)(2,1)}, u32[]{:S(2)}, u32[]{:S(2)}) collective-permute-start(bf16[128,1024]{1,0:T(8,128)(2,1)} %refs_1_.1), channel_id=1, source_target_pairs={{0,64},{8,72},{16,80},{24,88},{32,96},{40,104},{48,112},{56,120},{... | collective-permute-start | bytes 786440 | tf_op jit(solution)/shard_map/ppermute | solution.py:369
  17.7 22.8 %all-to-all-start = ((bf16[8,128,256]{2,1,0:T(8,128)(2,1)}), bf16[8,128,256]{2,1,0:T(8,128)(2,1)}, u32[]{:S(2)}, u32[]{:S(2)}) async-start(bf16[8,128,256]{2,1,0:T(8,128)(2,1)} %project.1), calls=%async_computation | async-start | bytes 1048576 | tf_op jit(solution)/shard_map/all_to_all | solution.py:382
  40.6 9.6 %collective-permute-start.5 = (bf16[2048,256]{1,0:T(8,128)(2,1)}, bf16[2048,256]{1,0:T(8,128)(2,1)}, u32[]{:S(2)}, u32[]{:S(2)}) collective-permute-start(bf16[2048,256]{1,0:T(8,128)(2,1)} %collective-permute-done.refs_4_), channel_id=1, source_target_pairs={{0,8},{8,0},{16,24},{24,16},{32,40},{40,32},{48,56},{56,48},{64,72... | collective-permute-start | bytes 3145736 | tf_op jit(solution)/shard_map/ppermute | solution.py:365
  44.3 30.6 %all-to-all-start.1 = ((bf16[16,128,256]{2,1,0:T(8,128)(2,1)}), bf16[16,128,256]{2,1,0:T(8,128)(2,1)}, u32[]{:S(2)}, u32[]{:S(2)}) async-start(bf16[16,128,256]{2,1,0:T(8,128)(2,1)} %relay.1), calls=%async_computation.1 | async-start | bytes 2097152 | tf_op jit(solution)/shard_map/all_to_all | solution.py:390
  65.8 23.7 %collective-permute-start.6 = (bf16[128,1152]{1,0:T(8,128)(2,1)}, bf16[128,1152]{1,0:T(8,128)(2,1)}, u32[]{:S(2)}, u32[]{:S(2)}) collective-permute-start(bf16[128,1152]{1,0:T(8,128)(2,1)} %get-tuple-element.21), channel_id=1, source_target_pairs={{0,96},{8,104},{16,112},{24,120},{32,0},{40,8},{48,16},{56,24},{64... | collective-permute-start | bytes 884744 | tf_op jit(solution)/shard_map/ppermute | solution.py:369
  66.9 22.6 %collective-permute-start.7 = (bf16[128,1152]{1,0:T(8,128)(2,1)}, bf16[128,1152]{1,0:T(8,128)(2,1)}, u32[]{:S(2)}, u32[]{:S(2)}) collective-permute-start(bf16[128,1152]{1,0:T(8,128)(2,1)} %get-tuple-element.25), channel_id=1, source_target_pairs={{0,32},{8,40},{16,48},{24,56},{32,64},{40,72},{48,80},{56,88},{64,... | collective-permute-start | bytes 884744 | tf_op jit(solution)/shard_map/ppermute | solution.py:369
  72.3 17.3 %collective-permute-start.8 = (bf16[128,1152]{1,0:T(8,128)(2,1)}, bf16[128,1152]{1,0:T(8,128)(2,1)}, u32[]{:S(2)}, u32[]{:S(2)}) collective-permute-start(bf16[128,1152]{1,0:T(8,128)(2,1)} %get-tuple-element.26), channel_id=1, source_target_pairs={{0,64},{8,72},{16,80},{24,88},{32,96},{40,104},{48,112},{56,120},{... | collective-permute-start | bytes 884744 | tf_op jit(solution)/shard_map/ppermute | solution.py:369

commit v7 on v6

--- a/solution.py
+++ b/solution.py
@@ -44,7 +44,7 @@
 def project(tokens, kv_weight):
     rows, depth = tokens.shape
     heads = kv_weight.shape[1] // (2 * HD)
-    at_once = 2
+    at_once = 4
     return pl.pallas_call(
         project_kernel,
         grid=(heads // at_once,),
@@ -112,18 +112,22 @@
         top = jnp.max(nt_dot(qb[...], kb[:256, :HD]), axis=-1, keepdims=True) * SCALE
         mm[...] = jnp.broadcast_to(top.astype(BF16).astype(F32), mm.shape)
 
-    def masked(vals, size, limit, slope, fill):
-        col = lax.broadcasted_iota(jnp.int32, (rows, size), 1)
-        row = lax.rem(lax.broadcasted_iota(jnp.int32, (rows, size), 0), 128)
-        return jnp.where(col <= limit + row * slope, vals, fill)
-
-    def accumulate(at, size, limit=None, slope=None):
+    def up_to(limit, size):
+        col = lax.broadcasted_iota(jnp.int32, (8, size), 1)
+        return (col <= limit)[:1]
+
+    def not_after():
+        col = lax.broadcasted_iota(jnp.int32, (rows, 128), 1)
+        row = lax.rem(lax.broadcasted_iota(jnp.int32, (rows, 128), 0), 128)
+        return col <= row
+
+    def accumulate(at, size, seen=None):
         at = pl.ds(pl.multiple_of(at, 128), size)
         s = nt_dot(qb[...], kb[at, :HD])
         tops = jnp.concatenate([mm[...]] * (size // 128), axis=1)
         p = jnp.exp2(s * SCALE - tops)
-        if limit is not None:
-            p = masked(p, size, limit, slope, 0.0)
+        if seen is not None:
+            p = jnp.where(seen, p, 0.0)
         acc[...] += nn_dot(p.astype(BF16), kb[at, HD:])
         total = ll[...]
         for g in range(size // 128):
@@ -135,25 +139,19 @@
         for i in range(1, nseg):
             owner = jnp.where(s == i, me ^ owner_xor[i], owner)
         length = jnp.clip(len_ref[owner], 0, seg)
+        if fresh:
+            length = jnp.where(s == nseg, me * 128, length)
         whole = length // 512 * 512
-        rest = length - whole
-        limit = rest - 1
-        slope = 0
-        if fresh:
-            is_fresh = s == nseg
-            before = me * 128
-            whole = jnp.where(is_fresh, before // 512 * 512, whole)
-            rest = jnp.where(is_fresh, before - whole + 128, rest)
-            limit = jnp.where(is_fresh, before - whole, limit)
-            slope = jnp.where(is_fresh, 1, 0)
-        return s * seg, whole, rest, limit, slope
+        return s * seg, whole, length - whole
+
+    diagonal = nseg * seg + me * 128
 
     def sweep(turn):
         acc[...] = jnp.zeros_like(acc)
         ll[...] = jnp.zeros_like(ll)
 
         def one(s, carry):
-            start, whole, rest, limit, slope = segment(s)
+            start, whole, rest = segment(s)
 
             for i in range(1, nsegs):
 
@@ -175,33 +173,37 @@
 
             @pl.when(rest > 256)
             def _():
-                accumulate(start + whole, 512, limit, slope)
+                accumulate(start + whole, 512, up_to(rest - 1, 512))
 
             @pl.when((rest > 0) & (rest <= 256))
             def _():
-                accumulate(start + whole, 256, limit, slope)
+                accumulate(start + whole, 256, up_to(rest - 1, 256))
 
             return carry
 
         lax.fori_loop(0, nsegs, one, 0)
+        if fresh:
+            accumulate(diagonal, 128, not_after())
 
     def raise_tops():
+        def part(at, seen):
+            at = pl.ds(pl.multiple_of(at, 128), 128)
+            s_now = nt_dot(qb[...], kb[at, :HD]) * SCALE
+            top = jnp.max(jnp.where(seen, s_now, -3.0e38), axis=-1, keepdims=True)
+            mm[...] = jnp.maximum(mm[...], top.astype(BF16).astype(F32))
+
         def one(s, carry):
-            start, whole, rest, limit, slope = segment(s)
-
-            def part(j, c):
-                at = pl.ds(pl.multiple_of(start + j * 128, 128), 128)
-                s_now = nt_dot(qb[...], kb[at, :HD]) * SCALE
-                edge = jnp.where(j * 128 < whole, 128, limit - (j * 128 - whole))
-                tilt = jnp.where(j * 128 < whole, 0, slope)
-                s_now = masked(s_now, 128, edge, tilt, -3.0e38)
-                top = jnp.max(s_now, axis=-1, keepdims=True)
-                mm[...] = jnp.maximum(mm[...], top.astype(BF16).astype(F32))
+            start, whole, rest = segment(s)
+
+            def step(j, c):
+                part(start + j * 128, up_to(whole + rest - 1 - j * 128, 128))
                 return c
 
-            return lax.fori_loop(0, (whole + rest + 127) // 128, part, carry)
+            return lax.fori_loop(0, (whole + rest + 127) // 128, step, carry)
 
         lax.fori_loop(0, nsegs, one, 0)
+        if fresh:
+            part(diagonal, not_after())
 
     def attempt(turn):
         @pl.when(turn == 1)
@@ -361,6 +363,26 @@
     )(parts)
 
 
+def pack_kernel(k_ref, v_ref, out_ref):
+    out_ref[:, :HD] = k_ref[...]
+    out_ref[:, HD:] = v_ref[...]
+
+
+def pack(keys, values):
+    rows = keys.shape[0]
+    block = pl.BlockSpec((rows // 2, HD), lambda i: (i, 0))
+    return pl.pallas_call(
+        pack_kernel,
+        grid=(2,),
+        in_specs=[block] * 2,
+        out_specs=pl.BlockSpec((rows // 2, 2 * HD), lambda i: (i, 0)),
+        out_shape=jax.ShapeDtypeStruct((rows, 2 * HD), BF16),
+        compiler_params=pltpu.CompilerParams(vmem_limit_bytes=VMEM_LIMIT),
+        cost_estimate=SMALL,
+        name="pack",
+    )(keys, values)
+
+
 def flip(x, bits):
     return lax.ppermute(x, "ctx", [(i, i ^ bits) for i in range(16)])
 
@@ -374,7 +396,7 @@
 ):
     order = (1, 3, 2)
     others = [turn(queries, k) for k in order]
-    own_kv = jnp.concatenate([cache_keys, cache_values], axis=1)
+    own_kv = pack(cache_keys, cache_values)
     far_kv = flip(own_kv, 2)
     core_kv = flip(own_kv, 1)
 

time: 92.6 us -> 91.8 us (level)
  the two profiles are of different devices: /device:TPU:1 before, /device:TPU:58 now
where the time goes in v7:
time: 91.8 us; the launch traced here: 92.6 us
  Pallas kernels  61 us (66%)
  starting transfers between devices  29.4 us (32%)
  waiting for transfers between devices  1.51 us (2%)
    pallas_call x3, Pallas kernels, attend(): pl.pallas_call(functools.partial(attend_kernel, cfg), grid=(1,), in_specs...  48.8 us
    ppermute x6, starting transfers between devices, turn(): return lax.ppermute(x, 'ctx', [(i, (i + 4 * k) % 16) for i in range(16)])  11.3 us
    all_to_all x1, starting transfers between devices, body(): lax.all_to_all(spread, 'ctx', 0, 0, tiled=True).reshape(16 * 128, 2 * HD)  10.5 us
    all_to_all x1, starting transfers between devices, body(): gathered = lax.all_to_all(partial, 'tp', 0, 0, tiled=True)  7.54 us
    pallas_call x1, Pallas kernels, project(): pl.pallas_call(project_kernel, grid=(heads // at_once,), in_specs=[pl.Blo...  5.05 us
    pallas_call x1, Pallas kernels, merge(): pl.pallas_call(merge_kernel, grid=(2,), in_specs=[pl.BlockSpec((rows // 2...  2.75 us
    pallas_call x1, Pallas kernels, relay(): pl.pallas_call(relay_kernel, in_specs=[vmem_spec()], out_specs=pl.BlockSp...  2.26 us
    pallas_call x1, Pallas kernels, pack(): pl.pallas_call(pack_kernel, grid=(2,), in_specs=[block] * 2, out_specs=pl...  2.11 us
  transfers between devices with their start and end apart: 11, of which 1 were waited for; matrix products, arithmetic and copies ran while one was open for 0% of the time, Pallas kernels for 61%

profile of v7, /device:TPU:58, one launch (start us, length us, event | category | flops | bytes accessed | tf_op | source)
XLA Modules:
  0.0 92.6 jit_solution(2134217593371318629)
XLA Ops:
  0.6 2.1 %pack.1.refs_4_.refs_2_ = bf16[2048,256]{1,0:T(8,128)(2,1)} custom-call(bf16[2048,128]{1,0:T(8,128)(2,1)} %k_ref.1, bf16[2048,128]{1,0:T(8,128)(2,1)} %v_ref.1), custom_call_target="tpu_custom_call" | custom-call | flops 1000 | bytes 1000 | tf_op jit(solution)/shard_map/pack/pallas_call | solution.py:374
  2.7 0.0 collective-permute-start.4
  2.7 0.1 collective-permute-start
  2.9 0.2 collective-permute-start.1
  3.1 1.8 %collective-permute-start.2 = (bf16[128,1024]{1,0:T(8,128)(2,1)}, bf16[128,1024]{1,0:T(8,128)(2,1)}, u32[]{:S(2)}, u32[]{:S(2)}) collective-permute-start(bf16[128,1024]{1,0:T(8,128)(2,1)} %refs_1_.1), channel_id=1, source_target_pairs={{0,96},{8,104},{16,112},{24,120},{32,0},{40,8},{48,16},{56,24},{64... | collective-permute-start | bytes 786440 | tf_op jit(solution)/shard_map/ppermute | solution.py:391
  4.9 1.2 %collective-permute-start.3 = (bf16[128,1024]{1,0:T(8,128)(2,1)}, bf16[128,1024]{1,0:T(8,128)(2,1)}, u32[]{:S(2)}, u32[]{:S(2)}) collective-permute-start(bf16[128,1024]{1,0:T(8,128)(2,1)} %refs_1_.1), channel_id=1, source_target_pairs={{0,64},{8,72},{16,80},{24,88},{32,96},{40,104},{48,112},{56,120},{... | collective-permute-start | bytes 786440 | tf_op jit(solution)/shard_map/ppermute | solution.py:391
  6.1 5.0 %project.1 = bf16[8,128,256]{2,1,0:T(8,128)(2,1)} custom-call(bf16[128,2048]{1,0:T(8,128)(2,1)} %tok_ref.1, bf16[2048,2048]{1,0:T(8,128)(2,1)} %w_ref.1), custom_call_target="tpu_custom_call" | custom-call | flops 1000 | bytes 1000 | tf_op jit(solution)/shard_map/project/pallas_call | solution.py:48
  11.2 7.5 %all-to-all-start = ((bf16[8,128,256]{2,1,0:T(8,128)(2,1)}), bf16[8,128,256]{2,1,0:T(8,128)(2,1)}, u32[]{:S(2)}, u32[]{:S(2)}) async-start(bf16[8,128,256]{2,1,0:T(8,128)(2,1)} %project.1), calls=%async_computation | async-start | bytes 1048576 | tf_op jit(solution)/shard_map/all_to_all | solution.py:404
  18.7 0.0 collective-permute-done.1.refs_1_
  18.7 0.0 collective-permute-done.2.refs_2_
  18.7 0.0 collective-permute-done.3.refs_3_
  18.7 0.0 collective-permute-done.4.refs_5_.refs_3_
  18.7 15.4 %attend.3 = (bf16[128,1152]{1,0:T(8,128)(2,1)}, bf16[128,1152]{1,0:T(8,128)(2,1)}, bf16[128,1152]{1,0:T(8,128)(2,1)}) custom-call(s32[16]{0:T(128)} %refs_0_.2, bf16[128,1024]{1,0:T(8,128)(2,1)} %collective-permute-done.1.refs_1_, bf16[128,1024]{1,0:T(8,128)(2,1)} %collective-permute-done.2.refs_2_, bf16[128,1024]{1,0:T(8,128)(2,1)} %collective-permute-done.3.refs_3_, ...), custom_call_target="tpu_custom_call" | custom-call | flops 4000000000 | bytes 1000 | tf_op jit(solution)/shard_map/attend/pallas_call | solution.py:280
  34.1 1.5 %all-to-all-done.parts = bf16[8,128,256]{2,1,0:T(8,128)(2,1)} async-done(((bf16[8,128,256]{2,1,0:T(8,128)(2,1)}), bf16[8,128,256]{2,1,0:T(8,128)(2,1)}, u32[]{:S(2)}, u32[]{:S(2)}) %all-to-all-start) | async-done | bytes 524320 | tf_op jit(solution)/shard_map/all_to_all | solution.py:404
  35.6 0.0 collective-permute-done.refs_4_
  35.6 0.0 collective-permute-start.5
  35.6 2.3 %relay.1 = bf16[16,128,256]{2,1,0:T(8,128)(2,1)} custom-call(bf16[8,128,256]{2,1,0:T(8,128)(2,1)} %all-to-all-done.parts), custom_call_target="tpu_custom_call" | custom-call | flops 20000000000 | bytes 1000 | tf_op jit(solution)/shard_map/relay/pallas_call | solution.py:352
  37.9 10.5 %all-to-all-start.1 = ((bf16[16,128,256]{2,1,0:T(8,128)(2,1)}), bf16[16,128,256]{2,1,0:T(8,128)(2,1)}, u32[]{:S(2)}, u32[]{:S(2)}) async-start(bf16[16,128,256]{2,1,0:T(8,128)(2,1)} %relay.1), calls=%async_computation.1 | async-start | bytes 2097152 | tf_op jit(solution)/shard_map/all_to_all | solution.py:412
  48.3 0.0 collective-permute-done.5.refs_5_
  48.3 16.7 %attend.4 = (bf16[128,1152]{1,0:T(8,128)(2,1)}, bf16[128,1152]{1,0:T(8,128)(2,1)}, bf16[128,1152]{1,0:T(8,128)(2,1)}) custom-call(s32[16]{0:T(128)} %refs_0_.2, bf16[128,1024]{1,0:T(8,128)(2,1)} %collective-permute-done.1.refs_1_, bf16[128,1024]{1,0:T(8,128)(2,1)} %collective-permute-done.2.refs_2_, bf16[128,1024]{1,0:T(8,128)(2,1)} %collective-permute-done.3.refs_3_, ...), custom_call_target="tpu_custom_call" | custom-call | flops 20000000000 | bytes 1000 | tf_op jit(solution)/shard_map/attend/pallas_call | solution.py:280
  65.0 5.6 %collective-permute-start.6 = (bf16[128,1152]{1,0:T(8,128)(2,1)}, bf16[128,1152]{1,0:T(8,128)(2,1)}, u32[]{:S(2)}, u32[]{:S(2)}) collective-permute-start(bf16[128,1152]{1,0:T(8,128)(2,1)} %get-tuple-element.21), channel_id=1, source_target_pairs={{0,96},{8,104},{16,112},{24,120},{32,0},{40,8},{48,16},{56,24},{64... | collective-permute-start | bytes 884744 | tf_op jit(solution)/shard_map/ppermute | solution.py:391
  70.6 0.0 collective-permute-start.7
  70.6 2.4 %collective-permute-start.8 = (bf16[128,1152]{1,0:T(8,128)(2,1)}, bf16[128,1152]{1,0:T(8,128)(2,1)}, u32[]{:S(2)}, u32[]{:S(2)}) collective-permute-start(bf16[128,1152]{1,0:T(8,128)(2,1)} %get-tuple-element.26), channel_id=1, source_target_pairs={{0,64},{8,72},{16,80},{24,88},{32,96},{40,104},{48,112},{56,120},{... | collective-permute-start | bytes 884744 | tf_op jit(solution)/shard_map/ppermute | solution.py:391
  73.0 0.0 all-to-all-done.1
  73.1 16.8 %attend.5 = (bf16[128,1152]{1,0:T(8,128)(2,1)}, bf16[256,256]{1,0:T(8,128)(2,1)}) custom-call(s32[16]{0:T(128)} %refs_0_.2, bf16[128,1024]{1,0:T(8,128)(2,1)} %refs_1_.1, bf16[2048,256]{1,0:T(8,128)(2,1)} %pack.1.refs_4_.refs_2_, bf16[2048,256]{1,0:T(8,128)(2,1)} %collective-permute-done.4.refs_5_.refs_3_, bf16[2048,256]{1,0:T(8,128)(2,1)} %collective-permute-done.refs_4_, ...), custom_call_target="tpu_custom_call" | custom-call | flops 20000000000 | bytes 1000 | tf_op jit(solution)/shard_map/attend/pallas_call | solution.py:280
  89.8 0.0 collective-permute-done.6.refs_1_
  89.8 0.0 collective-permute-done.7.refs_2_
  89.8 0.0 collective-permute-done.8.refs_3_
  89.8 2.8 %merge.1 = bf16[128,1024]{1,0:T(8,128)(2,1)} custom-call(bf16[128,1152]{1,0:T(8,128)(2,1)} %get-tuple-element.24.refs_0_, bf16[128,1152]{1,0:T(8,128)(2,1)} %collective-permute-done.6.refs_1_, bf16[128,1152]{1,0:T(8,128)(2,1)} %collective-permute-done.7.refs_2_, bf16[128,1152]{1,0:T(8,128)(2,1)} %collective-permute-done.8.refs_3_), custom_call_target="tpu_custom_call" | custom-call | flops 1000 | bytes 1000 | tf_op jit(solution)/shard_map/merge/pallas_call | solution.py:324
Async XLA Ops:
  2.7 16.0 %collective-permute-start.4 = (bf16[2048,256]{1,0:T(8,128)(2,1)}, bf16[2048,256]{1,0:T(8,128)(2,1)}, u32[]{:S(2)}, u32[]{:S(2)}) collective-permute-start(bf16[2048,256]{1,0:T(8,128)(2,1)} %pack.1.refs_4_.refs_2_), channel_id=1, source_target_pairs={{0,8},{8,0},{16,24},{24,16},{32,40},{40,32},{48,56},{56,48},{64,72... | collective-permute-start | bytes 3145736 | tf_op jit(solution)/shard_map/ppermute | solution.py:387
  2.7 32.9 %collective-permute-start = (bf16[2048,256]{1,0:T(8,128)(2,1)}, bf16[2048,256]{1,0:T(8,128)(2,1)}, u32[]{:S(2)}, u32[]{:S(2)}) collective-permute-start(bf16[2048,256]{1,0:T(8,128)(2,1)} %pack.1.refs_4_.refs_2_), channel_id=1, source_target_pairs={{0,16},{8,24},{16,0},{24,8},{32,48},{40,56},{48,32},{56,40},{64,80... | collective-permute-start | bytes 3145736 | tf_op jit(solution)/shard_map/ppermute | solution.py:387
  2.9 15.8 %collective-permute-start.1 = (bf16[128,1024]{1,0:T(8,128)(2,1)}, bf16[128,1024]{1,0:T(8,128)(2,1)}, u32[]{:S(2)}, u32[]{:S(2)}) collective-permute-start(bf16[128,1024]{1,0:T(8,128)(2,1)} %refs_1_.1), channel_id=1, source_target_pairs={{0,32},{8,40},{16,48},{24,56},{32,64},{40,72},{48,80},{56,88},{64,... | collective-permute-start | bytes 786440 | tf_op jit(solution)/shard_map/ppermute | solution.py:391
  3.1 15.6 %collective-permute-start.2 = (bf16[128,1024]{1,0:T(8,128)(2,1)}, bf16[128,1024]{1,0:T(8,128)(2,1)}, u32[]{:S(2)}, u32[]{:S(2)}) collective-permute-start(bf16[128,1024]{1,0:T(8,128)(2,1)} %refs_1_.1), channel_id=1, source_target_pairs={{0,96},{8,104},{16,112},{24,120},{32,0},{40,8},{48,16},{56,24},{64... | collective-permute-start | bytes 786440 | tf_op jit(solution)/shard_map/ppermute | solution.py:391
  4.9 13.8 %collective-permute-start.3 = (bf16[128,1024]{1,0:T(8,128)(2,1)}, bf16[128,1024]{1,0:T(8,128)(2,1)}, u32[]{:S(2)}, u32[]{:S(2)}) collective-permute-start(bf16[128,1024]{1,0:T(8,128)(2,1)} %refs_1_.1), channel_id=1, source_target_pairs={{0,64},{8,72},{16,80},{24,88},{32,96},{40,104},{48,112},{56,120},{... | collective-permute-start | bytes 786440 | tf_op jit(solution)/shard_map/ppermute | solution.py:391
  11.2 24.4 %all-to-all-start = ((bf16[8,128,256]{2,1,0:T(8,128)(2,1)}), bf16[8,128,256]{2,1,0:T(8,128)(2,1)}, u32[]{:S(2)}, u32[]{:S(2)}) async-start(bf16[8,128,256]{2,1,0:T(8,128)(2,1)} %project.1), calls=%async_computation | async-start | bytes 1048576 | tf_op jit(solution)/shard_map/all_to_all | solution.py:404
  35.6 12.7 %collective-permute-start.5 = (bf16[2048,256]{1,0:T(8,128)(2,1)}, bf16[2048,256]{1,0:T(8,128)(2,1)}, u32[]{:S(2)}, u32[]{:S(2)}) collective-permute-start(bf16[2048,256]{1,0:T(8,128)(2,1)} %collective-permute-done.refs_4_), channel_id=1, source_target_pairs={{0,8},{8,0},{16,24},{24,16},{32,40},{40,32},{48,56},{56,48},{64,72... | collective-permute-start | bytes 3145736 | tf_op jit(solution)/shard_map/ppermute | solution.py:387
  37.9 35.2 %all-to-all-start.1 = ((bf16[16,128,256]{2,1,0:T(8,128)(2,1)}), bf16[16,128,256]{2,1,0:T(8,128)(2,1)}, u32[]{:S(2)}, u32[]{:S(2)}) async-start(bf16[16,128,256]{2,1,0:T(8,128)(2,1)} %relay.1), calls=%async_computation.1 | async-start | bytes 2097152 | tf_op jit(solution)/shard_map/all_to_all | solution.py:412
  65.0 24.8 %collective-permute-start.6 = (bf16[128,1152]{1,0:T(8,128)(2,1)}, bf16[128,1152]{1,0:T(8,128)(2,1)}, u32[]{:S(2)}, u32[]{:S(2)}) collective-permute-start(bf16[128,1152]{1,0:T(8,128)(2,1)} %get-tuple-element.21), channel_id=1, source_target_pairs={{0,96},{8,104},{16,112},{24,120},{32,0},{40,8},{48,16},{56,24},{64... | collective-permute-start | bytes 884744 | tf_op jit(solution)/shard_map/ppermute | solution.py:391
  70.6 19.2 %collective-permute-start.7 = (bf16[128,1152]{1,0:T(8,128)(2,1)}, bf16[128,1152]{1,0:T(8,128)(2,1)}, u32[]{:S(2)}, u32[]{:S(2)}) collective-permute-start(bf16[128,1152]{1,0:T(8,128)(2,1)} %get-tuple-element.25), channel_id=1, source_target_pairs={{0,32},{8,40},{16,48},{24,56},{32,64},{40,72},{48,80},{56,88},{64,... | collective-permute-start | bytes 884744 | tf_op jit(solution)/shard_map/ppermute | solution.py:391
  70.6 19.2 %collective-permute-start.8 = (bf16[128,1152]{1,0:T(8,128)(2,1)}, bf16[128,1152]{1,0:T(8,128)(2,1)}, u32[]{:S(2)}, u32[]{:S(2)}) collective-permute-start(bf16[128,1152]{1,0:T(8,128)(2,1)} %get-tuple-element.26), channel_id=1, source_target_pairs={{0,64},{8,72},{16,80},{24,88},{32,96},{40,104},{48,112},{56,120},{... | collective-permute-start | bytes 884744 | tf_op jit(solution)/shard_map/ppermute | solution.py:391

commit v8 on v7

--- a/solution.py
+++ b/solution.py
@@ -109,7 +109,7 @@
                 at = (i * groups + g) * 128
                 mm[at : at + 128, :] = jnp.broadcast_to(sides[i][:, g : g + 1], (128, 128))
     else:
-        top = jnp.max(nt_dot(qb[...], kb[:256, :HD]), axis=-1, keepdims=True) * SCALE
+        top = jnp.max(nt_dot(qb[...], kb[:128, :HD]), axis=-1, keepdims=True) * SCALE
         mm[...] = jnp.broadcast_to(top.astype(BF16).astype(F32), mm.shape)
 
     def up_to(limit, size):
@@ -209,6 +209,13 @@
         @pl.when(turn == 1)
         def _():
             raise_tops()
+            if state_in:
+                for i in range(nq):
+                    for g in range(groups):
+                        at = (i * groups + g) * 128
+                        part = slice(g * 128, (g + 1) * 128)
+                        decay = jnp.exp2(sides[i][:, g : g + 1] - mm[at : at + 128, :])
+                        st[i, :, part] = (st[i, :, part].astype(F32) * decay).astype(BF16)
 
         sweep(turn)
         fits = jnp.max(ll[...]) < BIG
@@ -220,23 +227,24 @@
 
     for i in range(nq):
         out = outs[i]
-        side = jnp.zeros((128, 128), F32)
+        tops = jnp.zeros((128, 128), F32)
+        sums = jnp.zeros((128, 128), F32)
         for g in range(groups):
             rows_at = slice((i * groups + g) * 128, (i * groups + g + 1) * 128)
             part = slice(g * 128, (g + 1) * 128)
             mixed = acc[rows_at, :]
+            if state_in:
+                mixed = mixed + st[i, :, part].astype(F32)
+            out[:, part] = mixed.astype(BF16)
+            tops = jnp.where(lane == g, mm[rows_at, :], tops)
             total = jnp.sum(ll[rows_at, :], axis=-1, keepdims=True)
-            top = mm[rows_at, :]
-            if state_in:
-                before = sides[i]
-                decay = jnp.exp2(before[:, g : g + 1] - top)
-                mixed = mixed + st[i, :, part].astype(F32) * decay
-                total = total + (before[:, 8 + g : 9 + g] + before[:, 16 + g : 17 + g]) * decay
-            out[:, part] = mixed.astype(BF16)
-            high = total.astype(BF16).astype(F32)
-            side = jnp.where(lane == g, top, side)
-            side = jnp.where(lane == 8 + g, high, side)
-            side = jnp.where(lane == 16 + g, total - high, side)
+            sums = jnp.where(lane == 8 + g, total, sums)
+        if state_in:
+            before = sides[i] + pltpu.roll(sides[i], 120, 1)
+            decay = pltpu.roll(jnp.exp2(sides[i] - tops), 8, 1)
+            sums = jnp.where((lane >= 8) & (lane < 16), sums + before * decay, 0.0)
+        high = sums.astype(BF16).astype(F32)
+        side = tops + high + pltpu.roll(sums - high, 8, 1)
         out[:, groups * 128 :] = side.astype(BF16)
 
     if fresh:

time: 91.8 us -> 91.9 us (level)
  the two profiles are of different devices: /device:TPU:58 before, /device:TPU:1 now
where the time goes in v8:
time: 91.9 us; the launch traced here: 92.2 us
  Pallas kernels  65.4 us (71%)
  starting transfers between devices  25.9 us (28%)
    pallas_call x3, Pallas kernels, attend(): pl.pallas_call(functools.partial(attend_kernel, cfg), grid=(1,), in_specs...  53.3 us
    ppermute x6, starting transfers between devices, turn(): return lax.ppermute(x, 'ctx', [(i, (i + 4 * k) % 16) for i in range(16)])  9.81 us
    all_to_all x1, starting transfers between devices, body(): gathered = lax.all_to_all(partial, 'tp', 0, 0, tiled=True)  7.04 us
    pallas_call x1, Pallas kernels, project(): pl.pallas_call(project_kernel, grid=(heads // at_once,), in_specs=[pl.Blo...  5.05 us
    ppermute x3, starting transfers between devices, flip(): return lax.ppermute(x, 'ctx', [(i, i ^ bits) for i in range(16)])  4.61 us
    all_to_all x1, starting transfers between devices, body(): lax.all_to_all(spread, 'ctx', 0, 0, tiled=True).reshape(16 * 128, 2 * HD)  4.47 us
    pallas_call x1, Pallas kernels, merge(): pl.pallas_call(merge_kernel, grid=(2,), in_specs=[pl.BlockSpec((rows // 2...  2.75 us
    pallas_call x1, Pallas kernels, relay(): pl.pallas_call(relay_kernel, in_specs=[vmem_spec()], out_specs=pl.BlockSp...  2.26 us
  transfers between devices with their start and end apart: 11, of which 0 were waited for; matrix products, arithmetic and copies ran while one was open for 0% of the time, Pallas kernels for 66%

profile of v8, /device:TPU:1, one launch (start us, length us, event | category | flops | bytes accessed | tf_op | source)
XLA Modules:
  0.0 92.2 jit_solution(1315494456633182446)
XLA Ops:
  0.6 2.1 %pack.1.refs_4_.refs_2_ = bf16[2048,256]{1,0:T(8,128)(2,1)} custom-call(bf16[2048,128]{1,0:T(8,128)(2,1)} %k_ref.1, bf16[2048,128]{1,0:T(8,128)(2,1)} %v_ref.1), custom_call_target="tpu_custom_call" | custom-call | flops 1000 | bytes 1000 | tf_op jit(solution)/shard_map/pack/pallas_call | solution.py:382
  2.7 1.4 %collective-permute-start.4 = (bf16[2048,256]{1,0:T(8,128)(2,1)}, bf16[2048,256]{1,0:T(8,128)(2,1)}, u32[]{:S(2)}, u32[]{:S(2)}) collective-permute-start(bf16[2048,256]{1,0:T(8,128)(2,1)} %pack.1.refs_4_.refs_2_), channel_id=1, source_target_pairs={{0,8},{8,0},{16,24},{24,16},{32,40},{40,32},{48,56},{56,48},{64,72... | collective-permute-start | bytes 3145736 | tf_op jit(solution)/shard_map/ppermute | solution.py:395
  4.2 1.7 %collective-permute-start = (bf16[2048,256]{1,0:T(8,128)(2,1)}, bf16[2048,256]{1,0:T(8,128)(2,1)}, u32[]{:S(2)}, u32[]{:S(2)}) collective-permute-start(bf16[2048,256]{1,0:T(8,128)(2,1)} %pack.1.refs_4_.refs_2_), channel_id=1, source_target_pairs={{0,16},{8,24},{16,0},{24,8},{32,48},{40,56},{48,32},{56,40},{64,80... | collective-permute-start | bytes 3145736 | tf_op jit(solution)/shard_map/ppermute | solution.py:395
  5.9 1.3 %collective-permute-start.1 = (bf16[128,1024]{1,0:T(8,128)(2,1)}, bf16[128,1024]{1,0:T(8,128)(2,1)}, u32[]{:S(2)}, u32[]{:S(2)}) collective-permute-start(bf16[128,1024]{1,0:T(8,128)(2,1)} %refs_1_.1), channel_id=1, source_target_pairs={{0,32},{8,40},{16,48},{24,56},{32,64},{40,72},{48,80},{56,88},{64,... | collective-permute-start | bytes 786440 | tf_op jit(solution)/shard_map/ppermute | solution.py:399
  7.2 1.4 %collective-permute-start.2 = (bf16[128,1024]{1,0:T(8,128)(2,1)}, bf16[128,1024]{1,0:T(8,128)(2,1)}, u32[]{:S(2)}, u32[]{:S(2)}) collective-permute-start(bf16[128,1024]{1,0:T(8,128)(2,1)} %refs_1_.1), channel_id=1, source_target_pairs={{0,96},{8,104},{16,112},{24,120},{32,0},{40,8},{48,16},{56,24},{64... | collective-permute-start | bytes 786440 | tf_op jit(solution)/shard_map/ppermute | solution.py:399
  8.6 1.6 %collective-permute-start.3 = (bf16[128,1024]{1,0:T(8,128)(2,1)}, bf16[128,1024]{1,0:T(8,128)(2,1)}, u32[]{:S(2)}, u32[]{:S(2)}) collective-permute-start(bf16[128,1024]{1,0:T(8,128)(2,1)} %refs_1_.1), channel_id=1, source_target_pairs={{0,64},{8,72},{16,80},{24,88},{32,96},{40,104},{48,112},{56,120},{... | collective-permute-start | bytes 786440 | tf_op jit(solution)/shard_map/ppermute | solution.py:399
  10.3 5.0 %project.1 = bf16[8,128,256]{2,1,0:T(8,128)(2,1)} custom-call(bf16[128,2048]{1,0:T(8,128)(2,1)} %tok_ref.1, bf16[2048,2048]{1,0:T(8,128)(2,1)} %w_ref.1), custom_call_target="tpu_custom_call" | custom-call | flops 1000 | bytes 1000 | tf_op jit(solution)/shard_map/project/pallas_call | solution.py:48
  15.3 7.0 %all-to-all-start = ((bf16[8,128,256]{2,1,0:T(8,128)(2,1)}), bf16[8,128,256]{2,1,0:T(8,128)(2,1)}, u32[]{:S(2)}, u32[]{:S(2)}) async-start(bf16[8,128,256]{2,1,0:T(8,128)(2,1)} %project.1), calls=%async_computation | async-start | bytes 1048576 | tf_op jit(solution)/shard_map/all_to_all | solution.py:412
  22.4 0.0 collective-permute-done.1.refs_1_
  22.4 0.0 collective-permute-done.2.refs_2_
  22.4 0.0 collective-permute-done.3.refs_3_
  22.4 0.0 collective-permute-done.4.refs_5_.refs_3_
  22.4 19.6 %attend.3 = (bf16[128,1152]{1,0:T(8,128)(2,1)}, bf16[128,1152]{1,0:T(8,128)(2,1)}, bf16[128,1152]{1,0:T(8,128)(2,1)}) custom-call(s32[16]{0:T(128)} %refs_0_.2, bf16[128,1024]{1,0:T(8,128)(2,1)} %collective-permute-done.1.refs_1_, bf16[128,1024]{1,0:T(8,128)(2,1)} %collective-permute-done.2.refs_2_, bf16[128,1024]{1,0:T(8,128)(2,1)} %collective-permute-done.3.refs_3_, ...), custom_call_target="tpu_custom_call" | custom-call | flops 4000000000 | bytes 1000 | tf_op jit(solution)/shard_map/attend/pallas_call | solution.py:288
  42.0 0.0 all-to-all-done.parts
  42.0 0.0 collective-permute-done.refs_4_
  42.0 1.5 %collective-permute-start.5 = (bf16[2048,256]{1,0:T(8,128)(2,1)}, bf16[2048,256]{1,0:T(8,128)(2,1)}, u32[]{:S(2)}, u32[]{:S(2)}) collective-permute-start(bf16[2048,256]{1,0:T(8,128)(2,1)} %collective-permute-done.refs_4_), channel_id=1, source_target_pairs={{0,8},{8,0},{16,24},{24,16},{32,40},{40,32},{48,56},{56,48},{64,72... | collective-permute-start | bytes 3145736 | tf_op jit(solution)/shard_map/ppermute | solution.py:395
  43.5 2.3 %relay.1 = bf16[16,128,256]{2,1,0:T(8,128)(2,1)} custom-call(bf16[8,128,256]{2,1,0:T(8,128)(2,1)} %all-to-all-done.parts), custom_call_target="tpu_custom_call" | custom-call | flops 20000000000 | bytes 1000 | tf_op jit(solution)/shard_map/relay/pallas_call | solution.py:360
  45.8 4.5 %all-to-all-start.1 = ((bf16[16,128,256]{2,1,0:T(8,128)(2,1)}), bf16[16,128,256]{2,1,0:T(8,128)(2,1)}, u32[]{:S(2)}, u32[]{:S(2)}) async-start(bf16[16,128,256]{2,1,0:T(8,128)(2,1)} %relay.1), calls=%async_computation.1 | async-start | bytes 2097152 | tf_op jit(solution)/shard_map/all_to_all | solution.py:420
  50.2 0.0 collective-permute-done.5.refs_5_
  50.2 17.1 %attend.4 = (bf16[128,1152]{1,0:T(8,128)(2,1)}, bf16[128,1152]{1,0:T(8,128)(2,1)}, bf16[128,1152]{1,0:T(8,128)(2,1)}) custom-call(s32[16]{0:T(128)} %refs_0_.2, bf16[128,1024]{1,0:T(8,128)(2,1)} %collective-permute-done.1.refs_1_, bf16[128,1024]{1,0:T(8,128)(2,1)} %collective-permute-done.2.refs_2_, bf16[128,1024]{1,0:T(8,128)(2,1)} %collective-permute-done.3.refs_3_, ...), custom_call_target="tpu_custom_call" | custom-call | flops 20000000000 | bytes 1000 | tf_op jit(solution)/shard_map/attend/pallas_call | solution.py:288
  67.4 1.3 %collective-permute-start.6 = (bf16[128,1152]{1,0:T(8,128)(2,1)}, bf16[128,1152]{1,0:T(8,128)(2,1)}, u32[]{:S(2)}, u32[]{:S(2)}) collective-permute-start(bf16[128,1152]{1,0:T(8,128)(2,1)} %get-tuple-element.21), channel_id=1, source_target_pairs={{0,96},{8,104},{16,112},{24,120},{32,0},{40,8},{48,16},{56,24},{64... | collective-permute-start | bytes 884744 | tf_op jit(solution)/shard_map/ppermute | solution.py:399
  68.7 0.3 collective-permute-start.7
  68.9 3.9 %collective-permute-start.8 = (bf16[128,1152]{1,0:T(8,128)(2,1)}, bf16[128,1152]{1,0:T(8,128)(2,1)}, u32[]{:S(2)}, u32[]{:S(2)}) collective-permute-start(bf16[128,1152]{1,0:T(8,128)(2,1)} %get-tuple-element.26), channel_id=1, source_target_pairs={{0,64},{8,72},{16,80},{24,88},{32,96},{40,104},{48,112},{56,120},{... | collective-permute-start | bytes 884744 | tf_op jit(solution)/shard_map/ppermute | solution.py:399
  72.8 0.0 all-to-all-done.1
  72.8 16.6 %attend.5 = (bf16[128,1152]{1,0:T(8,128)(2,1)}, bf16[256,256]{1,0:T(8,128)(2,1)}) custom-call(s32[16]{0:T(128)} %refs_0_.2, bf16[128,1024]{1,0:T(8,128)(2,1)} %refs_1_.1, bf16[2048,256]{1,0:T(8,128)(2,1)} %pack.1.refs_4_.refs_2_, bf16[2048,256]{1,0:T(8,128)(2,1)} %collective-permute-done.4.refs_5_.refs_3_, bf16[2048,256]{1,0:T(8,128)(2,1)} %collective-permute-done.refs_4_, ...), custom_call_target="tpu_custom_call" | custom-call | flops 20000000000 | bytes 1000 | tf_op jit(solution)/shard_map/attend/pallas_call | solution.py:288
  89.4 0.0 collective-permute-done.6.refs_1_
  89.4 0.0 collective-permute-done.7.refs_2_
  89.4 0.0 collective-permute-done.8.refs_3_
  89.4 2.8 %merge.1 = bf16[128,1024]{1,0:T(8,128)(2,1)} custom-call(bf16[128,1152]{1,0:T(8,128)(2,1)} %get-tuple-element.24.refs_0_, bf16[128,1152]{1,0:T(8,128)(2,1)} %collective-permute-done.6.refs_1_, bf16[128,1152]{1,0:T(8,128)(2,1)} %collective-permute-done.7.refs_2_, bf16[128,1152]{1,0:T(8,128)(2,1)} %collective-permute-done.8.refs_3_), custom_call_target="tpu_custom_call" | custom-call | flops 1000 | bytes 1000 | tf_op jit(solution)/shard_map/merge/pallas_call | solution.py:332
Async XLA Ops:
  2.7 19.6 %collective-permute-start.4 = (bf16[2048,256]{1,0:T(8,128)(2,1)}, bf16[2048,256]{1,0:T(8,128)(2,1)}, u32[]{:S(2)}, u32[]{:S(2)}) collective-permute-start(bf16[2048,256]{1,0:T(8,128)(2,1)} %pack.1.refs_4_.refs_2_), channel_id=1, source_target_pairs={{0,8},{8,0},{16,24},{24,16},{32,40},{40,32},{48,56},{56,48},{64,72... | collective-permute-start | bytes 3145736 | tf_op jit(solution)/shard_map/ppermute | solution.py:395
  4.2 37.9 %collective-permute-start = (bf16[2048,256]{1,0:T(8,128)(2,1)}, bf16[2048,256]{1,0:T(8,128)(2,1)}, u32[]{:S(2)}, u32[]{:S(2)}) collective-permute-start(bf16[2048,256]{1,0:T(8,128)(2,1)} %pack.1.refs_4_.refs_2_), channel_id=1, source_target_pairs={{0,16},{8,24},{16,0},{24,8},{32,48},{40,56},{48,32},{56,40},{64,80... | collective-permute-start | bytes 3145736 | tf_op jit(solution)/shard_map/ppermute | solution.py:395
  5.9 16.5 %collective-permute-start.1 = (bf16[128,1024]{1,0:T(8,128)(2,1)}, bf16[128,1024]{1,0:T(8,128)(2,1)}, u32[]{:S(2)}, u32[]{:S(2)}) collective-permute-start(bf16[128,1024]{1,0:T(8,128)(2,1)} %refs_1_.1), channel_id=1, source_target_pairs={{0,32},{8,40},{16,48},{24,56},{32,64},{40,72},{48,80},{56,88},{64,... | collective-permute-start | bytes 786440 | tf_op jit(solution)/shard_map/ppermute | solution.py:399
  7.2 15.2 %collective-permute-start.2 = (bf16[128,1024]{1,0:T(8,128)(2,1)}, bf16[128,1024]{1,0:T(8,128)(2,1)}, u32[]{:S(2)}, u32[]{:S(2)}) collective-permute-start(bf16[128,1024]{1,0:T(8,128)(2,1)} %refs_1_.1), channel_id=1, source_target_pairs={{0,96},{8,104},{16,112},{24,120},{32,0},{40,8},{48,16},{56,24},{64... | collective-permute-start | bytes 786440 | tf_op jit(solution)/shard_map/ppermute | solution.py:399
  8.6 13.7 %collective-permute-start.3 = (bf16[128,1024]{1,0:T(8,128)(2,1)}, bf16[128,1024]{1,0:T(8,128)(2,1)}, u32[]{:S(2)}, u32[]{:S(2)}) collective-permute-start(bf16[128,1024]{1,0:T(8,128)(2,1)} %refs_1_.1), channel_id=1, source_target_pairs={{0,64},{8,72},{16,80},{24,88},{32,96},{40,104},{48,112},{56,120},{... | collective-permute-start | bytes 786440 | tf_op jit(solution)/shard_map/ppermute | solution.py:399
  15.3 26.7 %all-to-all-start = ((bf16[8,128,256]{2,1,0:T(8,128)(2,1)}), bf16[8,128,256]{2,1,0:T(8,128)(2,1)}, u32[]{:S(2)}, u32[]{:S(2)}) async-start(bf16[8,128,256]{2,1,0:T(8,128)(2,1)} %project.1), calls=%async_computation | async-start | bytes 1048576 | tf_op jit(solution)/shard_map/all_to_all | solution.py:412
  42.0 8.2 %collective-permute-start.5 = (bf16[2048,256]{1,0:T(8,128)(2,1)}, bf16[2048,256]{1,0:T(8,128)(2,1)}, u32[]{:S(2)}, u32[]{:S(2)}) collective-permute-start(bf16[2048,256]{1,0:T(8,128)(2,1)} %collective-permute-done.refs_4_), channel_id=1, source_target_pairs={{0,8},{8,0},{16,24},{24,16},{32,40},{40,32},{48,56},{56,48},{64,72... | collective-permute-start | bytes 3145736 | tf_op jit(solution)/shard_map/ppermute | solution.py:395
  45.8 27.0 %all-to-all-start.1 = ((bf16[16,128,256]{2,1,0:T(8,128)(2,1)}), bf16[16,128,256]{2,1,0:T(8,128)(2,1)}, u32[]{:S(2)}, u32[]{:S(2)}) async-start(bf16[16,128,256]{2,1,0:T(8,128)(2,1)} %relay.1), calls=%async_computation.1 | async-start | bytes 2097152 | tf_op jit(solution)/shard_map/all_to_all | solution.py:420
  67.4 22.0 %collective-permute-start.6 = (bf16[128,1152]{1,0:T(8,128)(2,1)}, bf16[128,1152]{1,0:T(8,128)(2,1)}, u32[]{:S(2)}, u32[]{:S(2)}) collective-permute-start(bf16[128,1152]{1,0:T(8,128)(2,1)} %get-tuple-element.21), channel_id=1, source_target_pairs={{0,96},{8,104},{16,112},{24,120},{32,0},{40,8},{48,16},{56,24},{64... | collective-permute-start | bytes 884744 | tf_op jit(solution)/shard_map/ppermute | solution.py:399
  68.7 20.7 %collective-permute-start.7 = (bf16[128,1152]{1,0:T(8,128)(2,1)}, bf16[128,1152]{1,0:T(8,128)(2,1)}, u32[]{:S(2)}, u32[]{:S(2)}) collective-permute-start(bf16[128,1152]{1,0:T(8,128)(2,1)} %get-tuple-element.25), channel_id=1, source_target_pairs={{0,32},{8,40},{16,48},{24,56},{32,64},{40,72},{48,80},{56,88},{64,... | collective-permute-start | bytes 884744 | tf_op jit(solution)/shard_map/ppermute | solution.py:399
  68.9 20.5 %collective-permute-start.8 = (bf16[128,1152]{1,0:T(8,128)(2,1)}, bf16[128,1152]{1,0:T(8,128)(2,1)}, u32[]{:S(2)}, u32[]{:S(2)}) collective-permute-start(bf16[128,1152]{1,0:T(8,128)(2,1)} %get-tuple-element.26), channel_id=1, source_target_pairs={{0,64},{8,72},{16,80},{24,88},{32,96},{40,104},{48,112},{56,120},{... | collective-permute-start | bytes 884744 | tf_op jit(solution)/shard_map/ppermute | solution.py:399
